TPU v7x, 32 devices: a whole 2x2x4 slice. The times are simulated.
32 devices in a mesh: dp: 8 (over y, x, core), mp: 4 (over z).
Axes of the slice: x: 2, y: 2, z: 4, core: 2. Of those that a mesh axis runs over, the one named last changes fastest.
Arguments:
- lengths: int32 [4, 8], P(None, 'dp'), may hold values from 2 to 1024, as said below
- owners: int32 [4, 8, 1024, 1], P(None, 'dp'), may hold values from 0 to 31; in each aligned block of 256 rows (0 to 255, 256 to 511, ..., all dimensions but the last counted through in order) at most 16 rows name the same one
- item_rows: int32 [4, 8, 1024], P(None, 'dp'), may hold values from 0 to 783
- buckets: int32 [4, 8, 1024], P(None, 'dp'), may hold values from 0 to 127
- negatives: int32 [4, 512], replicated, may hold values from 0 to 25087
- table: float32 [25088, 512], P(('dp', 'mp')), may hold values from -6 to 6
- table_m: float32 [25088, 512], P(('dp', 'mp')), may hold values from -0.00030517578 to 0.00030517578
- table_v: float32 [25088, 512], P(('dp', 'mp')), may hold values from 2.0065307e-09 to 8.010864e-09
- w_f1: float32 [512, 2048], P(None, 'mp'), may hold values from -0.25 to 0.25
- f1_m: float32 [512, 2048], P(None, 'mp'), may hold values from -0.0009765625 to 0.0009765625
- f1_v: float32 [512, 2048], P(None, 'mp'), may hold values from 2.0065308e-08 to 8.010864e-08
- w_f2: float32 [512, 512], P('mp'), may hold values from -0.25 to 0.25
- f2_m: float32 [512, 512], P('mp'), may hold values from -0.0009765625 to 0.0009765625
- f2_v: float32 [512, 512], P('mp'), may hold values from 2.0065308e-08 to 8.010864e-08
- gains: float32 [3, 512], replicated, may hold values from 0.5 to 1.5
- gains_m: float32 [3, 512], replicated, may hold values from -0.0034179688 to 0.0034179688
- gains_v: float32 [3, 512], replicated, may hold values from 2.0065308e-07 to 8.010864e-07
- bias: float32 [8, 128], P('mp'), may hold values from -6 to 6
- bias_m: float32 [8, 128], P('mp'), may hold values from -0.0034179688 to 0.0034179688
- bias_v: float32 [8, 128], P('mp'), may hold values from 2.0065308e-07 to 8.010864e-07
Outputs:
- loss_sum: float32 [], replicated
- loss_count: float32 [], replicated
- grad_norm: float32 [], replicated
- table_new: float32 [25088, 512], P(('dp', 'mp'))
- table_m_new: float32 [25088, 512], P(('dp', 'mp'))
- table_v_new: float32 [25088, 512], P(('dp', 'mp'))
- table_low: bfloat16 [25088, 512], P(('dp', 'mp'))
- f1_new: float32 [512, 2048], P(None, 'mp')
- f1_m_new: float32 [512, 2048], P(None, 'mp')
- f1_v_new: float32 [512, 2048], P(None, 'mp')
- f1_low: bfloat16 [512, 2048], P(None, 'mp')
- f2_new: float32 [512, 512], P('mp')
- f2_m_new: float32 [512, 512], P('mp')
- f2_v_new: float32 [512, 512], P('mp')
- f2_low: bfloat16 [512, 512], P('mp')
- gains_new: float32 [3, 512], replicated
- gains_m_new: float32 [3, 512], replicated
- gains_v_new: float32 [3, 512], replicated
- bias_new: float32 [8, 128], P('mp')
- bias_m_new: float32 [8, 128], P('mp')
- bias_v_new: float32 [8, 128], P('mp')
Inputs may be any that keep to these rules, and one draw needn't show every extreme that they name: `lengths`: in each micro-batch one history has exactly 1024 events. `owners`: counting the rows in order over all leading dimensions, in each aligned block of 256 rows (the lookups of one device) no owner appears more than 16 times; some owner appears exactly 16 times in some blocks.
All inputs are finite; a program needn't handle non-finite values.
Results may differ from a plain program's by a relative error of at most 0.0035.
The roundings to bfloat16 on the way count: a program that leaves them out, or rounds other values in their place, can miss the bound.
Values may be sent and summed in bfloat16 or wider, within the bound.
A program may use at most 320 MiB of HBM per device.

v0:
```python
import jax
import jax.numpy as jnp
from jax import lax
from jax.sharding import PartitionSpec as P

DH = 64
D = 512
NB = 128
ROWS_DEV = 784
LEN = 1024
MB = 4
STEP = 10


epsilon = 1e-06
clip_at = 1.0
beta_one = 0.9
beta_two = 0.95
adam_floor = 1e-08
highest = lax.Precision.HIGHEST


def from_behind(array, axis, by):
    length = lax.axis_size(axis)
    pairs = [(i, i + by) for i in range(length) if 0 <= i + by < length]
    return lax.ppermute(array, axis, pairs)


def norm_rows(values, gain):
    factor = lax.rsqrt(jnp.mean(values * values, -1, keepdims=True) + epsilon)
    return (values * factor * gain, factor)


def norm_back(values, factor, gain, grad_out, weight):
    scaled = grad_out * gain
    grad_in = factor * (
        scaled - values * factor * factor * jnp.mean(values * scaled, -1, keepdims=True)
    )
    grad_gain = jnp.sum(grad_out * values * factor * weight[:, None], 0)
    return (grad_in, grad_gain)


def silu_slope(values):
    sigma = jax.nn.sigmoid(values)
    return sigma * (1.0 + values * (1.0 - sigma))


def attn_mask(lens, length):
    place = jnp.arange(length)
    causal = place[None, :] <= place[:, None]
    live = place[None, :] < lens[:, None]
    return (causal[None, None] & live[:, None, None, :], (place + 1.0)[:, None])


def raw_scores(queries, key_rows, key_bias):
    scores = jnp.einsum("bqhd,bkhd->bhqk", queries, key_rows, preferred_element_type=jnp.float32)
    return scores * queries.shape[-1] ** (-0.5) + key_bias[:, :, None, :]


def attend(queries, key_rows, value_rows, key_bias, lens):
    mask, counts = attn_mask(lens, queries.shape[1])
    scores = raw_scores(queries, key_rows, key_bias)
    weights = (jnp.where(mask, jax.nn.silu(scores), 0.0) / counts).astype(jnp.bfloat16)
    return jnp.einsum("bhqk,bkhd->bqhd", weights, value_rows, preferred_element_type=jnp.float32)


def attend_back(queries, key_rows, value_rows, key_bias, lens, grad_out):
    mask, counts = attn_mask(lens, queries.shape[1])
    scores = raw_scores(queries, key_rows, key_bias)
    weights = (jnp.where(mask, jax.nn.silu(scores), 0.0) / counts).astype(jnp.bfloat16)
    grad_weights = jnp.einsum(
        "bqhd,bkhd->bhqk", grad_out, value_rows, preferred_element_type=jnp.float32
    )
    grad_values = jnp.einsum(
        "bhqk,bqhd->bkhd", weights, grad_out, preferred_element_type=jnp.float32
    )
    grad_scores = jnp.where(mask, grad_weights / counts * silu_slope(scores), 0.0).astype(
        jnp.bfloat16
    )
    scale = queries.shape[-1] ** (-0.5)
    grad_queries = (
        jnp.einsum("bhqk,bkhd->bqhd", grad_scores, key_rows, preferred_element_type=jnp.float32)
        * scale
    )
    grad_keys = (
        jnp.einsum("bhqk,bqhd->bkhd", grad_scores, queries, preferred_element_type=jnp.float32)
        * scale
    )
    grad_bias = jnp.sum(grad_scores.astype(jnp.float32), 2)
    return (grad_queries, grad_keys, grad_values, grad_bias)


def adam_step(weight, grad, first, second, rate, decay):
    first_new = beta_one * first + (1.0 - beta_one) * grad
    second_new = beta_two * second + (1.0 - beta_two) * grad * grad
    fix_one = 1.0 - beta_one**STEP
    fix_two = 1.0 - beta_two**STEP
    move = first_new / fix_one / (jnp.sqrt(second_new / fix_two) + adam_floor) + decay * weight
    return (weight - rate * move, first_new, second_new)


def per_device(
    lengths,
    owners,
    item_rows,
    buckets,
    negatives,
    table,
    table_m,
    table_v,
    w_f1,
    f1_m,
    f1_v,
    w_f2,
    f2_m,
    f2_v,
    gains,
    gains_m,
    gains_v,
    bias,
    bias_m,
    bias_v,
):
    n_model = lax.axis_size("mp")
    n_every = lax.axis_size(("dp", "mp"))
    device_at = lax.axis_index(("dp", "mp"))
    model_at = lax.axis_index("mp")
    data_at = lax.axis_index("dp")
    hist_dev = lengths.shape[1]
    tok_group = hist_dev * LEN
    look = tok_group // n_model
    capacity = max(2, 2 * look // n_every)
    heads_dev = bias.shape[0]
    width_dev = heads_dev * DH
    table_rows = table.astype(jnp.bfloat16)
    w1_low = w_f1.astype(jnp.bfloat16)
    w2_low = w_f2.astype(jnp.bfloat16)
    gain_in = gains[0]
    gain_attn = lax.dynamic_slice_in_dim(gains[1], model_at * width_dev, width_dev)
    gain_out = gains[2]
    start = model_at * look
    row_index = jnp.arange(tok_group)
    place = row_index % LEN
    hist_of = row_index // LEN
    table_grad = jnp.zeros(table.shape, jnp.float32)
    grad_one = jnp.zeros(w_f1.shape, jnp.float32)
    grad_two = jnp.zeros(w_f2.shape, jnp.float32)
    grad_bias = jnp.zeros(bias.shape, jnp.float32)
    gain_grad = jnp.zeros(gains.shape, jnp.float32)
    loss_sum = jnp.float32(0.0)
    loss_count = jnp.float32(0.0)
    for micro_idx in range(MB):
        lens = lengths[micro_idx]
        neg_ids = negatives[micro_idx]
        owner_blk = lax.dynamic_slice_in_dim(owners[micro_idx].reshape(tok_group), start, look)
        local_blk = lax.dynamic_slice_in_dim(item_rows[micro_idx].reshape(tok_group), start, look)
        onehot = (owner_blk[:, None] == jnp.arange(n_every)[None, :]).astype(jnp.int32)
        slot_of = jnp.sum((jnp.cumsum(onehot, 0) - 1) * onehot, 1)
        position = owner_blk * capacity + slot_of
        request = (
            jnp.full((n_every * capacity,), -1, jnp.int32)
            .at[position]
            .set(local_blk)
            .reshape(n_every, capacity)
        )
        asked = lax.all_to_all(request, ("dp", "mp"), split_axis=0, concat_axis=0, tiled=True)
        found = jnp.where(
            (asked >= 0)[..., None], table_rows[jnp.maximum(asked, 0)], jnp.zeros((), jnp.bfloat16)
        )
        returned = lax.all_to_all(found, ("dp", "mp"), split_axis=0, concat_axis=0, tiled=True)
        x_block = returned.reshape(n_every * capacity, D)[position]
        x_group = lax.all_gather(x_block, "mp", axis=0, tiled=True)
        neg_mine = neg_ids // ROWS_DEV == device_at
        neg_local = neg_ids % ROWS_DEV
        neg_term = jnp.where(neg_mine[:, None], table_rows[neg_local].astype(jnp.float32), 0.0)
        neg_rows = lax.psum(neg_term, ("dp", "mp")).astype(jnp.bfloat16)
        inputs = x_group.astype(jnp.float32)
        normed_f, factor_in = norm_rows(inputs, gain_in)
        normed = normed_f.astype(jnp.bfloat16)
        hidden = jnp.dot(normed, w1_low, preferred_element_type=jnp.float32)
        act = jax.nn.silu(hidden).reshape(hist_dev, LEN, heads_dev, 4, DH)
        upper = act[:, :, :, 0, :].reshape(tok_group, width_dev)
        value_rows = act[:, :, :, 1, :].astype(jnp.bfloat16)
        queries = act[:, :, :, 2, :].astype(jnp.bfloat16)
        key_rows = act[:, :, :, 3, :].astype(jnp.bfloat16)
        bucket_hot = (buckets[micro_idx][..., None] == jnp.arange(NB)).astype(jnp.float32)
        key_bias = jnp.einsum("bkn,hn->bhk", bucket_hot, bias, precision=highest)
        attended = attend(queries, key_rows, value_rows, key_bias, lens).reshape(
            tok_group, width_dev
        )
        squares = lax.psum(jnp.sum(attended * attended, 1), "mp")
        factor_attn = lax.rsqrt(squares / D + epsilon)[:, None]
        normed_attn = attended * factor_attn * gain_attn
        gated_rows = (normed_attn * upper).astype(jnp.bfloat16)
        partial_out = jnp.dot(gated_rows, w2_low, preferred_element_type=jnp.float32)
        branch = lax.psum(partial_out, "mp")
        resid = inputs + branch
        valid_group = place + 1 < lens[hist_of]
        target_group = jnp.concatenate([x_group[1:], jnp.zeros((1, D), jnp.bfloat16)], 0)
        target = target_group.astype(jnp.float32)
        in_block = jnp.arange(tok_group) // look == model_at
        valid_f = valid_group.astype(jnp.float32)
        owned_f = (valid_group & in_block).astype(jnp.float32)
        output_f, factor_out = norm_rows(resid, gain_out)
        output = output_f.astype(jnp.bfloat16)
        scale = 2.0 * D ** (-0.5)
        neg_logits = jnp.dot(output, neg_rows.T, preferred_element_type=jnp.float32) * scale
        pos_logits = jnp.sum(output.astype(jnp.float32) * target, 1) * scale
        top = jnp.maximum(jnp.max(neg_logits, 1), pos_logits)
        neg_exp = jnp.exp(neg_logits - top[:, None])
        pos_exp = jnp.exp(pos_logits - top)
        total = pos_exp + jnp.sum(neg_exp, 1)
        per_row = top + jnp.log(total) - pos_logits
        loss_local = jnp.sum(per_row * owned_f)
        count_local = jnp.sum(owned_f)
        grad_neg = (neg_exp / total[:, None] * valid_f[:, None]).astype(jnp.bfloat16)
        grad_pos = (pos_exp / total - 1.0) * valid_f
        grad_output = (
            jnp.dot(grad_neg, neg_rows, preferred_element_type=jnp.float32) * scale
            + grad_pos[:, None] * target * scale
        )
        owned_neg = grad_neg * owned_f[:, None].astype(jnp.bfloat16)
        neg_grad_term = (
            jnp.einsum("rn,rd->nd", owned_neg, output, preferred_element_type=jnp.float32) * scale
        )
        target_grad = (grad_pos * owned_f)[:, None] * output.astype(jnp.float32) * scale
        grad_resid, grad_gain_out = norm_back(resid, factor_out, gain_out, grad_output, owned_f)
        grad_low = grad_resid.astype(jnp.bfloat16)
        grad_skip = lax.dynamic_slice_in_dim(grad_resid, start, look)
        grad_gated = jnp.einsum("td,fd->tf", grad_low, w2_low, preferred_element_type=jnp.float32)
        grad_two = grad_two + jnp.einsum(
            "tf,td->fd", gated_rows, grad_low, preferred_element_type=jnp.float32
        )
        grad_normed = grad_gated * upper
        grad_upper = grad_gated * normed_attn
        grad_gain_attn = jnp.sum(grad_normed * attended * factor_attn, 0)
        inner = lax.psum(jnp.sum(attended * gain_attn * grad_normed, 1), "mp")
        grad_attended = factor_attn * (
            gain_attn * grad_normed - attended * factor_attn * factor_attn * (inner / D)[:, None]
        )
        grad_attended = grad_attended.astype(jnp.bfloat16).reshape(hist_dev, LEN, heads_dev, DH)
        grad_queries, grad_keys, grad_values, grad_key_bias = attend_back(
            queries, key_rows, value_rows, key_bias, lens, grad_attended
        )
        grad_bias = grad_bias + jnp.einsum(
            "bkn,bhk->hn", bucket_hot, grad_key_bias, precision=highest
        )
        grad_act = jnp.stack(
            [
                grad_upper.reshape(hist_dev, LEN, heads_dev, DH),
                grad_values,
                grad_queries,
                grad_keys,
            ],
            3,
        )
        grad_act = grad_act.reshape(tok_group, 4 * width_dev)
        grad_hidden = (grad_act * silu_slope(hidden)).astype(jnp.bfloat16)
        grad_one = grad_one + jnp.einsum(
            "td,tf->df", normed, grad_hidden, preferred_element_type=jnp.float32
        )
        grad_normed_in = jnp.einsum(
            "tf,df->td", grad_hidden, w1_low, preferred_element_type=jnp.float32
        )
        grad_in_blk = lax.psum_scatter(grad_normed_in, "mp", scatter_dimension=0, tiled=True)
        target_own = lax.dynamic_slice_in_dim(target_grad, start, look)
        edge_row = from_behind(target_own[look - 1 :], "mp", 1)
        target_blk = jnp.concatenate([edge_row, target_own[: look - 1]], 0)
        factor_blk = lax.dynamic_slice_in_dim(factor_in, start, look)
        grad_x, grad_gain_in = norm_back(
            x_block.astype(jnp.float32),
            factor_blk,
            gain_in,
            grad_in_blk,
            jnp.ones((look,), jnp.float32),
        )
        grad_x = grad_x + grad_skip + target_blk
        outgoing = (
            jnp.zeros((n_every * capacity, D), jnp.float32)
            .at[position]
            .set(grad_x)
            .reshape(n_every, capacity, D)
        )
        attn_gain_full = lax.dynamic_update_slice(
            jnp.zeros((D,), jnp.float32), grad_gain_attn, (model_at * width_dev,)
        )
        gain_term = jnp.stack([grad_gain_in, attn_gain_full, grad_gain_out])
        neg_grad, gain_part, loss_part, count_part = lax.psum(
            (neg_grad_term, gain_term, loss_local, count_local), ("dp", "mp")
        )
        table_grad = table_grad.at[neg_local].add(jnp.where(neg_mine[:, None], neg_grad, 0.0))
        incoming = lax.all_to_all(outgoing, ("dp", "mp"), split_axis=0, concat_axis=0, tiled=True)
        asked_flat = asked.reshape(-1)
        incoming_flat = jnp.where((asked_flat >= 0)[:, None], incoming.reshape(-1, D), 0.0)
        table_grad = table_grad.at[jnp.maximum(asked_flat, 0)].add(incoming_flat)
        gain_grad = gain_grad + gain_part
        loss_sum = loss_sum + loss_part
        loss_count = loss_count + count_part
    grad_one, grad_two, grad_bias = lax.psum((grad_one, grad_two, grad_bias), "dp")
    dense_squares = (
        jnp.sum(grad_one * grad_one) + jnp.sum(grad_two * grad_two) + jnp.sum(grad_bias * grad_bias)
    )
    local_squares = jnp.sum(table_grad * table_grad)
    local_squares = local_squares + jnp.where(data_at == 0, dense_squares, 0.0)
    local_squares = local_squares + jnp.where(device_at == 0, jnp.sum(gain_grad * gain_grad), 0.0)
    grad_norm = jnp.sqrt(lax.psum(local_squares, ("dp", "mp")))
    factor = jnp.minimum(1.0, clip_at / grad_norm)
    t_new, t_first, t_second = adam_step(table, table_grad * factor, table_m, table_v, 0.5, 0.1)
    a_new, a_first, a_second = adam_step(w_f1, grad_one * factor, f1_m, f1_v, 0.04, 0.1)
    b_new, b_first, b_second = adam_step(w_f2, grad_two * factor, f2_m, f2_v, 0.04, 0.1)
    c_new, c_first, c_second = adam_step(gains, gain_grad * factor, gains_m, gains_v, 0.5, 0.0)
    e_new, e_first, e_second = adam_step(bias, grad_bias * factor, bias_m, bias_v, 1.0, 0.0)
    return (
        loss_sum,
        loss_count,
        grad_norm,
        t_new,
        t_first,
        t_second,
        t_new.astype(jnp.bfloat16),
        a_new,
        a_first,
        a_second,
        a_new.astype(jnp.bfloat16),
        b_new,
        b_first,
        b_second,
        b_new.astype(jnp.bfloat16),
        c_new,
        c_first,
        c_second,
        e_new,
        e_first,
        e_second,
    )


def solution(mesh):
    in_specs = (
        P(None, "dp"),
        P(None, "dp", None, None),
        P(None, "dp", None),
        P(None, "dp", None),
        P(),
        P(("dp", "mp"), None),
        P(("dp", "mp"), None),
        P(("dp", "mp"), None),
        P(None, "mp"),
        P(None, "mp"),
        P(None, "mp"),
        P("mp", None),
        P("mp", None),
        P("mp", None),
        P(),
        P(),
        P(),
        P("mp", None),
        P("mp", None),
        P("mp", None),
    )
    out_specs = (
        P(),
        P(),
        P(),
        P(("dp", "mp"), None),
        P(("dp", "mp"), None),
        P(("dp", "mp"), None),
        P(("dp", "mp"), None),
        P(None, "mp"),
        P(None, "mp"),
        P(None, "mp"),
        P(None, "mp"),
        P("mp", None),
        P("mp", None),
        P("mp", None),
        P("mp", None),
        P(),
        P(),
        P(),
        P("mp", None),
        P("mp", None),
        P("mp", None),
    )
    return jax.shard_map(
        per_device, mesh=mesh, in_specs=in_specs, out_specs=out_specs, check_vma=False
    )
```

profile of v0, /device:TPU:0, one launch (start us, length us, event | category | flops | bytes accessed | tf_op | source)
XLA Modules:
  0.0 1289.4 jit_solution(4313566803962635376)
XLA Ops:
  11.7 7.3 all-to-all-start
  29.5 5.8 all-to-all-start.2
  47.8 11.9 all-to-all-done.1
  59.7 4.1 all-to-all-start.4
  70.9 4.5 all-to-all-start.3
  80.8 22.0 %all-to-all-done.3 = bf16[32,16,512]{2,1,0:T(8,128)(2,1)S(1)} async-done(((bf16[32,16,512]{2,1,0:T(8,128)(2,1)}), bf16[32,16,512]{2,1,0:T(8,128)(2,1)S(1)}, u32[]{:S(2)}, u32[]{:S(2)}) %all-to-all-start.3) | async-done | bytes 524320 | tf_op jit(solution)/shard_map/all_to_all | solution.py:170
  102.8 3.4 all-to-all-start.6
  113.3 4.5 all-to-all-start.5
  123.1 20.3 %all-to-all-done.5 = bf16[32,16,512]{2,1,0:T(8,128)(2,1)S(1)} async-done(((bf16[32,16,512]{2,1,0:T(8,128)(2,1)}), bf16[32,16,512]{2,1,0:T(8,128)(2,1)S(1)}, u32[]{:S(2)}, u32[]{:S(2)}) %all-to-all-start.5) | async-done | bytes 524320 | tf_op jit(solution)/shard_map/all_to_all | solution.py:170
  148.4 5.3 all-to-all-start.7
  158.2 15.9 %all-to-all-done.7 = bf16[32,16,512]{2,1,0:T(8,128)(2,1)S(1)} async-done(((bf16[32,16,512]{2,1,0:T(8,128)(2,1)}), bf16[32,16,512]{2,1,0:T(8,128)(2,1)S(1)}, u32[]{:S(2)}, u32[]{:S(2)}) %all-to-all-start.7) | async-done | bytes 524320 | tf_op jit(solution)/shard_map/all_to_all | solution.py:170
  177.5 4.3 fusion.43
  191.8 3.6 fusion.41
  196.6 18.0 %all-gather.15.cloned.1.call-done = bf16[1024,512]{1,0:T(8,128)(2,1)} async-done(((bf16[256,512]{1,0:T(8,128)(2,1)}), bf16[1024,512]{1,0:T(8,128)(2,1)}) %all-gather.15.cloned.1.call-update) | async-done | bytes 1048592 | tf_op jit(solution)/shard_map/all_gather | solution.py:172
  216.2 3.6 fusion.40
  221.7 4.5 fusion.252
  226.3 4.5 fusion.250
  230.8 4.5 fusion.248
  235.3 19.5 %divide_convert_fusion = (bf16[2,1024,1024]{2,1,0:T(8,128)(2,1)S(1)}, bf16[2,1024,1024]{2,1,0:T(8,128)(2,1)S(1)}, bf16[2,1024,1024]{2,1,0:T(8,128)(2,1)S(1)}, bf...) fusion(f32[2,1024]{1,0:T(2,128)S(1)} %copy-done.205, f32[1024]{0:T(1024)S(1)} %copy-done.181, ...), kind=kOutput, calls=%fused_computation.36 | convolution fusion | flops 343932928 | bytes 55087104 | tf_op jit(solution)/shard_map/bqhd,bkhd->bhqk/dot_general | solution.py:56
  254.9 5.3 fusion.148
  268.7 18.5 %all-reduce.9 = (f32[1024]{0:T(1024)}, f32[1024]{0:T(1024)}, f32[1024]{0:T(1024)}, f32[1024]{0:T(1024)}) all-reduce(f32[1024]{0:T(1024)} %get-tuple-element.193, f32[1024]{0:T(1024)} %get-tuple-element.195, f32[1024]{0:T(1024)} %get-tuple-element.197, f32[1024]{0:T(1024)} %get-tuple-element.199), channel_id=1, replica_groups=mesh['dp'=8,'mp'=4] {'mp'}, use_global_device_ids=true, to_apply=%region_6.7 | all-reduce | flops 4096 | bytes 32768 | tf_op jit(solution)/shard_map/psum | solution.py:191
  322.1 112.5 %all-reduce.21 = (bf16[512,512]{1,0:T(8,128)(2,1)}, bf16[512,512]{1,0:T(8,128)(2,1)S(1)}, bf16[512,512]{1,0:T(8,128)(2,1)}, bf16[512,512]{1,0:T(8,128)(2,1)}) all-reduce(f32[512,512]{1,0:T(8,128)S(1)} %convert_select_fusion.3, f32[512,512]{1,0:T(8,128)} %convert_select_fusion.2, ...), channel_id=1, replica_groups=mesh['dp'=8,'mp'=4] {'dp','mp'}, use_global_device_ids=true, to_apply=%region_9.10 | all-reduce | flops 1048576 | bytes 6291456 | tf_op jit(solution)/shard_map/psum | solution.py:176
  440.9 166.4 %all-reduce.20.cloned.1.call-done = (f32[1024,512]{1,0:T(8,128)}, f32[1024,512]{1,0:T(8,128)}, f32[1024,512]{1,0:T(8,128)}, f32[1024,512]{1,0:T(8,128)}) async-done(((f32[1024,512]{1,0:T(8,128)}, f32[1024,512]{1,0:T(8,128)}, f32[1024,512]{1,0:T(8,128)}, f32[1024,512]{1,0:T(8,128)}), (f32[1024,512]{1,0:T(8,128)}, f32[1024,512]{1,0:T(8,128)}, f32[1024,512]{1,0:T(8,128)}, ...) | async-done | bytes 8388624 | tf_op jit(solution)/shard_map/psum | solution.py:196
  613.7 4.1 fusion.319
  637.0 3.4 fusion.30
  652.0 16.4 %all-reduce.8 = (f32[1024]{0:T(1024)S(1)}, f32[1024]{0:T(1024)S(1)}, f32[1024]{0:T(1024)S(1)}, f32[1024]{0:T(1024)S(1)}) all-reduce(f32[1024]{0:T(1024)S(1)} %get-tuple-element.168, f32[1024]{0:T(1024)S(1)} %get-tuple-element.171, f32[1024]{0:T(1024)S(1)} %get-tuple-element.174, ...), channel_id=1, replica_groups=mesh['dp'=8,'mp'=4] {'mp'}, use_global_device_ids=true, to_apply=%region_72.73 | all-reduce | flops 4096 | bytes 32768 | tf_op jit(solution)/shard_map/psum | solution.py:237
  673.1 7.9 convert_reduce_fusion
  689.9 3.2 convolution_bitcast_fusion.1
  693.1 7.8 convert_reduce_fusion.1
  709.0 3.2 convolution_bitcast_fusion.2
  712.3 7.2 convert_reduce_fusion.2
  727.6 3.2 convolution_bitcast_fusion.3
  730.8 7.5 convert_reduce_fusion.3
  760.1 17.8 %reduce-scatter.9.cloned.1.call-done = f32[256,512]{1,0:T(8,128)} async-done(((f32[1024,512]{1,0:T(8,128)}), f32[256,512]{1,0:T(8,128)}) %reduce-scatter.9.cloned.1.call-update) | async-done | bytes 524304 | tf_op jit(solution)/shard_map/reduce_scatter | solution.py:265
  777.9 45.5 %reduce-scatter.7.cloned.1.call-done = f32[256,512]{1,0:T(8,128)} async-done(((f32[1024,512]{1,0:T(8,128)}), f32[256,512]{1,0:T(8,128)}) %reduce-scatter.7.cloned.1.call-update) | async-done | bytes 524304 | tf_op jit(solution)/shard_map/reduce_scatter | solution.py:265
  823.4 45.6 %reduce-scatter.5.cloned.1.call-done = f32[256,512]{1,0:T(8,128)} async-done(((f32[1024,512]{1,0:T(8,128)}), f32[256,512]{1,0:T(8,128)}) %reduce-scatter.5.cloned.1.call-update) | async-done | bytes 524304 | tf_op jit(solution)/shard_map/reduce_scatter | solution.py:265
  871.5 3.2 scatter_custom_fusion.5
  874.6 3.9 all-to-all-start.8
  881.5 3.9 collective-permute-start.2
  888.1 3.4 collective-permute-start.1
  898.8 3.9 scatter_custom_fusion.11
  904.6 8.0 all-to-all-start.10
  920.7 3.2 convolution_multiply_fusion.1
  928.5 9.1 all-to-all-done.10
  937.7 4.6 all-to-all-start.9
  943.5 3.7 collective-permute-start.3
  947.2 3.2 convolution_multiply_fusion.3
  954.4 14.7 %psum.282 = f32[2,128]{1,0:T(2,128)S(1)} all-reduce(f32[2,128]{1,0:T(2,128)S(1)} %convolution_add_fusion.6), channel_id=1, replica_groups=mesh['dp'=8,'mp'=4] {'dp'}, use_global_device_ids=true, to_apply=%region_113.114 | all-reduce | flops 256 | bytes 2048 | tf_op jit(solution)/shard_map/psum | solution.py:299
  969.2 3.2 scatter_custom_fusion.14
  972.4 3.6 all-to-all-start.11
  979.3 13.3 %all-reduce.18.cloned.1.call-done = (f32[512,512]{1,0:T(8,128)}, f32[128,512]{1,0:T(8,128)}) async-done(((f32[512,512]{1,0:T(8,128)}, f32[128,512]{1,0:T(8,128)}), (f32[512,512]{1,0:T(8,128)}, f32[128,512]{1,0:T(8,128)})) %all-reduce.18.cloned.1.call-update) | async-done | bytes 1310736 | tf_op jit(solution)/shard_map/psum | solution.py:299
  998.3 146.3 %all-reduce.16.cloned.1.call-done = (f32[512,512]{1,0:T(8,128)}, f32[512,512]{1,0:T(8,128)}, f32[512,512]{1,0:T(8,128)}, f32[512,512]{1,0:T(8,128)}) async-done(((f32[512,512]{1,0:T(8,128)}, f32[512,512]{1,0:T(8,128)}, f32[512,512]{1,0:T(8,128)}, f32[512,512]{1,0:T(8,128)}), (f32[512,512]{1,0:T(8,128)}, f32[512,512]{1,0:T(8,128)}, f32[512,512]{1,0:T(8,128)}, ...) | async-done | bytes 4194320 | tf_op jit(solution)/shard_map/psum | solution.py:288
  1144.6 4.8 scatter_custom_fusion.4
  1149.4 39.2 %psum.296 = f32[3,512]{1,0:T(4,128)S(1)} all-reduce(f32[3,512]{1,0:T(4,128)S(1)} %fusion.269), channel_id=1, replica_groups=mesh['dp'=8,'mp'=4] {'dp','mp'}, use_global_device_ids=true, to_apply=%region_118.119 | all-reduce | flops 1536 | bytes 12288 | tf_op jit(solution)/shard_map/psum | solution.py:288
  1191.3 4.2 scatter_fusion
  1195.5 5.0 scatter_custom_fusion.7
  1201.9 4.4 scatter_fusion.1
  1206.4 5.0 scatter_custom_fusion.10
  1212.8 4.2 scatter_fusion.2
  1217.0 5.0 scatter_custom_fusion.13
  1223.5 4.2 scatter_fusion.3
  1229.4 40.3 %all-reduce.4 = (f32[]{:T(128)}, f32[]{:T(128)}, f32[]{:T(128)}) all-reduce(f32[]{:T(128)S(6)} %add.1138, f32[]{:T(128)S(6)} %add.1141, f32[]{:T(128)S(6)} %add.1177), channel_id=1, replica_groups=mesh['dp'=8,'mp'=4] {'dp','mp'}, use_global_device_ids=true, to_apply=%region_14.15 | all-reduce | flops 3 | bytes 24 | tf_op jit(solution)/shard_map/psum | solution.py:288
  1273.7 4.1 fusion.315
  1277.8 3.4 fusion.317
  (774 shorter events, 263.3 us)
Async XLA Ops:
  9.6 37.9 %copy-start.180 = (s32[256,1]{0,1:T(1,128)}, s32[256,1]{0,1:T(1,128)S(1)}, u32[]{:S(2)}) copy-start(s32[256,1]{0,1:T(1,128)S(1)} %compare_select_fusion.7) | copy-start | bytes 3076
  11.7 17.7 %all-to-all-start = ((s32[32,1,16]{2,1,0:T(1,128)}), s32[32,1,16]{2,1,0:T(1,128)S(1)}, u32[]{:S(2)}, u32[]{:S(2)}) async-start(s32[32,1,16]{2,1,0:T(1,128)} %bitcast.8), calls=%async_computation | async-start | bytes 32768 | tf_op jit(solution)/shard_map/all_to_all | solution.py:166
  25.0 22.5 %copy-start.178 = (s32[256,1]{0,1:T(1,128)}, s32[256,1]{0,1:T(1,128)S(1)}, u32[]{:S(2)}) copy-start(s32[256,1]{0,1:T(1,128)S(1)} %compare_select_fusion.6) | copy-start | bytes 3076
  29.5 12.9 %all-to-all-start.2 = ((s32[32,1,16]{2,1,0:T(1,128)}), s32[32,1,16]{2,1,0:T(1,128)S(1)}, u32[]{:S(2)}, u32[]{:S(2)}) async-start(s32[32,1,16]{2,1,0:T(1,128)} %bitcast.37), calls=%async_computation.2 | async-start | bytes 32768 | tf_op jit(solution)/shard_map/all_to_all | solution.py:166
  42.4 17.3 %all-to-all-start.1 = ((bf16[32,16,512]{2,1,0:T(8,128)(2,1)}), bf16[32,16,512]{2,1,0:T(8,128)(2,1)S(1)}, u32[]{:S(2)}, u32[]{:S(2)}) async-start(bf16[32,16,512]{2,1,0:T(8,128)(2,1)} %broadcast_select_fusion.3), calls=%async_computation.1 | async-start | bytes 1048576 | tf_op jit(solution)/shard_map/all_to_all | solution.py:170
  47.6 29.8 %copy-start.177 = (s32[256,1]{0,1:T(1,128)}, s32[256,1]{0,1:T(1,128)S(1)}, u32[]{:S(2)}) copy-start(s32[256,1]{0,1:T(1,128)S(1)} %compare_select_fusion.4) | copy-start | bytes 3076
  47.7 29.8 %copy-start.187 = (s32[1,1,1024]{2,1,0:T(1,128)}, s32[1,1,1024]{2,1,0:T(1,128)S(1)}, u32[]{:S(2)}) copy-start(s32[1,1,1024]{2,1,0:T(1,128)S(1)} %get-tuple-element.113) | copy-start | bytes 12292
  47.7 30.9 %copy-start.183 = (s32[1,1,1024]{2,1,0:T(1,128)}, s32[1,1,1024]{2,1,0:T(1,128)S(1)}, u32[]{:S(2)}) copy-start(s32[1,1,1024]{2,1,0:T(1,128)S(1)} %get-tuple-element.112) | copy-start | bytes 12292
  47.7 31.9 %copy-start.189 = (s32[1,1,1024]{2,1,0:T(1,128)}, s32[1,1,1024]{2,1,0:T(1,128)S(1)}, u32[]{:S(2)}) copy-start(s32[1,1,1024]{2,1,0:T(1,128)S(1)} %get-tuple-element.114) | copy-start | bytes 12292
  47.7 72.3 %copy-start.185 = (s32[1,1,1024]{2,1,0:T(1,128)}, s32[1,1,1024]{2,1,0:T(1,128)S(1)}, u32[]{:S(2)}) copy-start(s32[1,1,1024]{2,1,0:T(1,128)S(1)} %get-tuple-element.115) | copy-start | bytes 12292
  59.7 11.2 all-to-all-start.4
  63.8 112.2 %all-gather.9.cloned.1.call-start = ((), (), s32[]{:S(2)}) async-start(), calls=%async_computation.20 | async-start | bytes 1310720 | tf_op jit(solution)/shard_map/all_gather | solution.py:172
  70.9 31.9 %all-to-all-start.3 = ((bf16[32,16,512]{2,1,0:T(8,128)(2,1)}), bf16[32,16,512]{2,1,0:T(8,128)(2,1)S(1)}, u32[]{:S(2)}, u32[]{:S(2)}) async-start(bf16[32,16,512]{2,1,0:T(8,128)(2,1)} %broadcast_select_fusion.2), calls=%async_computation.3 | async-start | bytes 1048576 | tf_op jit(solution)/shard_map/all_to_all | solution.py:170
  80.8 27.7 %copy-start.125 = (s32[32,1,16]{0,2,1:T(8,128)}, s32[32,1,16]{0,2,1:T(8,128)S(1)}, u32[]{:S(2)}) copy-start(s32[32,1,16]{0,2,1:T(8,128)S(1)} %copy.107) | copy-start | bytes 6148
  102.8 10.5 all-to-all-start.6
  106.2 75.6 %all-gather.11.cloned.1.call-start = ((), (), s32[]{:S(2)}) async-start(), calls=%async_computation.21 | async-start | bytes 1310720 | tf_op jit(solution)/shard_map/all_gather | solution.py:172
  113.3 30.1 %all-to-all-start.5 = ((bf16[32,16,512]{2,1,0:T(8,128)(2,1)}), bf16[32,16,512]{2,1,0:T(8,128)(2,1)S(1)}, u32[]{:S(2)}, u32[]{:S(2)}) async-start(bf16[32,16,512]{2,1,0:T(8,128)(2,1)} %broadcast_select_fusion.1), calls=%async_computation.5 | async-start | bytes 1048576 | tf_op jit(solution)/shard_map/all_to_all | solution.py:170
  117.8 72.5 %all-gather.13.cloned.1.call-start = ((), (), s32[]{:S(2)}) async-start(), calls=%async_computation.22 | async-start | bytes 1310720 | tf_op jit(solution)/shard_map/all_gather | solution.py:172
  120.0 96.1 %copy-start.24 = (bf16[512,512]{1,0:T(8,128)(2,1)}, bf16[512,512]{1,0:T(8,128)(2,1)S(1)}, u32[]{:S(2)}) copy-start(bf16[512,512]{1,0:T(8,128)(2,1)S(1)} %convert_element_type.482) | copy-start | bytes 1572868
  121.7 70.1 %copy-start.128 = (f32[1,512]{1,0:T(1,128)}, f32[1,512]{1,0:T(1,128)S(1)}, u32[]{:S(2)}) copy-start(f32[1,512]{1,0:T(1,128)S(1)} %get-tuple-element.141) | copy-start | bytes 6148
  123.0 24.4 %copy-start.123 = (s32[32,1,16]{0,2,1:T(8,128)}, s32[32,1,16]{0,2,1:T(8,128)S(1)}, u32[]{:S(2)}) copy-start(s32[32,1,16]{0,2,1:T(8,128)S(1)} %copy.115) | copy-start | bytes 6148
  148.4 25.6 %all-to-all-start.7 = ((bf16[32,16,512]{2,1,0:T(8,128)(2,1)}), bf16[32,16,512]{2,1,0:T(8,128)(2,1)S(1)}, u32[]{:S(2)}, u32[]{:S(2)}) async-start(bf16[32,16,512]{2,1,0:T(8,128)(2,1)} %broadcast_select_fusion), calls=%async_computation.7 | async-start | bytes 1048576 | tf_op jit(solution)/shard_map/all_to_all | solution.py:170
  153.7 60.9 %all-gather.15.cloned.1.call-start = ((), (), s32[]{:S(2)}) async-start(), calls=%async_computation.23 | async-start | bytes 1310720 | tf_op jit(solution)/shard_map/all_gather | solution.py:172
  175.9 431.3 %all-reduce.20.cloned.1.call-start = ((), (), s32[]{:S(2)}) async-start(), calls=%async_computation.26 | async-start | bytes 16777216 | tf_op jit(solution)/shard_map/psum | solution.py:196
  184.7 105.2 %copy-start.37 = (f32[1,1024,2,1,64]{1,4,3,2,0:T(8,128)}, f32[1,1024,2,1,64]{1,4,3,2,0:T(8,128)S(1)}, u32[]{:S(2)}) copy-start(f32[1,1024,2,1,64]{1,4,3,2,0:T(8,128)S(1)} %slice.276) | copy-start | bytes 1572868
  265.9 24.1 %copy-start.39 = (f32[1,1024,2,1,64]{1,4,3,2,0:T(8,128)S(1)}, f32[1,1024,2,1,64]{1,4,3,2,0:T(8,128)}, u32[]{:S(2)}) copy-start(f32[1,1024,2,1,64]{1,4,3,2,0:T(8,128)} %slice.282) | copy-start | bytes 1572868
  299.4 460.7 %reduce-scatter.11.cloned.1.call-start = ((), (), s32[]{:S(2)}) async-start(), calls=%async_computation.19 | async-start | bytes 2621440 | tf_op jit(solution)/shard_map/reduce_scatter | solution.py:265
  314.5 120.0 %copy-start.171 = (pred[512]{0:T(512)(128)(4,1)}, pred[512]{0:T(512)(128)(4,1)S(1)}, u32[]{:S(2)}) copy-start(pred[512]{0:T(512)(128)(4,1)S(1)} %fusion.283) | copy-start | bytes 1540
  315.7 118.9 %copy-start.169 = (pred[512]{0:T(512)(128)(4,1)}, pred[512]{0:T(512)(128)(4,1)S(1)}, u32[]{:S(2)}) copy-start(pred[512]{0:T(512)(128)(4,1)S(1)} %fusion.284) | copy-start | bytes 1540
  689.9 88.0 %reduce-scatter.9.cloned.1.call-start = ((), (), s32[]{:S(2)}) async-start(), calls=%async_computation.18 | async-start | bytes 2621440 | tf_op jit(solution)/shard_map/reduce_scatter | solution.py:265
  708.9 114.5 %reduce-scatter.7.cloned.1.call-start = ((), (), s32[]{:S(2)}) async-start(), calls=%async_computation.17 | async-start | bytes 2621440 | tf_op jit(solution)/shard_map/reduce_scatter | solution.py:265
  727.5 141.5 %reduce-scatter.5.cloned.1.call-start = ((), (), s32[]{:S(2)}) async-start(), calls=%async_computation.16 | async-start | bytes 2621440 | tf_op jit(solution)/shard_map/reduce_scatter | solution.py:265
  746.2 122.8 %copy-start.76 = (bf16[256,512]{1,0:T(8,128)(2,1)S(1)}, bf16[256,512]{1,0:T(8,128)(2,1)}, u32[]{:S(2)}) copy-start(bf16[256,512]{1,0:T(8,128)(2,1)} %gather_fusion.4) | copy-start | bytes 786436
  746.2 122.8 %copy-start.77 = (bf16[256,512]{1,0:T(8,128)(2,1)S(1)}, bf16[256,512]{1,0:T(8,128)(2,1)}, u32[]{:S(2)}) copy-start(bf16[256,512]{1,0:T(8,128)(2,1)} %gather_fusion.10) | copy-start | bytes 786436
  746.2 122.8 %copy-start.79 = (bf16[256,512]{1,0:T(8,128)(2,1)S(1)}, bf16[256,512]{1,0:T(8,128)(2,1)}, u32[]{:S(2)}) copy-start(bf16[256,512]{1,0:T(8,128)(2,1)} %gather_fusion.1) | copy-start | bytes 786436
  746.2 122.8 %copy-start.80 = (bf16[256,512]{1,0:T(8,128)(2,1)S(1)}, bf16[256,512]{1,0:T(8,128)(2,1)}, u32[]{:S(2)}) copy-start(bf16[256,512]{1,0:T(8,128)(2,1)} %gather_fusion.7) | copy-start | bytes 786436
  746.2 122.8 %copy-start.129 = (f32[1,512]{1,0:T(1,128)S(1)}, f32[1,512]{1,0:T(1,128)}, u32[]{:S(2)}) copy-start(f32[1,512]{1,0:T(1,128)} %copy-done.128) | copy-start | bytes 6148
  758.8 112.7 %collective-permute-start = (f32[1,512]{1,0:T(1,128)S(1)}, f32[1,512]{1,0:T(1,128)S(1)}, u32[]{:S(2)}, u32[]{:S(2)}) collective-permute-start(f32[1,512]{1,0:T(1,128)S(1)} %slice.296), channel_id=1, source_target_pairs={{0,1},{1,2},{2,3},{4,5},{5,6},{6,7},{8,9},{9,10},{10,11},{12,13},{... | collective-permute-start | bytes 6152 | tf_op jit(solution)/shard_map/ppermute | solution.py:26
  874.6 29.0 %all-to-all-start.8 = ((f32[32,16,512]{2,1,0:T(8,128)}), f32[32,16,512]{2,1,0:T(8,128)S(1)}, u32[]{:S(2)}, u32[]{:S(2)}) async-start(f32[32,16,512]{2,1,0:T(8,128)} %bitcast.120), calls=%async_computation.9 | async-start | bytes 2097152 | tf_op jit(solution)/shard_map/all_to_all | solution.py:292
  881.5 17.3 %collective-permute-start.2 = (f32[1,512]{1,0:T(1,128)S(1)}, f32[1,512]{1,0:T(1,128)S(1)}, u32[]{:S(2)}, u32[]{:S(2)}) collective-permute-start(f32[1,512]{1,0:T(1,128)S(1)} %slice.300), channel_id=1, source_target_pairs={{0,1},{1,2},{2,3},{4,5},{5,6},{6,7},{8,9},{9,10},{10,11},{12,13},{... | collective-permute-start | bytes 6152 | tf_op jit(solution)/shard_map/ppermute | solution.py:26
  888.1 37.6 %collective-permute-start.1 = (f32[1,512]{1,0:T(1,128)S(1)}, f32[1,512]{1,0:T(1,128)S(1)}, u32[]{:S(2)}, u32[]{:S(2)}) collective-permute-start(f32[1,512]{1,0:T(1,128)S(1)} %slice.298), channel_id=1, source_target_pairs={{0,1},{1,2},{2,3},{4,5},{5,6},{6,7},{8,9},{9,10},{10,11},{12,13},{... | collective-permute-start | bytes 6152 | tf_op jit(solution)/shard_map/ppermute | solution.py:26
  904.6 33.1 %all-to-all-start.10 = ((f32[32,16,512]{2,1,0:T(8,128)}), f32[32,16,512]{2,1,0:T(8,128)}, u32[]{:S(2)}, u32[]{:S(2)}) async-start(f32[32,16,512]{2,1,0:T(8,128)} %bitcast.617), calls=%async_computation.13 | async-start | bytes 2097152 | tf_op jit(solution)/shard_map/all_to_all | solution.py:292
  912.6 80.0 %all-reduce.18.cloned.1.call-start = ((), (), s32[]{:S(2)}) async-start(), calls=%async_computation.25 | async-start | bytes 2621440 | tf_op jit(solution)/shard_map/psum | solution.py:299
  937.7 34.7 %all-to-all-start.9 = ((f32[32,16,512]{2,1,0:T(8,128)}), f32[32,16,512]{2,1,0:T(8,128)S(1)}, u32[]{:S(2)}, u32[]{:S(2)}) async-start(f32[32,16,512]{2,1,0:T(8,128)} %bitcast.616), calls=%async_computation.11 | async-start | bytes 2097152 | tf_op jit(solution)/shard_map/all_to_all | solution.py:292
  942.2 202.3 %all-reduce.16.cloned.1.call-start = ((), (), s32[]{:S(2)}) async-start(), calls=%async_computation.24 | async-start | bytes 8388608 | tf_op jit(solution)/shard_map/psum | solution.py:288
  943.5 25.6 %collective-permute-start.3 = (f32[1,512]{1,0:T(1,128)S(1)}, f32[1,512]{1,0:T(1,128)S(1)}, u32[]{:S(2)}, u32[]{:S(2)}) collective-permute-start(f32[1,512]{1,0:T(1,128)S(1)} %slice.302), channel_id=1, source_target_pairs={{0,1},{1,2},{2,3},{4,5},{5,6},{6,7},{8,9},{9,10},{10,11},{12,13},{... | collective-permute-start | bytes 6152 | tf_op jit(solution)/shard_map/ppermute | solution.py:26
  972.3 172.2 %copy-start.176 = (pred[512]{0:T(512)(128)(4,1)S(1)}, pred[512]{0:T(512)(128)(4,1)}, u32[]{:S(2)}) copy-start(pred[512]{0:T(512)(128)(4,1)} %copy-done.175) | copy-start | bytes 1540
  972.4 172.2 %copy-start.73 = (f32[32,16,512]{2,1,0:T(8,128)}, f32[32,16,512]{2,1,0:T(8,128)S(1)}, u32[]{:S(2)}) copy-start(f32[32,16,512]{2,1,0:T(8,128)S(1)} %all-to-all-done.9) | copy-start | bytes 3145732
  972.4 249.6 %all-to-all-start.11 = ((f32[32,16,512]{2,1,0:T(8,128)}), f32[32,16,512]{2,1,0:T(8,128)}, u32[]{:S(2)}, u32[]{:S(2)}) async-start(f32[32,16,512]{2,1,0:T(8,128)} %bitcast.165), calls=%async_computation.15 | async-start | bytes 2097152 | tf_op jit(solution)/shard_map/all_to_all | solution.py:292
  975.9 173.4 %copy-start.150 = (f32[512]{0:T(512)S(1)}, f32[512]{0:T(512)}, u32[]{:S(2)}) copy-start(f32[512]{0:T(512)} %get-tuple-element.21) | copy-start | bytes 6148
  975.9 173.4 %copy-start.151 = (f32[512]{0:T(512)S(1)}, f32[512]{0:T(512)}, u32[]{:S(2)}) copy-start(f32[512]{0:T(512)} %get-tuple-element.155) | copy-start | bytes 6148
  975.9 173.4 %copy-start.152 = (f32[512]{0:T(512)S(1)}, f32[512]{0:T(512)}, u32[]{:S(2)}) copy-start(f32[512]{0:T(512)} %get-tuple-element.25) | copy-start | bytes 6148
  975.9 173.4 %copy-start.191 = (f32[512]{0:T(512)S(1)}, f32[512]{0:T(512)}, u32[]{:S(2)}) copy-start(f32[512]{0:T(512)} %get-tuple-element.27) | copy-start | bytes 6148
  1144.6 46.7 %copy-start.141 = (s32[512]{0:T(512)S(1)}, s32[512]{0:T(512)}, u32[]{:S(2)}) copy-start(s32[512]{0:T(512)} %copy-done.140) | copy-start | bytes 6148
  1223.4 47.0 %copy-start.193 = (f32[2,128]{1,0:T(2,128)S(1)}, f32[2,128]{1,0:T(2,128)}, u32[]{:S(2)}) copy-start(f32[2,128]{1,0:T(2,128)} %param.37) | copy-start | bytes 3076
  1223.4 47.0 %copy-start.194 = (f32[2,128]{1,0:T(2,128)S(1)}, f32[2,128]{1,0:T(2,128)}, u32[]{:S(2)}) copy-start(f32[2,128]{1,0:T(2,128)} %param.38) | copy-start | bytes 3076
  1223.4 47.0 %copy-start.195 = (f32[2,128]{1,0:T(2,128)S(1)}, f32[2,128]{1,0:T(2,128)}, u32[]{:S(2)}) copy-start(f32[2,128]{1,0:T(2,128)} %param.39) | copy-start | bytes 3076
  1223.4 47.6 %copy-start.139 = (f32[3,512]{1,0:T(4,128)S(1)}, f32[3,512]{1,0:T(4,128)}, u32[]{:S(2)}) copy-start(f32[3,512]{1,0:T(4,128)} %param.34) | copy-start | bytes 18436
  1223.4 47.6 %copy-start.153 = (f32[3,512]{1,0:T(4,128)S(1)}, f32[3,512]{1,0:T(4,128)}, u32[]{:S(2)}) copy-start(f32[3,512]{1,0:T(4,128)} %param.35) | copy-start | bytes 18436
  1223.4 47.6 %copy-start.154 = (f32[3,512]{1,0:T(4,128)S(1)}, f32[3,512]{1,0:T(4,128)}, u32[]{:S(2)}) copy-start(f32[3,512]{1,0:T(4,128)} %param.36) | copy-start | bytes 18436
  1223.4 48.2 %copy-start.110 = (f32[128,512]{1,0:T(8,128)S(1)}, f32[128,512]{1,0:T(8,128)}, u32[]{:S(2)}) copy-start(f32[128,512]{1,0:T(8,128)} %param.31) | copy-start | bytes 786436
  1223.5 48.2 %copy-start.111 = (f32[128,512]{1,0:T(8,128)S(1)}, f32[128,512]{1,0:T(8,128)}, u32[]{:S(2)}) copy-start(f32[128,512]{1,0:T(8,128)} %get-tuple-element.61) | copy-start | bytes 786436
  1223.5 48.2 %copy-start.118 = (f32[128,512]{1,0:T(8,128)S(1)}, f32[128,512]{1,0:T(8,128)}, u32[]{:S(2)}) copy-start(f32[128,512]{1,0:T(8,128)} %param.32) | copy-start | bytes 786436
  1227.7 46.0 %copy-start.66 = (f32[512,512]{1,0:T(8,128)S(1)}, f32[512,512]{1,0:T(8,128)}, u32[]{:S(2)}) copy-start(f32[512,512]{1,0:T(8,128)} %param.28) | copy-start | bytes 3145732
  (173 other events, 765.4 us)
Sparse Core Ops, SparseCore 0:
  66.2 40.9 all-gather.8
  109.3 40.6 all-gather.10
  152.2 33.7 all-gather.12
  188.0 26.5 all-gather.14
  299.5 307.6 all-reduce.19
  690.0 42.2 reduce-scatter.10
  734.7 43.1 reduce-scatter.8
  780.2 43.1 reduce-scatter.6
  825.8 43.1 reduce-scatter.4
  920.8 71.7 all-reduce.17
  1000.7 143.8 all-reduce.15
where the time goes:
time: 1300 us; the launch traced here: 1290 us
  waiting for transfers between devices  539 us (41%)
  blocking collectives  242 us (19%)
  matrix products  171 us (13%)
  other arithmetic  153 us (12%)
  local copies, waits for them, and re-layouts  86.2 us (7%)
  starting transfers between devices  70.8 us (5%)
  between operations  28 us (2%)
    psum x1, waiting for transfers between devices, per_device(): branch = lax.psum(partial_out, 'mp')  166 us
    psum x1, waiting for transfers between devices, per_device(): lax.psum((neg_grad_term, gain_term, loss_local, count_local), ('dp', 'mp'))  146 us
    psum x1, blocking collectives, per_device(): neg_rows = lax.psum(neg_term, ('dp', 'mp')).astype(jnp.bfloat16)  112 us
    reduce_scatter x4, waiting for transfers between devices, per_device(): lax.psum_scatter(grad_normed_in, 'mp', scatter_dimension=0, tiled=True)  109 us
    psum x2, blocking collectives, per_device(): lax.psum((neg_grad_term, gain_term, loss_local, count_local), ('dp', 'mp'))  79.5 us
    all_to_all x4, waiting for transfers between devices, per_device(): lax.all_to_all(found, ('dp', 'mp'), split_axis=0, concat_axis=0, tiled=True)  70.1 us
    dot_general x4, matrix products, raw_scores(): jnp.einsum('bqhd,bkhd->bhqk', queries, key_rows, preferred_element_type=j...  33 us
    dot_general x4, matrix products, attend_back(): jnp.einsum('bqhd,bkhd->bhqk', grad_out, value_rows, preferred_element_typ...  30.4 us
  transfers between devices with their start and end apart: 27, of which 16 were waited for; matrix products, arithmetic and copies ran while one was open for 18% of the time, Pallas kernels for 0%

commit v1 on v0

v1 whole, which is shorter than its diff:
```python
import functools

import jax
import jax.numpy as jnp
from jax import lax
from jax.experimental import pallas as pl
from jax.experimental.pallas import tpu as pltpu
from jax.sharding import PartitionSpec as P

DH = 64
D = 512
NB = 128
LEN = 1024
MB = 4
STEP = 10

TB = 256
NT = LEN // TB
HEADS = D // DH
PAIRS = HEADS // 2
WIDE = 2 * DH
CH = 16
LANES = 128
ASK = 4

epsilon = 1e-06
clip_at = 1.0
beta_one = 0.9
beta_two = 0.95
adam_floor = 1e-08
highest = lax.Precision.HIGHEST
f32 = jnp.float32
bf16 = jnp.bfloat16
MESH = pl.DeviceIdType.MESH
VM = pl.BlockSpec(memory_space=pltpu.VMEM)
LIMIT = 60 * 1024 * 1024

NN = (((1,), (0,)), ((), ()))
NT_ = (((1,), (1,)), ((), ()))
TN = (((0,), (0,)), ((), ()))


def mm(a, b, dims=NN):
    return lax.dot_general(a, b, dims, preferred_element_type=f32)


def spot(index, n_model):
    return (index // n_model, lax.rem(index, n_model))


def greet(n_every, n_model, me):
    barrier = pltpu.get_barrier_semaphore()

    def signal(i, carry):
        pl.semaphore_signal(
            barrier, inc=1, device_id=spot(lax.rem(me + i, n_every), n_model), device_id_type=MESH
        )
        return carry

    lax.fori_loop(1, n_every, signal, 0)
    pl.semaphore_wait(barrier, n_every - 1)


def fetch_kernel(
    n_data, n_model, groups, table_ref, req_ref, got_ref, asked_ref, low_ref, send_ref,
    ask_send, ask_recv, row_send, row_recv, own_sem,
):
    n_every = n_data * n_model
    slots = groups * CH
    rows_dev = table_ref.shape[0]
    me = lax.axis_index("dp") * n_model + lax.axis_index("mp")
    greet(n_every, n_model, me)

    def ask(i, carry):
        to = lax.rem(me + i, n_every)
        pltpu.make_async_remote_copy(
            src_ref=req_ref.at[to],
            dst_ref=asked_ref.at[me],
            send_sem=ask_send.at[to],
            recv_sem=ask_recv.at[me],
            device_id=spot(to, n_model),
            device_id_type=MESH,
        ).start()
        return carry

    lax.fori_loop(1, n_every, ask, 0)
    asked_ref[me] = req_ref[me]
    low_ref[...] = table_ref[...].astype(bf16)
    eye = lax.broadcasted_iota(jnp.int32, (LANES, LANES), 0) == lax.broadcasted_iota(
        jnp.int32, (LANES, LANES), 1
    )
    lane = lax.broadcasted_iota(jnp.int32, (ASK * slots, rows_dev), 1).astype(f32)

    def asked_copy(src):
        return pltpu.make_async_remote_copy(
            src_ref=req_ref.at[src],
            dst_ref=asked_ref.at[src],
            send_sem=ask_send.at[src],
            recv_sem=ask_recv.at[src],
            device_id=spot(src, n_model),
            device_id_type=MESH,
        )

    def row_copy(src, dst, to):
        return pltpu.make_async_remote_copy(
            src_ref=send_ref.at[to],
            dst_ref=got_ref.at[:, dst],
            send_sem=row_send.at[to],
            recv_sem=row_recv.at[src],
            device_id=spot(to, n_model),
            device_id_type=MESH,
        )

    def serve(first, own):
        columns = []
        for j in range(ASK):
            src = lax.rem(me + first + j, n_every)
            if not (own and j == 0):
                asked_copy(src).wait_recv()
            wanted = jnp.broadcast_to(asked_ref[src], (LANES, LANES))
            column = jnp.sum(jnp.where(eye, wanted, 0.0), axis=1, keepdims=True)
            columns.append(column[:slots])
        column = jnp.concatenate(columns, axis=0)
        hot = jnp.where(lane == column, 1.0, 0.0).astype(bf16)
        found = mm(hot, low_ref[...]).astype(bf16)
        for j in range(ASK):
            to = lax.rem(me + first + j, n_every)
            piece = found[j * slots : (j + 1) * slots].reshape(groups, CH, D)
            send_ref[to] = piece
            if own and j == 0:
                pltpu.make_async_copy(send_ref.at[to], got_ref.at[:, me], own_sem).start()
            else:
                row_copy(me, me, to).start()

    serve(0, True)

    def more(b, carry):
        serve(b * ASK, False)
        return carry

    lax.fori_loop(1, n_every // ASK, more, 0)

    def finish(i, carry):
        other = lax.rem(me + i, n_every)
        asked_copy(other).wait_send()
        row_copy(other, other, other).wait_send()
        row_copy(other, other, other).wait_recv()
        return carry

    lax.fori_loop(1, n_every, finish, 0)
    pltpu.make_async_copy(send_ref.at[me], got_ref.at[:, me], own_sem).wait()


def fetch(table, req, n_data, n_model, groups):
    n_every = n_data * n_model
    slots = groups * CH
    return pl.pallas_call(
        functools.partial(fetch_kernel, n_data, n_model, groups),
        out_shape=(
            jax.ShapeDtypeStruct((groups, n_every, CH, D), bf16),
            jax.ShapeDtypeStruct((n_every, 1, LANES), f32),
        ),
        in_specs=[VM, VM],
        out_specs=(VM, VM),
        scratch_shapes=[
            pltpu.VMEM(table.shape, bf16),
            pltpu.VMEM((n_every, groups, CH, D), bf16),
            pltpu.SemaphoreType.DMA((n_every,)),
            pltpu.SemaphoreType.DMA((n_every,)),
            pltpu.SemaphoreType.DMA((n_every,)),
            pltpu.SemaphoreType.DMA((n_every,)),
            pltpu.SemaphoreType.DMA,
        ],
        compiler_params=pltpu.CompilerParams(
            collective_id=0, has_side_effects=True, vmem_limit_bytes=LIMIT
        ),
        cost_estimate=pl.CostEstimate(
            flops=2 * n_every * slots * table.shape[0] * D,
            bytes_accessed=8 * n_every * slots * D,
            transcendentals=0,
        ),
    )(table, req)


def give_kernel(
    n_data, n_model, out_ref, pack_ref, got_ref, packs_ref, row_send, row_recv, pack_send, pack_recv, own_sem
):
    n_every = n_data * n_model
    me = lax.axis_index("dp") * n_model + lax.axis_index("mp")
    greet(n_every, n_model, me)

    def row_copy(src, dst, to):
        return pltpu.make_async_remote_copy(
            src_ref=out_ref.at[:, to],
            dst_ref=got_ref.at[dst],
            send_sem=row_send.at[to],
            recv_sem=row_recv.at[src],
            device_id=spot(to, n_model),
            device_id_type=MESH,
        )

    def pack_copy(src, dst, to):
        return pltpu.make_async_remote_copy(
            src_ref=pack_ref,
            dst_ref=packs_ref.at[dst],
            send_sem=pack_send.at[to],
            recv_sem=pack_recv.at[src],
            device_id=spot(to, n_model),
            device_id_type=MESH,
        )

    def start(i, carry):
        to = lax.rem(me + i, n_every)
        row_copy(me, me, to).start()
        pack_copy(me, me, to).start()
        return carry

    lax.fori_loop(1, n_every, start, 0)
    own = pltpu.make_async_copy(out_ref.at[:, me], got_ref.at[me], own_sem)
    own.start()
    packs_ref[me] = pack_ref[...]

    def finish(i, carry):
        other = lax.rem(me + i, n_every)
        row_copy(other, other, other).wait_send()
        row_copy(other, other, other).wait_recv()
        pack_copy(other, other, other).wait_send()
        pack_copy(other, other, other).wait_recv()
        return carry

    lax.fori_loop(1, n_every, finish, 0)
    own.wait()


def give(out, pack, n_data, n_model):
    groups, n_every = out.shape[:2]
    return pl.pallas_call(
        functools.partial(give_kernel, n_data, n_model),
        out_shape=(
            jax.ShapeDtypeStruct((n_every, groups, CH, D), bf16),
            jax.ShapeDtypeStruct((n_every,) + pack.shape, f32),
        ),
        in_specs=[VM, VM],
        out_specs=(VM, VM),
        scratch_shapes=[pltpu.SemaphoreType.DMA((n_every,))] * 4 + [pltpu.SemaphoreType.DMA],
        compiler_params=pltpu.CompilerParams(
            collective_id=1, has_side_effects=True, vmem_limit_bytes=LIMIT
        ),
        cost_estimate=pl.CostEstimate(
            flops=0, bytes_accessed=4 * out.size * 4, transcendentals=0
        ),
    )(out, pack)


def silu_parts(values):
    sigma = 0.5 + 0.5 * jnp.tanh(0.5 * values)
    return sigma, sigma * (1.0 + values * (1.0 - sigma))


def halves(tile):
    low = lax.broadcasted_iota(jnp.int32, tile.shape, 1) < DH
    zero = jnp.zeros_like(tile)
    return jnp.concatenate([jnp.where(low, tile, zero), jnp.where(low, zero, tile)], axis=0)


def beside(tile):
    half = tile.shape[0] // 2
    return jnp.concatenate([tile[:half], tile[half:]], axis=1)


def row_sum(values):
    return jnp.sum(values, axis=0, keepdims=True)


def ahead_kernel(
    group_len, got_ref, slot_ref, w1_ref, w2_ref, kb_ref, neg_ref, gains_ref, live_ref,
    x_ref, n1_ref, q_ref, k_ref, v_ref, do_ref, ghu_ref, gres_ref, gw2_ref, gneg_ref, stat_ref,
    xf_ref, hu_ref, o_ref, carry_ref,
):
    slots = got_ref.shape[1]
    gain_in = gains_ref[0:1, :]
    gain_attn = gains_ref[1:2, :]
    gain_out = gains_ref[2:3, :]

    def inputs(i, carry):
        rows = pl.ds(pl.multiple_of(i * TB, TB), TB)
        group = i * TB // group_len
        hot = (
            lax.broadcasted_iota(jnp.int32, (TB, slots), 1) == slot_ref[rows, :]
        )
        x = mm(jnp.where(hot, 1.0, 0.0).astype(bf16), got_ref[group])
        x_ref[rows, :] = x.astype(bf16)
        xf_ref[rows, :] = x
        factor = lax.rsqrt(jnp.mean(x * x, -1, keepdims=True) + epsilon)
        n1 = (x * factor * gain_in).astype(bf16)
        n1_ref[rows, :] = n1
        hu_ref[rows, :] = mm(n1, w1_ref[0], NT_)
        for c, ref in ((1, v_ref), (2, q_ref), (3, k_ref)):
            hidden = mm(n1, w1_ref[c], NT_)
            act = (hidden * silu_parts(hidden)[0]).astype(bf16)
            if c == 2:
                act = act * jnp.asarray(0.5 * DH ** (-0.5), bf16)
            for p in range(PAIRS):
                ref[p, rows, :] = act[:, p * WIDE : (p + 1) * WIDE]
        return carry

    lax.fori_loop(0, NT, inputs, 0)
    xf_ref[LEN:, :] = jnp.zeros((8, D), f32)
    carry_ref[...] = jnp.zeros_like(carry_ref)
    stat_ref[...] = jnp.zeros_like(stat_ref)
    gw2_ref[...] = jnp.zeros_like(gw2_ref)
    gneg_ref[...] = jnp.zeros_like(gneg_ref)
    scale = 2.0 * D ** (-0.5)
    in_row = lax.broadcasted_iota(jnp.int32, (2 * TB, TB), 0)
    in_col = lax.broadcasted_iota(jnp.int32, (2 * TB, TB), 1)
    causal = in_col <= lax.rem(in_row, TB)
    first_half = in_row < TB

    def block(i, carry):
        rows = pl.ds(pl.multiple_of(i * TB, TB), TB)
        place = lax.broadcasted_iota(jnp.int32, (TB, 1), 0) + i * TB
        inv = 1.0 / (place.astype(f32) + 1.0)
        inv2 = jnp.concatenate([inv, inv], axis=0)
        for p in range(PAIRS):
            q2 = halves(q_ref[p, rows, :])

            def part(j, total, masked, p=p, q2=q2):
                keys = pl.ds(pl.multiple_of(j * TB, TB), TB)
                kb = kb_ref[p, j]
                h = mm(q2, k_ref[p, keys, :], NT_) + jnp.where(first_half, kb[0:1, :], kb[1:2, :])
                w = (h + h * jnp.tanh(h)) * inv2
                if masked:
                    w = jnp.where(causal, w, 0.0)
                return total + mm(beside(w.astype(bf16)), halves(v_ref[p, keys, :]))

            total = lax.fori_loop(
                0, i, functools.partial(part, masked=False), jnp.zeros((TB, WIDE), f32)
            )
            o_ref[p] = part(i, total, True)
        o = jnp.concatenate([o_ref[p] for p in range(PAIRS)], axis=1)
        factor_attn = lax.rsqrt(jnp.mean(o * o, -1, keepdims=True) + epsilon)
        na = o * factor_attn * gain_attn
        hu = hu_ref[rows, :]
        sigma, slope = silu_parts(hu)
        upper = hu * sigma
        gated = (na * upper).astype(bf16)
        y = xf_ref[rows, :] + mm(gated, w2_ref[...])
        factor_out = lax.rsqrt(jnp.mean(y * y, -1, keepdims=True) + epsilon)
        z = (y * factor_out * gain_out).astype(bf16)
        zf = z.astype(f32)
        after = xf_ref[pl.ds(pl.multiple_of(i * TB + TB, 8), 8), :]
        last = lax.broadcasted_iota(jnp.int32, (TB, 1), 0) == TB - 1
        target = jnp.where(last, after[0:1, :], pltpu.roll(xf_ref[rows, :], TB - 1, 0))
        neg_logits = mm(z, neg_ref[...], NT_) * scale
        pos = jnp.sum(zf * target, -1, keepdims=True) * scale
        top = jnp.maximum(jnp.max(neg_logits, -1, keepdims=True), pos)
        neg_exp = jnp.exp(neg_logits - top)
        pos_exp = jnp.exp(pos - top)
        total = pos_exp + jnp.sum(neg_exp, -1, keepdims=True)
        live = live_ref[rows, :]
        per = (top + jnp.log(total) - pos) * live
        gneg = (neg_exp / total * live).astype(bf16)
        gpos = (pos_exp / total - 1.0) * live
        gz = mm(gneg, neg_ref[...]) * scale + gpos * target * scale
        gneg_ref[...] += mm(gneg, z, TN) * scale
        target_grad = gpos * zf * scale
        first = lax.broadcasted_iota(jnp.int32, (TB, 1), 0) == 0
        shifted = jnp.where(first, carry_ref[0:1, :], pltpu.roll(target_grad, 1, 0))
        carry_ref[0:1, :] = target_grad[TB - 1 : TB, :]
        scaled = gz * gain_out
        gy = factor_out * (
            scaled - y * factor_out * factor_out * jnp.mean(y * scaled, -1, keepdims=True)
        )
        gres_ref[rows, :] = gy + shifted
        low = gy.astype(bf16)
        gg = mm(low, w2_ref[...], NT_)
        gw2_ref[...] += mm(gated, low, TN)
        gnorm = gg * upper
        gup = gg * na
        og = gain_attn * gnorm
        inner = jnp.sum(o * og, -1, keepdims=True)
        go = factor_attn * (og - o * factor_attn * factor_attn * (inner / D))
        go = go.astype(bf16)
        for p in range(PAIRS):
            do_ref[p, rows, :] = go[:, p * WIDE : (p + 1) * WIDE]
        ghu_ref[rows, :] = (gup * slope).astype(bf16)
        stat_ref[1:2, :] += row_sum(gnorm * o * factor_attn)
        stat_ref[2:3, :] += row_sum(gz * y * factor_out)
        stat_ref[3:4, :] += jnp.broadcast_to(row_sum(per), (1, D))
        stat_ref[4:5, :] += jnp.broadcast_to(row_sum(live), (1, D))
        return carry

    lax.fori_loop(0, NT, block, 0)


def ahead(got, slot_col, w1, w2, kb, neg, gains, live, group_len):
    sds = jax.ShapeDtypeStruct
    pairs_shape = sds((PAIRS, LEN, WIDE), bf16)
    return pl.pallas_call(
        functools.partial(ahead_kernel, group_len),
        out_shape=(
            sds((LEN, D), bf16), sds((LEN, D), bf16),
            pairs_shape, pairs_shape, pairs_shape, pairs_shape,
            sds((LEN, D), bf16), sds((LEN, D), f32),
            sds((D, D), f32), sds(neg.shape, f32), sds((8, D), f32),
        ),
        in_specs=[VM] * 8,
        out_specs=(VM,) * 11,
        scratch_shapes=[
            pltpu.VMEM((LEN + 8, D), f32),
            pltpu.VMEM((LEN, D), f32),
            pltpu.VMEM((PAIRS, TB, WIDE), f32),
            pltpu.VMEM((8, D), f32),
        ],
        compiler_params=pltpu.CompilerParams(vmem_limit_bytes=LIMIT),
        cost_estimate=pl.CostEstimate(
            flops=60_000_000_000, bytes_accessed=20_000_000, transcendentals=6_000_000
        ),
    )(got, slot_col, w1, w2, kb, neg, gains, live)


def back_kernel(
    group_len, x_ref, n1_ref, q_ref, k_ref, v_ref, do_ref, ghu_ref, gres_ref, kb_ref, w1_ref, gains_ref,
    slot_ref, bucket_ref, out_ref, gw1_ref, stat_ref,
    gh_ref, hid_ref, kt_ref, dq_ref, dk_ref, dv_ref, bs_ref,
):
    groups, slots = out_ref.shape[:2]
    gain_in = gains_ref[0:1, :]

    def inputs(i, carry):
        rows = pl.ds(pl.multiple_of(i * TB, TB), TB)
        for c in (1, 2, 3):
            hid_ref[c - 1, rows, :] = mm(n1_ref[rows, :], w1_ref[c], NT_)
        return carry

    lax.fori_loop(0, NT, inputs, 0)
    bs_ref[...] = jnp.zeros_like(bs_ref)
    in_row = lax.broadcasted_iota(jnp.int32, (2 * TB, TB), 0)
    in_col = lax.broadcasted_iota(jnp.int32, (2 * TB, TB), 1)
    causal = lax.rem(in_row, TB) <= in_col
    ones_lane = lax.broadcasted_iota(jnp.int32, (2 * TB, LANES), 1)
    ones_half = lax.broadcasted_iota(jnp.int32, (2 * TB, LANES), 0) >= TB

    for p in range(PAIRS):
        lanes = slice(p * WIDE, (p + 1) * WIDE)
        dq_ref[...] = jnp.zeros_like(dq_ref)
        mark = jnp.where(
            ones_lane == jnp.where(ones_half, 2 * p + 1, 2 * p), 1.0, 0.0
        ).astype(bf16)

        def keys_step(j, carry, p=p, lanes=lanes, mark=mark):
            keys = pl.ds(pl.multiple_of(j * TB, TB), TB)
            k2 = halves(k_ref[p, keys, :])
            v2 = halves(v_ref[p, keys, :])
            kt = k_ref[p, keys, :].astype(f32).T
            low = lax.broadcasted_iota(jnp.int32, kt.shape, 0) < DH
            kt2 = jnp.concatenate(
                [jnp.where(low, kt, 0.0), jnp.where(low, 0.0, kt)], axis=1
            ).astype(bf16)
            kb = jnp.concatenate(
                [kb_ref[keys, 2 * p : 2 * p + 1], kb_ref[keys, 2 * p + 1 : 2 * p + 2]], axis=0
            )
            dk_ref[...] = jnp.zeros_like(dk_ref)
            dv_ref[...] = jnp.zeros_like(dv_ref)

            def part(i, masked):
                rows = pl.ds(pl.multiple_of(i * TB, TB), TB)
                q = q_ref[p, rows, :]
                do = do_ref[p, rows, :]
                place = lax.broadcasted_iota(jnp.int32, (1, TB), 1) + i * TB
                inv = 1.0 / (place.astype(f32) + 1.0)
                h = mm(k2, q, NT_) + kb
                t = jnp.tanh(h)
                m = h * t
                w = (h + m) * inv
                ds = mm(v2, do, NT_) * ((1.0 + t) * (0.5 * inv)) * (1.0 + h - m)
                if masked:
                    w = jnp.where(causal, w, 0.0)
                    ds = jnp.where(causal, ds, 0.0)
                ds = ds.astype(bf16)
                dv_ref[...] += mm(beside(w.astype(bf16)), halves(do))
                dk_ref[...] += mm(beside(ds), jnp.concatenate([halves(q), mark], axis=1))
                dq_ref[i] += mm(kt2, ds)

            part(j, True)

            def later(i, inner):
                part(i, False)
                return inner

            lax.fori_loop(j + 1, NT, later, 0)
            slope_v = silu_parts(hid_ref[0, keys, lanes])[1]
            slope_k = silu_parts(hid_ref[2, keys, lanes])[1]
            gh_ref[0, keys, lanes] = (dv_ref[...] * slope_v).astype(bf16)
            gh_ref[2, keys, lanes] = (dk_ref[:, :WIDE] * 2.0 * slope_k).astype(bf16)
            bs_ref[keys, :] += dk_ref[:, WIDE:]
            return carry

        lax.fori_loop(0, NT, keys_step, 0)
        for i in range(NT):
            rows = slice(i * TB, (i + 1) * TB)
            slope_q = silu_parts(hid_ref[1, rows, lanes])[1]
            gh_ref[1, rows, lanes] = (dq_ref[i].T * DH ** (-0.5) * slope_q).astype(bf16)

    stat_ref[...] = jnp.zeros_like(stat_ref)
    hot = jnp.where(
        lax.broadcasted_iota(jnp.int32, (LEN, NB), 1) == bucket_ref[...], 1.0, 0.0
    )
    bias_grad = lax.dot_general(bs_ref[...], hot, TN, precision=highest, preferred_element_type=f32)
    stat_ref[8:16, 0:NB] = bias_grad[0:8, :]
    gw1_ref[0] = mm(ghu_ref[...], n1_ref[...], TN)
    for c in (1, 2, 3):
        gw1_ref[c] = mm(gh_ref[c - 1], n1_ref[...], TN)
    per_group = group_len // TB

    def outputs(i, carry):
        rows = pl.ds(pl.multiple_of(i * TB, TB), TB)
        gn = mm(ghu_ref[rows, :], w1_ref[0])
        for c in (1, 2, 3):
            gn += mm(gh_ref[c - 1, rows, :], w1_ref[c])
        x = x_ref[rows, :].astype(f32)
        factor = lax.rsqrt(jnp.mean(x * x, -1, keepdims=True) + epsilon)
        scaled = gn * gain_in
        gx = factor * (scaled - x * factor * factor * jnp.mean(x * scaled, -1, keepdims=True))
        gx = (gx + gres_ref[rows, :]).astype(bf16)
        stat_ref[0:1, :] += row_sum(gn * x * factor)
        group = i // per_group
        hot = lax.broadcasted_iota(jnp.int32, (slots, TB), 0) == slot_ref[i]
        mine = mm(jnp.where(hot, 1.0, 0.0).astype(bf16), gx).astype(bf16)
        if per_group == 1:
            out_ref[group] = mine
        else:
            out_ref[group] = jnp.where(lax.rem(i, per_group) == 0, mine, out_ref[group] + mine)
        return carry

    lax.fori_loop(0, NT, outputs, 0)


def back(x, n1, q, k, v, do, ghu, gres, kb, w1, gains, slot_row, bucket, groups, slots):
    sds = jax.ShapeDtypeStruct
    return pl.pallas_call(
        functools.partial(back_kernel, LEN // groups),
        out_shape=(sds((groups, slots, D), bf16), sds(w1.shape, f32), sds((16, D), f32)),
        in_specs=[VM] * 13,
        out_specs=(VM,) * 3,
        scratch_shapes=[
            pltpu.VMEM((3, LEN, D), bf16),
            pltpu.VMEM((3, LEN, D), f32),
            pltpu.VMEM((8, LANES), f32),
            pltpu.VMEM((NT, WIDE, TB), f32),
            pltpu.VMEM((TB, WIDE + LANES), f32),
            pltpu.VMEM((TB, WIDE), f32),
            pltpu.VMEM((LEN, LANES), f32),
        ],
        compiler_params=pltpu.CompilerParams(vmem_limit_bytes=LIMIT),
        cost_estimate=pl.CostEstimate(
            flops=60_000_000_000, bytes_accessed=20_000_000, transcendentals=6_000_000
        ),
    )(x, n1, q, k, v, do, ghu, gres, kb, w1, gains, slot_row, bucket)


def adam_step(weight, grad, first, second, rate, decay):
    first_new = beta_one * first + (1.0 - beta_one) * grad
    second_new = beta_two * second + (1.0 - beta_two) * grad * grad
    fix_one = 1.0 - beta_one**STEP
    fix_two = 1.0 - beta_two**STEP
    move = first_new / fix_one / (jnp.sqrt(second_new / fix_two) + adam_floor) + decay * weight
    return (weight - rate * move, first_new, second_new)


def pick(array, index):
    return lax.dynamic_index_in_dim(array, index, 0, keepdims=False)


def per_device(
    lengths, owners, item_rows, buckets, negatives, table, table_m, table_v, w_f1, f1_m, f1_v,
    w_f2, f2_m, f2_v, gains, gains_m, gains_v, bias, bias_m, bias_v,
):
    n_model = lax.axis_size("mp")
    n_data = lax.axis_size("dp")
    n_every = n_model * n_data
    device_at = lax.axis_index(("dp", "mp"))
    model_at = lax.axis_index("mp")
    rows_dev = table.shape[0]
    copies = n_model // MB
    micro = model_at // copies
    lead = (lax.rem(model_at, copies) == 0).astype(f32)
    look = LEN // n_model
    cap = max(2, 2 * look // n_every)
    group_len = look * max(1, CH // cap)
    groups = LEN // group_len
    slots = n_every * CH
    heads_dev = bias.shape[0]
    fw = heads_dev * DH

    owner = pick(owners, micro).reshape(groups, group_len)
    local = pick(item_rows, micro).reshape(groups, group_len)
    bucket = pick(buckets, micro).reshape(LEN)
    length = pick(lengths, micro)[0]
    owner_hot = (owner[..., None] == jnp.arange(n_every)).astype(bf16)
    spots = jnp.arange(group_len)
    earlier = (spots[None, :] < spots[:, None]).astype(bf16)
    before = jnp.einsum("ij,gjn->gin", earlier, owner_hot, preferred_element_type=f32)
    rank = jnp.sum(before * owner_hot.astype(f32), -1)
    slot = owner * CH + rank.astype(jnp.int32)
    slot_hot = (slot[:, None, :] == jnp.arange(slots)[None, :, None]).astype(bf16)
    marked = local + 1
    digits = jnp.stack([marked // 32, marked % 32], -1).astype(bf16)
    found = jnp.einsum("gse,gev->gsv", slot_hot, digits, preferred_element_type=f32)
    want = (found[..., 0] * 32.0 + found[..., 1] - 1.0).reshape(groups, n_every, CH)
    want = want.transpose(1, 0, 2).reshape(n_every, 1, groups * CH)
    want = jnp.pad(want, ((0, 0), (0, 0), (0, LANES - groups * CH)), constant_values=-1.0)

    w1_mine = w_f1.astype(bf16).T
    weights = jnp.concatenate([w1_mine, w_f2.astype(bf16)], 0)
    every = lax.all_gather(weights, "mp", axis=0)
    w1 = every[:, : 4 * fw].reshape(n_model, heads_dev, 4, DH, D)
    w1 = w1.transpose(2, 0, 1, 3, 4).reshape(4, D, D)
    w2 = every[:, 4 * fw :].reshape(D, D)
    bias_all = lax.all_gather(bias, "mp", axis=0, tiled=True)
    bucket_hot = (bucket[:, None] == jnp.arange(NB)).astype(f32)
    key_bias = jnp.einsum("kn,hn->kh", bucket_hot, bias_all, precision=highest)
    in_length = jnp.arange(LEN) < length
    key_bias = jnp.where(in_length[:, None], 0.5 * key_bias, -1e30)
    kb_col = key_bias
    kb_row = key_bias.reshape(NT, TB, PAIRS, 2).transpose(2, 0, 3, 1)
    live = ((jnp.arange(LEN) + 1 < length).astype(f32) * lead)[:, None]

    neg_ids = negatives.reshape(-1)
    neg_mine = neg_ids // rows_dev == device_at
    neg_local = jnp.where(neg_mine, neg_ids % rows_dev, -1)
    neg_hot = (neg_local[:, None] == jnp.arange(rows_dev)).astype(bf16)
    neg_term = jnp.dot(neg_hot, table.astype(bf16), preferred_element_type=f32).astype(bf16)
    neg_all = lax.psum(neg_term, ("dp", "mp"))
    neg = pick(neg_all.reshape(MB, -1, D), micro)

    got, asked = fetch(table, want, n_data, n_model, groups)
    got = got.reshape(groups, slots, D)

    x, n1, q, k, v, do, ghu, gres, gw2, gneg, stat_a = ahead(
        got, slot.reshape(LEN, 1), w1, w2, kb_row, neg, gains, live, group_len
    )
    out, gw1, stat_b = back(
        x, n1, q, k, v, do, ghu, gres, kb_col, w1, gains,
        slot.reshape(NT, 1, TB), bucket.reshape(LEN, 1), groups, slots,
    )
    pack = jnp.concatenate([stat_b[0:1], stat_a[1:5], stat_b[8:16]], 0)
    pack = jnp.pad(pack, ((0, 3), (0, 0)))
    incoming, packs = give(out.reshape(groups, n_every, CH, D), pack, n_data, n_model)

    gneg_sum = lax.psum_scatter(gneg, "dp", scatter_dimension=0, tiled=True)
    gneg_all = lax.all_gather(gneg_sum.astype(bf16), ("dp", "mp"), axis=0)
    rows_neg = gneg.shape[0] // n_data
    gneg_all = gneg_all.reshape(n_data, MB, copies, rows_neg, D)[:, :, 0]
    gneg_all = gneg_all.transpose(1, 0, 2, 3).reshape(-1, D)
    grad_two = lax.psum(
        lax.psum_scatter(gw2, "mp", scatter_dimension=0, tiled=True), "dp"
    )
    gw1 = gw1.reshape(4, n_model, fw, D)
    grad_one = lax.psum(lax.psum_scatter(gw1, "mp", scatter_dimension=1, tiled=True), "dp")
    grad_one = grad_one.reshape(4, heads_dev, DH, D).transpose(3, 1, 0, 2).reshape(D, 4 * fw)

    sums = jnp.sum(packs, 0)
    gain_grad = sums[0:3]
    loss_sum = sums[3, 0]
    loss_count = sums[4, 0]
    grad_bias = lax.dynamic_slice_in_dim(sums[5:13, :NB], model_at * heads_dev, heads_dev)

    asked_flat = asked[:, 0, : groups * CH].reshape(-1)
    table_at = jnp.arange(rows_dev)
    hot_rows = (table_at[:, None].astype(f32) == asked_flat[None, :]).astype(bf16)
    table_grad = jnp.dot(hot_rows, incoming.reshape(-1, D), preferred_element_type=f32)
    hot_neg = (table_at[:, None] == neg_local[None, :]).astype(bf16)
    table_grad = table_grad + jnp.dot(hot_neg, gneg_all, preferred_element_type=f32)

    local = jnp.sum(table_grad * table_grad)
    dense = jnp.sum(grad_one * grad_one) + jnp.sum(grad_two * grad_two) + jnp.sum(grad_bias * grad_bias)
    local = local + jnp.where(lax.axis_index("dp") == 0, dense, 0.0)
    local = local + jnp.where(device_at == 0, jnp.sum(gain_grad * gain_grad), 0.0)
    grad_norm = jnp.sqrt(lax.psum(local, ("dp", "mp")))
    factor = jnp.minimum(1.0, clip_at / grad_norm)
    t_new, t_first, t_second = adam_step(table, table_grad * factor, table_m, table_v, 0.5, 0.1)
    a_new, a_first, a_second = adam_step(w_f1, grad_one * factor, f1_m, f1_v, 0.04, 0.1)
    b_new, b_first, b_second = adam_step(w_f2, grad_two * factor, f2_m, f2_v, 0.04, 0.1)
    c_new, c_first, c_second = adam_step(gains, gain_grad * factor, gains_m, gains_v, 0.5, 0.0)
    e_new, e_first, e_second = adam_step(bias, grad_bias * factor, bias_m, bias_v, 1.0, 0.0)
    return (
        loss_sum, loss_count, grad_norm,
        t_new, t_first, t_second, t_new.astype(bf16),
        a_new, a_first, a_second, a_new.astype(bf16),
        b_new, b_first, b_second, b_new.astype(bf16),
        c_new, c_first, c_second,
        e_new, e_first, e_second,
    )


def solution(mesh):
    rows, cols = P(("dp", "mp"), None), P(None, "mp")
    heads = P("mp", None)
    in_specs = (
        P(None, "dp"), P(None, "dp", None, None), P(None, "dp", None), P(None, "dp", None), P(),
        rows, rows, rows, cols, cols, cols, heads, heads, heads, P(), P(), P(), heads, heads, heads,
    )
    out_specs = (
        P(), P(), P(), rows, rows, rows, rows, cols, cols, cols, cols,
        heads, heads, heads, heads, P(), P(), P(), heads, heads, heads,
    )
    return jax.shard_map(
        per_device, mesh=mesh, in_specs=in_specs, out_specs=out_specs, check_vma=False
    )
```

time: 1300 us -> 646 us (0.50)
  waiting for transfers between devices: 539 us -> 191 us
  Pallas kernels: 0 us -> 308 us
  blocking collectives: 242 us -> 51.9 us
  matrix products: 171 us -> 14.3 us
  other arithmetic: 153 us -> 26.2 us
  starting transfers between devices: 70.8 us -> 0.69 us
  local copies, waits for them, and re-layouts: 86.2 us -> 31.2 us
    pallas_call x0 -> x4, Pallas kernels: none -> 308 us  [the longest x1 141 us: give(): pl.pallas_call(functools.partial(give_kernel, n_data, n_model), out_shape...]
    psum x6 -> x1, blocking collectives: 242 us -> 39.3 us  [per_device(): grad_norm = jnp.sqrt(lax.psum(local, ('dp', 'mp')))]
    psum x3 -> x2, waiting for transfers between devices: 326 us -> 156 us  [the longest x1 101 us: per_device(): neg_all = lax.psum(neg_term, ('dp', 'mp'))]
    dot_general x68 -> x6, matrix products: 171 us -> 14.3 us  [the longest x1 5.03 us: per_device(): jnp.dot(neg_hot, table.astype(bf16), preferred_element_type=f32)]
    all_to_all x12 -> x0, waiting for transfers between devices: 85.8 us -> none  [the longest x4 70.1 us: per_device(): lax.all_to_all(found, ('dp', 'mp'), split_axis=0, concat_axis=0, tiled=True)]
    reduce_scatter x4 -> x3, waiting for transfers between devices: 109 us -> 35 us  [the longest x1 35 us: per_device(): gneg_sum = lax.psum_scatter(gneg, 'dp', scatter_dimension=0, tiled=True)]
    all_to_all x12 -> x0, starting transfers between devices: 57.9 us -> none  [the longest x4 20.7 us: per_device(): lax.all_to_all(request, ('dp', 'mp'), split_axis=0, concat_axis=0, tiled=...]
    scatter-add x8 -> x0, other arithmetic: 36.7 us -> none  [the longest x4 19.8 us: per_device(): table_grad.at[neg_local].add(jnp.where(neg_mine[:, None], neg_grad, 0.0))]
  transfers between devices with their start and end apart: 27 -> 7, of which waited for: 16 -> 3; matrix products, arithmetic and copies ran while one was open for 18% -> 5% of each run, Pallas kernels for 0% -> 42%
where the time goes in v1:
time: 646 us; the launch traced here: 645 us
  Pallas kernels  308 us (48%)
  waiting for transfers between devices  191 us (30%)
  blocking collectives  51.9 us (8%)
  local copies, waits for them, and re-layouts  31.2 us (5%)
  other arithmetic  26.2 us (4%)
  between operations  21.1 us (3%)
  matrix products  14.3 us (2%)
    pallas_call x1, Pallas kernels, give(): pl.pallas_call(functools.partial(give_kernel, n_data, n_model), out_shape...  141 us
    psum x1, waiting for transfers between devices, per_device(): neg_all = lax.psum(neg_term, ('dp', 'mp'))  101 us
    pallas_call x1, Pallas kernels, fetch(): pl.pallas_call(functools.partial(fetch_kernel, n_data, n_model, groups),...  89.9 us
    psum x1, waiting for transfers between devices, per_device(): lax.psum(lax.psum_scatter(gw1, 'mp', scatter_dimension=1, tiled=True), 'dp')  55 us
    pallas_call x1, Pallas kernels, back(): pl.pallas_call(functools.partial(back_kernel, LEN // groups), out_shape=(...  41.4 us
    psum x1, blocking collectives, per_device(): grad_norm = jnp.sqrt(lax.psum(local, ('dp', 'mp')))  39.3 us
    pallas_call x1, Pallas kernels, ahead(): pl.pallas_call(functools.partial(ahead_kernel, group_len), out_shape=(sds...  35.5 us
    reduce_scatter x1, waiting for transfers between devices, per_device(): gneg_sum = lax.psum_scatter(gneg, 'dp', scatter_dimension=0, tiled=True)  35 us
  transfers between devices with their start and end apart: 7, of which 3 were waited for; matrix products, arithmetic and copies ran while one was open for 5% of the time, Pallas kernels for 42%

profile of v1, /device:TPU:0, one launch (start us, length us, event | category | flops | bytes accessed | tf_op | source)
XLA Modules:
  0.0 644.7 jit_solution(15324797414307012974)
XLA Ops:
  8.1 0.7 divide_bitcast_fusion
  8.8 0.7 fusion.33
  9.6 5.0 fusion.8
  14.7 0.9 copy-done.9
  15.6 0.1 copy.114
  15.7 0.2 copy-done.4
  16.0 0.9 pad_maximum_fusion
  17.0 0.7 dynamic-slice_add_fusion
  17.7 0.2 fusion.16
  18.0 0.5 fusion.9
  18.5 0.1 sub.37
  18.6 0.1 copy.112
  18.8 1.0 copy.120.slot_ref
  19.8 0.6 constant_dynamic-slice_fusion.2
  20.4 12.6 %all-gather.2 = f32[4,2,128]{2,1,0:T(2,128)S(1)} all-gather(f32[1,2,128]{2,1,0:T(2,128)S(1)} %bitcast.97), channel_id=1, replica_groups=mesh['dp'=8,'mp'=4] {'mp'}, dimensions={0}, use_global_device_ids=true | all-gather | bytes 5120 | tf_op jit(solution)/shard_map/all_gather | solution.py:620
  33.0 0.6 iota_compare_fusion.14
  33.7 1.3 fusion.14.kb_ref
  35.0 0.2 copy.118
  35.2 0.6 copy.139
  35.8 0.6 pad.8.req_ref
  36.4 1.5 fusion.21.live_ref
  38.0 89.9 %shard_map.355 = (bf16[4,32,16,512]{3,2,1,0:T(8,128)(2,1)}, f32[32,1,128]{2,1,0:T(1,128)}) custom-call(f32[784,512]{1,0:T(8,128)} %table_ref.1, f32[32,1,128]{2,1,0:T(1,128)} %pad.8.req_ref), custom_call_target="tpu_custom_call" | custom-call | flops 1644167168 | bytes 8388608 | tf_op jit(solution)/shard_map/pallas_call | solution.py:157
  127.9 101.2 %all-reduce.6.cloned.1.call-done = bf16[4,512,512]{2,1,0:T(8,128)(2,1)} async-done(((bf16[4,512,512]{2,1,0:T(8,128)(2,1)}), bf16[4,512,512]{2,1,0:T(8,128)(2,1)}) %all-reduce.6.cloned.1.call-update) | async-done | bytes 2097168 | tf_op jit(solution)/shard_map/psum | solution.py:634
  229.1 1.9 dynamic-slice_bitcast_fusion.neg_ref
  231.0 3.0 copy.115
  234.0 0.1 slice.50
  234.1 0.8 slice.51
  234.9 1.6 copy.116
  236.5 35.5 %shard_map.356 = (bf16[1024,512]{1,0:T(8,128)(2,1)}, bf16[1024,512]{1,0:T(8,128)(2,1)}, bf16[4,1024,128]{2,1,0:T(8,128)(2,1)}, bf16[4,1024,128]{2,1,0:T(8,128)(2...) custom-call(bf16[4,512,512]{2,1,0:T(8,128)(2,1)} %bitcast.99, ...), custom_call_target="tpu_custom_call" | custom-call | flops 60000002048 | bytes 20000000 | tf_op jit(solution)/shard_map/pallas_call | solution.py:399
  272.1 35.0 %reduce-scatter.4.cloned.1.call-done = f32[64,512]{1,0:T(8,128)} async-done(((f32[512,512]{1,0:T(8,128)}), f32[64,512]{1,0:T(8,128)}) %reduce-scatter.4.cloned.1.call-update) | async-done | bytes 131088 | tf_op jit(solution)/shard_map/reduce_scatter | solution.py:651
  307.1 1.5 convert_element_type.83
  308.8 1.0 copy.121.bucket_ref
  309.8 0.6 reshape_add_fusion.slot_ref
  310.4 0.2 reduce-scatter.6.cloned.1.call-start
  310.7 41.4 %shard_map.357 = (bf16[4,512,512]{2,1,0:T(8,128)(2,1)}, f32[4,512,512]{2,1,0:T(8,128)}, f32[16,512]{1,0:T(8,128)}) custom-call(bf16[1024,512]{1,0:T(8,128)(2,1)} %get-tuple-element.40.x_ref, bf16[1024,512]{1,0:T(8,128)(2,1)} %get-tuple-element.41.n1_ref, bf16[4,1024,128]{2,1,0:T(8,128)(2,1)} %get-tuple-element.42.q_ref, ...), custom_call_target="tpu_custom_call" | custom-call | flops 60000002048 | bytes 20000000 | tf_op jit(solution)/shard_map/pallas_call | solution.py:541
  352.0 4.8 copy.123
  356.8 0.3 all-reduce.8.cloned.1.call-start
  357.1 0.9 copy-done.5
  358.0 0.3 copy.128
  358.5 0.3 copy.124
  358.8 1.6 copy.126
  360.5 0.6 select_maximum_fusion.pack_ref
  361.1 141.2 %shard_map.358 = (bf16[32,4,16,512]{3,2,1,0:T(8,128)(2,1)}, f32[32,16,512]{2,1,0:T(8,128)}) custom-call(bf16[4,32,16,512]{3,2,1,0:T(8,128)(2,1)} %bitcast.83, f32[16,512]{1,0:T(8,128)} %select_maximum_fusion.pack_ref), custom_call_target="tpu_custom_call" | custom-call | bytes 16777216 | tf_op jit(solution)/shard_map/pallas_call | solution.py:237
  502.3 1.3 reduce_sum.64
  503.6 0.6 multiply_reduce_fusion.3
  504.9 0.6 multiply_reduce_fusion.4
  505.5 3.2 copy.122
  508.7 3.6 fusion.1
  512.3 3.8 multiply_reduce_fusion
  516.1 55.0 %all-reduce.8.cloned.1.call-done = (f32[4,1,128,512]{3,2,0,1:T(8,128)}, f32[128,512]{1,0:T(8,128)}) async-done(((f32[4,1,128,512]{3,2,0,1:T(8,128)}, f32[128,512]{1,0:T(8,128)}), (f32[4,1,128,512]{3,2,0,1:T(8,128)}, f32[128,512]{1,0:T(8,128)})) %all-reduce.8.cloned.1.call-update) | async-done | bytes 1310736 | tf_op jit(solution)/shard_map/psum | solution.py:660
  571.0 2.1 multiply_reduce_fusion.1
  573.1 1.6 multiply_reduce_fusion.2
  577.3 0.5 fusion.50
  577.9 39.3 %psum.31 = f32[]{:T(128)} all-reduce(f32[]{:T(128)S(6)} %add.254), channel_id=1, replica_groups=mesh['dp'=8,'mp'=4] {'dp','mp'}, use_global_device_ids=true, to_apply=%region_13.14 | all-reduce | flops 1 | bytes 8 | tf_op jit(solution)/shard_map/psum | solution.py:680
  617.9 1.3 broadcast_multiply_fusion
  619.3 2.4 fusion.45
  621.7 2.7 copy.129
  624.4 1.3 copy.130
  625.8 1.3 copy.131
  627.1 1.0 copy.132
  628.1 0.6 add_subtract_fusion
  628.7 0.6 multiply_subtract_fusion.3
  629.4 1.1 fusion.43
  630.4 5.8 fusion.48
  (96 shorter events, 1.0 us)
Async XLA Ops:
  8.0 25.7 %copy-start = (s32[4,1,1024]{2,1,0:T(1,128)S(1)}, s32[4,1,1024]{2,1,0:T(1,128)}, u32[]{:S(2)}) copy-start(s32[4,1,1024]{2,1,0:T(1,128)} %param.23) | copy-start | bytes 49156
  8.0 221.1 %all-reduce.6.cloned.1.call-start = ((), (), s32[]{:S(2)}) async-start(), calls=%async_computation.3 | async-start | bytes 4194304 | tf_op jit(solution)/shard_map/psum | solution.py:634
  14.6 0.9 copy-start.9
  14.6 1.3 copy-start.4
  14.6 216.3 %all-gather.6.cloned.1.call-start = ((), (), s32[]{:S(2)}) async-start(), calls=%async_computation.7 | async-start | bytes 3276800 | tf_op jit(solution)/shard_map/all_gather | solution.py:616
  15.9 1.0 copy-start.21
  16.9 2.9 copy-start.27
  16.9 3.5 copy-start.22
  16.9 290.2 %reduce-scatter.4.cloned.1.call-start = ((), (), s32[]{:S(2)}) async-start(), calls=%async_computation.4 | async-start | bytes 1179648 | tf_op jit(solution)/shard_map/reduce_scatter | solution.py:651
  35.0 92.9 %copy-start.6 = (f32[1024,8]{1,0:T(8,128)}, f32[1024,8]{1,0:T(8,128)S(1)}, u32[]{:S(2)}) copy-start(f32[1024,8]{1,0:T(8,128)S(1)} %fusion.14.kb_ref) | copy-start | bytes 98308
  272.0 233.5 %all-gather.8.cloned.1.call-start = ((), (), s32[]{:S(2)}) async-start(), calls=%async_computation.8 | async-start | bytes 2162688 | tf_op jit(solution)/shard_map/all_gather | solution.py:652
  308.7 200.0 %reduce-scatter.8.cloned.1.call-start = ((), (), s32[]{:S(2)}) async-start(), calls=%async_computation.6 | async-start | bytes 1310720 | tf_op jit(solution)/shard_map/reduce_scatter | solution.py:657
  310.4 198.2 %reduce-scatter.6.cloned.1.call-start = ((), (), s32[]{:S(2)}) async-start(), calls=%async_computation.5 | async-start | bytes 5242880 | tf_op jit(solution)/shard_map/reduce_scatter | solution.py:660
  356.8 1.2 copy-start.5
  356.8 1.5 copy-start.15
  356.8 1.7 copy-start.12
  356.8 214.2 %all-reduce.8.cloned.1.call-start = ((), (), s32[]{:S(2)}) async-start(), calls=%async_computation.9 | async-start | bytes 2621440 | tf_op jit(solution)/shard_map/psum | solution.py:660
  358.5 1.9 copy-start.16
  358.5 2.0 copy-start.20
  508.7 3.6 copy-start.26
  621.7 2.7 copy-start.3
  621.7 4.0 copy-start.2
  624.4 2.7 copy-start.7
  625.7 2.4 copy-start.23
  625.7 2.4 copy-start.24
  625.7 2.4 copy-start.25
  625.7 3.0 copy-start.17
  625.7 3.0 copy-start.18
  625.7 3.0 copy-start.19
  625.7 3.6 copy-start.10
  625.8 3.6 copy-start.11
  625.8 3.6 copy-start.13
  625.8 3.6 copy-start.14
  627.1 3.3 copy-start.8
  630.4 5.8 copy-start.1
Sparse Core Ops, SparseCore 0:
  14.7 214.3 all-reduce.5
  272.2 34.9 reduce-scatter.3
  311.1 171.4 all-gather.7
  508.8 62.1 all-reduce.7
Sparse Core Ops, SparseCore 1:
  17.3 98.3 all-gather.5
  311.6 28.1 reduce-scatter.7
  356.9 130.5 reduce-scatter.5

commit v2 on v1

v2 whole, which is shorter than its diff:
```python
import functools

import jax
import jax.numpy as jnp
from jax import lax
from jax.experimental import pallas as pl
from jax.experimental.pallas import tpu as pltpu
from jax.sharding import PartitionSpec as P

DH = 64
D = 512
NB = 128
LEN = 1024
MB = 4
STEP = 10

TB = 256
NT = LEN // TB
HEADS = D // DH
PAIRS = HEADS // 2
WIDE = 2 * DH
CH = 16
LANES = 128
ASK = 4

epsilon = 1e-06
clip_at = 1.0
beta_one = 0.9
beta_two = 0.95
adam_floor = 1e-08
highest = lax.Precision.HIGHEST
f32 = jnp.float32
bf16 = jnp.bfloat16
MESH = pl.DeviceIdType.MESH
VM = pl.BlockSpec(memory_space=pltpu.VMEM)
LIMIT = 60 * 1024 * 1024

NN = (((1,), (0,)), ((), ()))
NT_ = (((1,), (1,)), ((), ()))
TN = (((0,), (0,)), ((), ()))


def mm(a, b, dims=NN):
    return lax.dot_general(a, b, dims, preferred_element_type=f32)


def spot(index, n_model):
    return (index // n_model, lax.rem(index, n_model))


def cross(rows):
    lane = lax.broadcasted_iota(jnp.int32, (LANES, LANES), 1)
    eye = lax.broadcasted_iota(jnp.int32, (LANES, LANES), 0) == lane
    spread = jnp.broadcast_to(rows, (LANES, LANES))
    return jnp.sum(jnp.where(eye, spread, 0.0), axis=1, keepdims=True)


def remote(src, dst, send_sem, recv_sem, to):
    return pltpu.make_async_remote_copy(
        src_ref=src,
        dst_ref=dst,
        send_sem=send_sem,
        recv_sem=recv_sem,
        device_id=to,
        device_id_type=MESH,
    )


class Sizes:
    def __init__(self, n_data, n_model, heads_dev, rows_dev, negs):
        self.n_data, self.n_model, self.heads_dev, self.rows_dev = n_data, n_model, heads_dev, rows_dev
        self.n_every = n_data * n_model
        self.copies = n_model // MB
        look = LEN // n_model
        cap = max(2, 2 * look // self.n_every)
        self.group_len = look * max(1, CH // cap)
        self.groups = LEN // self.group_len
        self.slots = self.n_every * CH
        self.fw = heads_dev * DH
        self.half = n_data // 2
        self.r1 = 4 * self.fw // n_data
        self.r2 = self.fw // n_data
        self.r2p = -(-self.r2 // 16) * 16
        self.rw = self.r1 + self.r2p
        self.rn = negs // n_data
        self.ra = n_model * self.r2p + self.rn
        self.npp = n_model // PAIRS

    def order(self, d):
        return (d % 2) * self.half + d // 2

    def block(self, d):
        flat = d * self.r1
        return flat // (4 * DH), flat % (4 * DH) // DH, flat % DH


def silu_parts(values):
    sigma = 0.5 + 0.5 * jnp.tanh(0.5 * values)
    return sigma, sigma * (1.0 + values * (1.0 - sigma))


def halves(tile):
    low = lax.broadcasted_iota(jnp.int32, tile.shape, 1) < DH
    zero = jnp.zeros_like(tile)
    return jnp.concatenate([jnp.where(low, tile, zero), jnp.where(low, zero, tile)], axis=0)


def beside(tile):
    half = tile.shape[0] // 2
    return jnp.concatenate([tile[:half], tile[half:]], axis=1)


def row_sum(values):
    return jnp.sum(values, axis=0, keepdims=True)


def place_weights(z, w_ref, w1_ref, w2_ref):
    for d in range(z.n_data):
        head, part, first = z.block(d)
        for k in range(z.n_model):
            at = k * z.fw + head * DH + first
            w1_ref[part, at : at + z.r1, :] = w_ref[z.order(d), k, 0 : z.r1, :]
            if w2_ref is not None:
                at = k * z.fw + d * z.r2
                w2_ref[at : at + z.r2, :] = w_ref[z.order(d), k, z.r1 : z.r1 + z.r2, :]


def key_bias(bias_ref, bucket_ref, length):
    table = jnp.sum(bias_ref[...], axis=0)
    hot = jnp.where(
        lax.broadcasted_iota(jnp.int32, (NB, LEN), 0) == bucket_ref[...], 1.0, 0.0
    )
    rows = lax.dot_general(table, hot, NN, precision=highest, preferred_element_type=f32)
    inside = lax.broadcasted_iota(jnp.int32, (8, LEN), 1) < length
    return jnp.where(inside, 0.5 * rows, -1e30)


def front_kernel(
    z, len_ref, table_ref, f1_ref, f2_ref, bias_ref, owner_ref, local_ref, ids_ref, bucket_ref, gains_ref,
    asked_ref, slot_ref, w_ref, bias_all_ref,
    x_ref, n1o_ref, q_ref, k_ref, v_ref, do_ref, ghu_ref, gres_ref, ga_ref, stat_ref,
    low_ref, req_ref, send_ref, got_ref, t2_ref, n1_ref, n2_ref, n3_ref, acc_ref, plane_ref, neg_ref,
    xf_ref, hu_ref, o_ref, carry_ref, kb_ref, w1_ref, w2_ref, gw2_ref, gneg_ref,
    ask_send, ask_recv, row_send, row_recv,
    wz_send, wz_recv, wc_send, wc_recv, wp_send, wp_recv, bz_send, bz_recv,
    n1_send, n1_recv, n2_send, n2_recv, n3_send, n3_recv, n4_send, n4_recv, n5_send, n5_recv,
):
    n_every, n_model, half = z.n_every, z.n_model, z.half
    mine = z.groups * CH
    d = lax.axis_index("dp")
    k = lax.axis_index("mp")
    me = d * n_model + k
    side = lax.rem(d, 2)
    chip = d // 2
    here = side * half + chip
    other = d + 1 - 2 * side
    barrier = pltpu.get_barrier_semaphore()

    def signal(i, carry):
        to = spot(lax.rem(me + i, n_every), n_model)
        pl.semaphore_signal(barrier, inc=1, device_id=to, device_id_type=MESH)
        return carry

    lax.fori_loop(1, n_every, signal, 0)

    micro = k // z.copies
    owner_row = owner_ref[micro].astype(f32)
    value_row = local_ref[micro].astype(f32) + 1.0
    high_row = jnp.floor(value_row * (1.0 / 32.0))
    low_row = value_row - 32.0 * high_row
    length = z.group_len
    earlier = jnp.where(
        lax.broadcasted_iota(jnp.int32, (length, length), 0)
        < lax.broadcasted_iota(jnp.int32, (length, length), 1), 1.0, 0.0
    ).astype(bf16)
    pieces = []
    for g in range(z.groups):
        lanes = slice(g * length, (g + 1) * length)
        own = owner_row[:, lanes]
        owner_at = lax.broadcasted_iota(jnp.int32, (n_every, length), 0).astype(f32)
        hot = jnp.where(owner_at == own, 1.0, 0.0)
        rank = row_sum(mm(hot.astype(bf16), earlier) * hot)
        place = own * CH + rank
        for b in range(length // TB):
            slot_ref[g * (length // TB) + b] = place[:, b * TB : (b + 1) * TB]
        ranks = lax.broadcasted_iota(jnp.int32, (CH, length), 0).astype(f32)
        rank_hot = jnp.where(ranks == rank, 1.0, 0.0).astype(bf16)
        high = mm((hot * high_row[:, lanes]).astype(bf16), rank_hot, NT_)
        lower = mm((hot * low_row[:, lanes]).astype(bf16), rank_hot, NT_)
        pieces.append(high * 32.0 + lower - 1.0)
    pieces.append(jnp.full((n_every, LANES - mine), -1.0, f32))
    wanted = jnp.concatenate(pieces, axis=1)
    for o in range(n_every):
        req_ref[o] = wanted[o : o + 1]

    pl.semaphore_wait(barrier, n_every - 1)

    def ask_copy(src, dst, to):
        return remote(
            req_ref.at[to], asked_ref.at[dst], ask_send.at[to], ask_recv.at[src], spot(to, n_model)
        )

    def ask(i, carry):
        to = lax.rem(me + i, n_every)
        ask_copy(me, me, to).start()
        return carry

    lax.fori_loop(1, n_every, ask, 0)
    asked_ref[me] = req_ref[me]

    take = (
        lax.broadcasted_iota(jnp.int32, (z.r1, 4 * z.fw), 1)
        == lax.broadcasted_iota(jnp.int32, (z.r1, 4 * z.fw), 0) + d * z.r1
    )
    w_ref[here, k, 0 : z.r1, :] = mm(
        jnp.where(take, 1.0, 0.0).astype(bf16), f1_ref[...].astype(bf16), NT_
    ).astype(bf16)
    take = (
        lax.broadcasted_iota(jnp.int32, (z.r2p, z.fw), 1)
        == lax.broadcasted_iota(jnp.int32, (z.r2p, z.fw), 0) + d * z.r2
    )
    w_ref[here, k, z.r1 :, :] = mm(
        jnp.where(take, 1.0, 0.0).astype(bf16), f2_ref[...].astype(bf16)
    ).astype(bf16)
    bias_all_ref[k] = bias_ref[...]

    def wz_copy(i, at, to):
        return remote(
            w_ref.at[here, at], w_ref.at[here, at], wz_send.at[i], wz_recv.at[at], (d, to)
        )

    def bz_copy(i, at, to):
        return remote(bias_ref, bias_all_ref.at[at], bz_send.at[i], bz_recv.at[at], (d, to))

    for i in range(1, n_model):
        to = lax.rem(k + i, n_model)
        wz_copy(i, k, to).start()
        bz_copy(i, k, to).start()
    low_ref[...] = table_ref[...].astype(bf16)

    def row_copy(g, src, dst, to):
        return remote(
            send_ref.at[g, to], got_ref.at[g, dst], row_send.at[g, to], row_recv.at[g, src],
            spot(to, n_model),
        )

    def asked_all(i, carry):
        src = lax.rem(me + i, n_every)
        ask_copy(src, src, src).wait_recv()
        return carry

    lax.fori_loop(1, n_every, asked_all, 0)
    asked = asked_ref[...].reshape(n_every, LANES) + 1.0
    asked_high = jnp.floor(asked * (1.0 / 32.0))
    asked_low = (asked - 32.0 * asked_high).astype(bf16)
    asked_high = asked_high.astype(bf16)
    per = min(TB // CH, n_every)
    spread = jnp.where(
        lax.broadcasted_iota(jnp.int32, (per * CH, CH), 1)
        == lax.rem(lax.broadcasted_iota(jnp.int32, (per * CH, CH), 0), CH), 1.0, 0.0
    ).astype(bf16)
    turn = lax.broadcasted_iota(jnp.int32, (per * CH, n_every), 0) // CH
    asker = lax.broadcasted_iota(jnp.int32, (per * CH, n_every), 1)
    lane = lax.broadcasted_iota(jnp.int32, (per * CH, z.rows_dev), 1).astype(f32)

    def serve(g):
        lanes = slice(g * CH, (g + 1) * CH)
        for b in range(n_every // per):
            at = mm(spread, asked_high[:, lanes], NT_) * 32.0 + mm(spread, asked_low[:, lanes], NT_)
            at = jnp.where(asker == turn + b * per, at, 0.0)
            column = jnp.sum(at, axis=1, keepdims=True) - 1.0
            hot = jnp.where(lane == column, 1.0, 0.0).astype(bf16)
            found = mm(hot, low_ref[...]).astype(bf16)
            send_ref[g, b * per : (b + 1) * per] = found.reshape(per, CH, D)
        got_ref[g, me] = send_ref[g, me]

    def send_group(g):
        def send(i, carry):
            row_copy(g, me, me, lax.rem(me + i, n_every)).start()
            return carry

        lax.fori_loop(1, n_every, send, 0)

    def release(g):
        def follow(i, carry):
            at = lax.rem(me + i, n_every)
            row_copy(g - 1, at, at, at).wait_send()
            row_copy(g, me, me, at).start()
            return carry

        lax.fori_loop(1, n_every, follow, 0)

    serve(0)
    send_group(0)

    per_side = half * MB * z.rn
    span = MB * z.rn
    n_lane = lax.broadcasted_iota(jnp.int32, (TB, z.rows_dev), 1).astype(f32)

    def negatives(i, carry, first):
        at = first * (per_side // TB) + i
        columns = [cross(ids_ref[at * (TB // LANES) + j]) for j in range(TB // LANES)]
        column = jnp.concatenate(columns, axis=0) - (me * z.rows_dev).astype(f32)
        hot = jnp.where(n_lane == column, 1.0, 0.0).astype(bf16)
        t2_ref[first, pl.ds(pl.multiple_of(i * TB, TB), TB), :] = mm(hot, low_ref[...]).astype(bf16)
        return carry

    def wc_copy(i, at, to):
        return remote(
            w_ref.at[at], w_ref.at[at], wc_send.at[i], wc_recv.at[at], (2 * to + side, k)
        )

    def wp_copy(at):
        return remote(w_ref.at[at], w_ref.at[at], wp_send.at[at], wp_recv.at[at], (other, k))

    n1_copy = remote(t2_ref.at[1 - side], n1_ref, n1_send, n1_recv, (other, k))

    def n2_copy(i, at, to):
        return remote(
            acc_ref.at[pl.ds(pl.multiple_of(to * span, 16), span)], n2_ref.at[at],
            n2_send.at[i], n2_recv.at[at], (2 * to + side, k),
        )

    def n3_copy(i, at, to):
        return remote(
            plane_ref.at[to // z.copies], n3_ref.at[at], n3_send.at[i], n3_recv.at[at], (d, to)
        )

    def n4_copy(i, at, to):
        return remote(
            neg_ref.at[at], neg_ref.at[at], n4_send.at[i], n4_recv.at[at], (2 * to + side, k)
        )

    def n5_copy(at):
        return remote(neg_ref.at[at], neg_ref.at[at], n5_send.at[at], n5_recv.at[at], (other, k))

    for i in range(1, n_model):
        wz_copy(i, lax.rem(k + i, n_model), k).wait_recv()
    for i in range(1, half):
        wc_copy(i, here, lax.rem(chip + i, half)).start()
    wp_copy(here).start()
    lax.fori_loop(0, per_side // TB, functools.partial(negatives, first=1 - side), 0)
    n1_copy.start()
    lax.fori_loop(0, per_side // TB, functools.partial(negatives, first=side), 0)
    if z.groups > 1:
        serve(1)
    n1_copy.wait_recv()
    acc_ref[...] = t2_ref[side] + n1_ref[...]
    for i in range(1, half):
        n2_copy(i, chip, lax.rem(chip + i, half)).start()
    for g in range(2, z.groups):
        serve(g)

    length = len_ref[0]
    lead = len_ref[1]
    gain_in = gains_ref[0:1, :]
    gain_attn = gains_ref[1:2, :]
    gain_out = gains_ref[2:3, :]
    for i in range(1, n_model):
        at = lax.rem(k + i, n_model)
        bz_copy(i, at, k).wait_recv()
    kb = key_bias(bias_all_ref, bucket_ref, length)
    for j in range(NT):
        kb_ref[j] = kb[:, j * TB : (j + 1) * TB]
    xf_ref[LEN:, :] = jnp.zeros((8, D), f32)
    carry_ref[...] = jnp.zeros_like(carry_ref)
    stat_ref[...] = jnp.zeros_like(stat_ref)
    gw2_ref[...] = jnp.zeros_like(gw2_ref)
    gneg_ref[...] = jnp.zeros_like(gneg_ref)
    if z.groups > 1:
        release(1)
    for i in range(1, half):
        from_chip = lax.rem(chip + i, half)
        wc_copy(i, side * half + from_chip, chip).wait_recv()
        wp_copy(side * half + from_chip).start()
    for g in range(2, min(3, z.groups)):
        release(g)
    for i in range(half):
        wp_copy((1 - side) * half + i).wait_recv()
    place_weights(z, w_ref, w1_ref, w2_ref)

    def neg_one():
        total = acc_ref[pl.ds(pl.multiple_of(chip * span, 16), span), :]
        for i in range(1, half):
            from_chip = lax.rem(chip + i, half)
            n2_copy(i, from_chip, chip).wait_recv()
            total = total + n2_ref[from_chip]
        plane_ref[...] = total.reshape(MB, z.rn, D)
        for i in range(1, n_model):
            n3_copy(i, k, lax.rem(k + i, n_model)).start()

    def neg_two():
        total = plane_ref[micro]
        for i in range(1, n_model):
            at = lax.rem(k + i, n_model)
            n3_copy(i, at, k).wait_recv()
            total = total + n3_ref[at]
        neg_ref[here] = total
        for i in range(1, half):
            n4_copy(i, here, lax.rem(chip + i, half)).start()
        n5_copy(here).start()

    def neg_three():
        for i in range(1, half):
            at = side * half + lax.rem(chip + i, half)
            n4_copy(i, at, chip).wait_recv()
            n5_copy(at).start()

    def neg_four():
        for i in range(half):
            n5_copy((1 - side) * half + i).wait_recv()

    slots = z.slots

    def arrive(g):
        def wait(i, carry):
            at = lax.rem(me + i, n_every)
            row_copy(g, at, at, at).wait_recv()
            return carry

        lax.fori_loop(1, n_every, wait, 0)

    def inputs(i):
        rows = pl.ds(pl.multiple_of(i * TB, TB), TB)
        hot = lax.broadcasted_iota(jnp.int32, (slots, TB), 0).astype(f32) == slot_ref[i]
        found = got_ref[i * TB // z.group_len]
        x = mm(jnp.where(hot, 1.0, 0.0).astype(bf16), found.reshape(slots, D), TN)
        x_ref[rows, :] = x.astype(bf16)
        xf_ref[rows, :] = x
        factor = lax.rsqrt(jnp.mean(x * x, -1, keepdims=True) + epsilon)
        n1 = (x * factor * gain_in).astype(bf16)
        n1o_ref[rows, :] = n1
        hu_ref[rows, :] = mm(n1, w1_ref[0], NT_)
        for c, ref in ((1, v_ref), (2, q_ref), (3, k_ref)):
            hidden = mm(n1, w1_ref[c], NT_)
            act = (hidden * silu_parts(hidden)[0]).astype(bf16)
            if c == 2:
                act = act * jnp.asarray(0.5 * DH ** (-0.5), bf16)
            for p in range(PAIRS):
                ref[p, rows, :] = act[:, p * WIDE : (p + 1) * WIDE]

    scale = 2.0 * D ** (-0.5)
    in_row = lax.broadcasted_iota(jnp.int32, (2 * TB, TB), 0)
    in_col = lax.broadcasted_iota(jnp.int32, (2 * TB, TB), 1)
    causal = in_col <= lax.rem(in_row, TB)
    first_half = in_row < TB

    def attend(i):
        rows = pl.ds(pl.multiple_of(i * TB, TB), TB)
        place = lax.broadcasted_iota(jnp.int32, (TB, 1), 0) + i * TB
        inv = 1.0 / (place.astype(f32) + 1.0)
        inv2 = jnp.concatenate([inv, inv], axis=0)
        for p in range(PAIRS):
            q2 = halves(q_ref[p, rows, :])

            def part(j, total, masked, p=p, q2=q2):
                keys = pl.ds(pl.multiple_of(j * TB, TB), TB)
                kb = kb_ref[j]
                kb = jnp.where(first_half, kb[2 * p : 2 * p + 1, :], kb[2 * p + 1 : 2 * p + 2, :])
                h = mm(q2, k_ref[p, keys, :], NT_) + kb
                w = (h + h * jnp.tanh(h)) * inv2
                if masked:
                    w = jnp.where(causal, w, 0.0)
                return total + mm(beside(w.astype(bf16)), halves(v_ref[p, keys, :]))

            total = lax.fori_loop(
                0, i, functools.partial(part, masked=False), jnp.zeros((TB, WIDE), f32)
            )
            o_ref[p, rows, :] = part(i, total, True)

    def lose(i):
        rows = pl.ds(pl.multiple_of(i * TB, TB), TB)
        place = lax.broadcasted_iota(jnp.int32, (TB, 1), 0) + i * TB
        o = jnp.concatenate([o_ref[p, rows, :] for p in range(PAIRS)], axis=1)
        factor_attn = lax.rsqrt(jnp.mean(o * o, -1, keepdims=True) + epsilon)
        na = o * factor_attn * gain_attn
        hu = hu_ref[rows, :]
        sigma, slope = silu_parts(hu)
        upper = hu * sigma
        gated = (na * upper).astype(bf16)
        y = xf_ref[rows, :] + mm(gated, w2_ref[...])
        factor_out = lax.rsqrt(jnp.mean(y * y, -1, keepdims=True) + epsilon)
        out = (y * factor_out * gain_out).astype(bf16)
        zf = out.astype(f32)
        after = xf_ref[pl.ds(pl.multiple_of(i * TB + TB, 8), 8), :]
        last = lax.broadcasted_iota(jnp.int32, (TB, 1), 0) == TB - 1
        target = jnp.where(last, after[0:1, :], pltpu.roll(xf_ref[rows, :], TB - 1, 0))
        neg_logits = mm(out, neg_ref[...].reshape(half * 2 * z.rn, D), NT_) * scale
        pos = jnp.sum(zf * target, -1, keepdims=True) * scale
        top = jnp.maximum(jnp.max(neg_logits, -1, keepdims=True), pos)
        neg_exp = jnp.exp(neg_logits - top)
        pos_exp = jnp.exp(pos - top)
        total = pos_exp + jnp.sum(neg_exp, -1, keepdims=True)
        live = jnp.where(place + 1 < length, 1.0, 0.0) * lead.astype(f32)
        per = (top + jnp.log(total) - pos) * live
        gneg = (neg_exp / total * live).astype(bf16)
        gpos = (pos_exp / total - 1.0) * live
        gz = mm(gneg, neg_ref[...].reshape(half * 2 * z.rn, D)) * scale + gpos * target * scale
        gneg_ref[...] += mm(gneg, out, TN) * scale
        target_grad = gpos * zf * scale
        first = lax.broadcasted_iota(jnp.int32, (TB, 1), 0) == 0
        shifted = jnp.where(first, carry_ref[0:1, :], pltpu.roll(target_grad, 1, 0))
        carry_ref[0:1, :] = target_grad[TB - 1 : TB, :]
        scaled = gz * gain_out
        gy = factor_out * (
            scaled - y * factor_out * factor_out * jnp.mean(y * scaled, -1, keepdims=True)
        )
        gres_ref[rows, :] = gy + shifted
        low = gy.astype(bf16)
        gg = mm(low, w2_ref[...], NT_)
        gw2_ref[...] += mm(gated, low, TN)
        gnorm = gg * upper
        gup = gg * na
        og = gain_attn * gnorm
        inner = jnp.sum(o * og, -1, keepdims=True)
        go = factor_attn * (og - o * factor_attn * factor_attn * (inner / D))
        go = go.astype(bf16)
        for p in range(PAIRS):
            do_ref[p, rows, :] = go[:, p * WIDE : (p + 1) * WIDE]
        ghu_ref[rows, :] = (gup * slope).astype(bf16)
        stat_ref[1:2, :] += row_sum(gnorm * o * factor_attn)
        stat_ref[2:3, :] += row_sum(gz * y * factor_out)
        stat_ref[3:4, :] += jnp.broadcast_to(row_sum(per), (1, D))
        stat_ref[4:5, :] += jnp.broadcast_to(row_sum(live), (1, D))


    per_group = z.group_len // TB
    arrive(0)

    def last(i, carry):
        lose(i)
        return carry

    def after_one():
        neg_one()
        for g in range(3, z.groups):
            release(g)

    def after_two():
        neg_two()
        neg_three()
        neg_four()
        lax.fori_loop(0, NT - 2, last, 0)

    def step(i, carry):
        if per_group == 1:
            pl.when(i > 0)(lambda: arrive(i))
        inputs(i)
        attend(i)
        pl.when(i == 1)(after_one)
        pl.when(i == NT - 2)(after_two)
        return carry

    lax.fori_loop(0, NT, step, 0)
    lax.fori_loop(NT - 2, NT, last, 0)
    for dd in range(z.n_data):
        at = z.order(dd)
        for kk in range(z.n_model):
            piece = gw2_ref[kk * z.fw + dd * z.r2 : kk * z.fw + (dd + 1) * z.r2, :]
            if z.r2p > z.r2:
                piece = jnp.concatenate([piece, jnp.zeros((z.r2p - z.r2, D), f32)], axis=0)
            ga_ref[at, kk * z.r2p : (kk + 1) * z.r2p, :] = piece
        ga_ref[at, z.n_model * z.r2p :, :] = gneg_ref[at * z.rn : (at + 1) * z.rn, :]

    for i in range(half):
        wp_copy(side * half + i).wait_send()
        n5_copy(side * half + i).wait_send()
    for i in range(1, half):
        to = lax.rem(chip + i, half)
        wc_copy(i, here, to).wait_send()
        n2_copy(i, chip, to).wait_send()
        n4_copy(i, here, to).wait_send()
    for i in range(1, n_model):
        at = lax.rem(k + i, n_model)
        wz_copy(i, k, at).wait_send()
        n3_copy(i, k, at).wait_send()
        bz_copy(i, k, at).wait_send()
    n1_copy.wait_send()

    def finish(i, carry):
        at = lax.rem(me + i, n_every)
        ask_copy(at, at, at).wait_send()
        row_copy(z.groups - 1, at, at, at).wait_send()
        return carry

    lax.fori_loop(1, n_every, finish, 0)


def front(z, scalars, table, w_f1, w_f2, bias_tile, owner, local, ids, bucket, gains):
    sds = jax.ShapeDtypeStruct
    dma = pltpu.SemaphoreType.DMA
    vm = pltpu.VMEM
    per_side = z.half * MB * z.rn
    every, model, half, data = (z.n_every,), (z.n_model,), (z.half,), (z.n_data,)
    groups_every = (z.groups, z.n_every)
    pairs_shape = sds((PAIRS, LEN, WIDE), bf16)
    return pl.pallas_call(
        functools.partial(front_kernel, z),
        out_shape=(
            sds((z.n_every, 1, LANES), f32),
            sds((NT, 1, TB), f32),
            sds((z.n_data, z.n_model, z.rw, D), bf16),
            sds((z.n_model, 8, LANES), f32),
            sds((LEN, D), bf16), sds((LEN, D), bf16),
            pairs_shape, pairs_shape, pairs_shape, pairs_shape,
            sds((LEN, D), bf16), sds((LEN, D), f32),
            sds((z.n_data, z.ra, D), f32), sds((8, D), f32),
        ),
        in_specs=[pl.BlockSpec(memory_space=pltpu.SMEM)] + [VM] * 9,
        out_specs=(VM,) * 14,
        scratch_shapes=[
            vm(table.shape, bf16),
            vm((z.n_every, 1, LANES), f32),
            vm((z.groups, z.n_every, CH, D), bf16),
            vm((z.groups, z.n_every, CH, D), bf16),
            vm((2, per_side, D), bf16),
            vm((per_side, D), bf16),
            vm((z.half, MB * z.rn, D), bf16),
            vm((z.n_model, z.rn, D), bf16),
            vm((per_side, D), bf16),
            vm((MB, z.rn, D), bf16),
            vm((z.n_data, z.rn, D), bf16),
            vm((LEN + 8, D), f32),
            vm((LEN, D), f32),
            vm((PAIRS, LEN, WIDE), f32),
            vm((8, D), f32),
            vm((NT, 8, TB), f32),
            vm((4, D, D), bf16),
            vm((D, D), bf16),
            vm((D, D), f32),
            vm((z.n_data * z.rn, D), f32),
            dma(every), dma(every), dma(groups_every), dma(groups_every),
            dma(model), dma(model), dma(half), dma(data), dma(data), dma(data), dma(model), dma(model),
            dma, dma, dma(half), dma(half), dma(model), dma(model), dma(half), dma(data), dma(data), dma(data),
        ],
        compiler_params=pltpu.CompilerParams(
            collective_id=0, has_side_effects=True, vmem_limit_bytes=LIMIT
        ),
        cost_estimate=pl.CostEstimate(
            flops=60_000_000_000, bytes_accessed=30_000_000, transcendentals=6_000_000
        ),
        name="front",
    )(scalars, table, w_f1, w_f2, bias_tile, owner, local, ids, bucket, gains)


def rear_kernel(
    z, len_ref, x_ref, n1_ref, q_ref, k_ref, v_ref, do_ref, ghu_ref, gres_ref, w_ref, bias_ref, bucket_ref,
    gains_ref, slot_ref, stat_in_ref, ga_ref, asked_ref, ids_ref,
    tg_ref, wg_ref, packs_ref, squares_ref,
    gh_ref, hid_ref, kb_ref, dq_ref, dk_ref, dv_ref, bs_ref, w1_ref, stat_ref, pack_ref, out_ref, gb_ref,
    got_ref, pa_ref, pb_ref, sa_ref, sb_ref, ca_ref, cb_ref, zs_ref, zr_ref, ng_ref, sq_ref,
    row_send, row_recv, pack_send, pack_recv,
    pa_send, pa_recv, pb_send, pb_recv, ca_send, ca_recv, cb_send, cb_recv,
    zw_send, zw_recv, zn_send, zn_recv, gw_send, gw_recv, gn_send, gn_recv,
    hw_send, hw_recv, hn_send, hn_recv, sq_send, sq_recv,
):
    n_every, n_model, half = z.n_every, z.n_model, z.half
    slots = z.slots
    d = lax.axis_index("dp")
    k = lax.axis_index("mp")
    me = d * n_model + k
    side = lax.rem(d, 2)
    chip = d // 2
    here = side * half + chip
    other = d + 1 - 2 * side
    barrier = pltpu.get_barrier_semaphore()

    def signal(i, carry):
        to = spot(lax.rem(me + i, n_every), n_model)
        pl.semaphore_signal(barrier, inc=1, device_id=to, device_id_type=MESH)
        return carry

    lax.fori_loop(1, n_every, signal, 0)

    pa_copy = remote(ga_ref.at[1 - side], pa_ref, pa_send, pa_recv, (other, k))

    def pb_copy(p):
        return remote(gb_ref.at[1 - side, p], pb_ref.at[p], pb_send.at[p], pb_recv.at[p], (other, k))

    def row_copy(g, src, dst, to):
        return remote(
            out_ref.at[g, to], got_ref.at[g, dst], row_send.at[g, to], row_recv.at[g, src],
            spot(to, n_model),
        )

    def pack_copy(src, dst, to):
        return remote(
            pack_ref, packs_ref.at[dst], pack_send.at[to], pack_recv.at[src], spot(to, n_model)
        )

    def ca_copy(i, at, to):
        return remote(
            sa_ref.at[to], ca_ref.at[at], ca_send.at[i], ca_recv.at[at], (2 * to + side, k)
        )

    def cb_copy(p, i, at, to):
        return remote(
            sb_ref.at[p, to], cb_ref.at[p, at], cb_send.at[p, i], cb_recv.at[p, at], (2 * to + side, k)
        )

    def zn_copy(i, at, to):
        return remote(
            ng_ref.at[here, at], ng_ref.at[here, at], zn_send.at[i], zn_recv.at[at], (d, to)
        )

    def zw_copy(at, to):
        return remote(zs_ref.at[to], zr_ref.at[at], zw_send.at[to], zw_recv.at[at], (d, to))

    def gw_copy(i, at, to):
        return remote(
            wg_ref.at[at], wg_ref.at[at], gw_send.at[i], gw_recv.at[at], (2 * to + side, k)
        )

    def gn_copy(i, at, to):
        return remote(
            ng_ref.at[at], ng_ref.at[at], gn_send.at[i], gn_recv.at[at], (2 * to + side, k)
        )

    def hw_copy(at):
        return remote(wg_ref.at[at], wg_ref.at[at], hw_send.at[at], hw_recv.at[at], (other, k))

    def hn_copy(at):
        return remote(ng_ref.at[at], ng_ref.at[at], hn_send.at[at], hn_recv.at[at], (other, k))

    def sq_copy(src, dst, to):
        return remote(
            sq_ref, squares_ref.at[dst], sq_send.at[to], sq_recv.at[src], spot(to, n_model)
        )

    def chips_a():
        pa_copy.wait_recv()
        sa_ref[...] = (ga_ref[side] + pa_ref[...]).astype(bf16)
        for i in range(1, half):
            ca_copy(i, chip, lax.rem(chip + i, half)).start()

    def chips_b(p):
        pb_copy(p).wait_recv()
        sb_ref[p] = (gb_ref[side, p] + pb_ref[p]).astype(bf16)
        for i in range(1, half):
            cb_copy(p, i, chip, lax.rem(chip + i, half)).start()

    def planes_a():
        total = sa_ref[chip].astype(f32)
        for i in range(1, half):
            at = lax.rem(chip + i, half)
            ca_copy(i, at, chip).wait_recv()
            total = total + ca_ref[at].astype(f32)
        ng_ref[here, k] = total[n_model * z.r2p :].astype(bf16)
        zs_ref[:, z.r1 :, :] = total[: n_model * z.r2p].reshape(n_model, z.r2p, D)
        for i in range(1, n_model):
            zn_copy(i, k, lax.rem(k + i, n_model)).start()

    def planes_b(p):
        total = sb_ref[p, chip].astype(f32)
        for i in range(1, half):
            at = lax.rem(chip + i, half)
            cb_copy(p, i, at, chip).wait_recv()
            total = total + cb_ref[p, at].astype(f32)
        for i in range(z.npp):
            to = p * z.npp + i
            zs_ref[to, : z.r1, :] = total[i * z.r1 : (i + 1) * z.r1]
            pl.when(k != to)(lambda to=to: zw_copy(k, to).start())

    def spread_a():
        for i in range(1, n_model):
            zn_copy(i, lax.rem(k + i, n_model), k).wait_recv()
        for i in range(1, half):
            gn_copy(i, here, lax.rem(chip + i, half)).start()
        hn_copy(here).start()

    def swap_a():
        for i in range(1, half):
            at = side * half + lax.rem(chip + i, half)
            gn_copy(i, at, chip).wait_recv()
            hn_copy(at).start()

    gain_in = gains_ref[0:1, :]
    place_weights(z, w_ref, w1_ref, None)
    kb_ref[...] = key_bias(bias_ref, bucket_ref, len_ref[0]).T

    def inputs(i, carry):
        rows = pl.ds(pl.multiple_of(i * TB, TB), TB)
        for c in (1, 2, 3):
            hid_ref[c - 1, rows, :] = mm(n1_ref[rows, :], w1_ref[c], NT_)
        return carry

    lax.fori_loop(0, NT, inputs, 0)
    bs_ref[...] = jnp.zeros_like(bs_ref)
    in_row = lax.broadcasted_iota(jnp.int32, (2 * TB, TB), 0)
    in_col = lax.broadcasted_iota(jnp.int32, (2 * TB, TB), 1)
    causal = lax.rem(in_row, TB) <= in_col
    ones_lane = lax.broadcasted_iota(jnp.int32, (2 * TB, LANES), 1)
    ones_half = lax.broadcasted_iota(jnp.int32, (2 * TB, LANES), 0) >= TB
    stat_ref[...] = jnp.zeros_like(stat_ref)
    per_group = z.group_len // TB

    def outputs(i):
        rows = pl.ds(pl.multiple_of(i * TB, TB), TB)
        gn = mm(ghu_ref[rows, :], w1_ref[0])
        for c in (1, 2, 3):
            gn += mm(gh_ref[c - 1, rows, :], w1_ref[c])
        x = x_ref[rows, :].astype(f32)
        factor = lax.rsqrt(jnp.mean(x * x, -1, keepdims=True) + epsilon)
        scaled = gn * gain_in
        gx = factor * (scaled - x * factor * factor * jnp.mean(x * scaled, -1, keepdims=True))
        gx = (gx + gres_ref[rows, :]).astype(bf16)
        stat_ref[0:1, :] += row_sum(gn * x * factor)
        group = i // per_group
        hot = lax.broadcasted_iota(jnp.int32, (slots, TB), 0).astype(f32) == slot_ref[i]
        mine = mm(jnp.where(hot, 1.0, 0.0).astype(bf16), gx).astype(bf16)
        mine = mine.reshape(z.n_every, CH, D)
        if per_group == 1:
            out_ref[group] = mine
        else:
            out_ref[group] = jnp.where(lax.rem(i, per_group) == 0, mine, out_ref[group] + mine)

    def send_group(g):
        def send(i, carry):
            row_copy(g, me, me, lax.rem(me + i, n_every)).start()
            return carry

        lax.fori_loop(1, n_every, send, 0)
        got_ref[g, me] = out_ref[g, me]

    def weights_grad(p):
        lanes = slice(p * WIDE, (p + 1) * WIDE)
        for c in range(4):
            left = ghu_ref[:, lanes] if c == 0 else gh_ref[c - 1, :, lanes]
            grads = mm(left, n1_ref[...], TN)
            for side_head in range(2):
                head = 2 * p + side_head
                for dd in range(z.n_data):
                    own_head, part, first = z.block(dd)
                    if part == c and own_head == head % z.heads_dev:
                        at = head // z.heads_dev - p * z.npp
                        gb_ref[dd % 2, p, dd // 2, at * z.r1 : (at + 1) * z.r1, :] = grads[
                            side_head * DH + first : side_head * DH + first + z.r1
                        ]
        pb_copy(p).start()

    pl.semaphore_wait(barrier, n_every - 1)
    pa_copy.start()

    for p in range(PAIRS):
        lanes = slice(p * WIDE, (p + 1) * WIDE)
        dq_ref[...] = jnp.zeros_like(dq_ref)
        mark = jnp.where(
            ones_lane == jnp.where(ones_half, 2 * p + 1, 2 * p), 1.0, 0.0
        ).astype(bf16)

        def keys_step(j, carry, p=p, lanes=lanes, mark=mark):
            keys = pl.ds(pl.multiple_of(j * TB, TB), TB)
            k2 = halves(k_ref[p, keys, :])
            v2 = halves(v_ref[p, keys, :])
            kt = k_ref[p, keys, :].astype(f32).T
            low = lax.broadcasted_iota(jnp.int32, kt.shape, 0) < DH
            kt2 = jnp.concatenate(
                [jnp.where(low, kt, 0.0), jnp.where(low, 0.0, kt)], axis=1
            ).astype(bf16)
            kb = jnp.concatenate(
                [kb_ref[keys, 2 * p : 2 * p + 1], kb_ref[keys, 2 * p + 1 : 2 * p + 2]], axis=0
            )
            dk_ref[...] = jnp.zeros_like(dk_ref)
            dv_ref[...] = jnp.zeros_like(dv_ref)

            def part(i, masked):
                rows = pl.ds(pl.multiple_of(i * TB, TB), TB)
                q = q_ref[p, rows, :]
                do = do_ref[p, rows, :]
                place = lax.broadcasted_iota(jnp.int32, (1, TB), 1) + i * TB
                inv = 1.0 / (place.astype(f32) + 1.0)
                h = mm(k2, q, NT_) + kb
                t = jnp.tanh(h)
                m = h * t
                w = (h + m) * inv
                ds = mm(v2, do, NT_) * ((1.0 + t) * (0.5 * inv)) * (1.0 + h - m)
                if masked:
                    w = jnp.where(causal, w, 0.0)
                    ds = jnp.where(causal, ds, 0.0)
                ds = ds.astype(bf16)
                dv_ref[...] += mm(beside(w.astype(bf16)), halves(do))
                dk_ref[...] += mm(beside(ds), jnp.concatenate([halves(q), mark], axis=1))
                dq_ref[i] += mm(kt2, ds)

            part(j, True)

            def later(i, inner):
                part(i, False)
                return inner

            lax.fori_loop(j + 1, NT, later, 0)
            slope_v = silu_parts(hid_ref[0, keys, lanes])[1]
            slope_k = silu_parts(hid_ref[2, keys, lanes])[1]
            gh_ref[0, keys, lanes] = (dv_ref[...] * slope_v).astype(bf16)
            gh_ref[2, keys, lanes] = (dk_ref[:, :WIDE] * 2.0 * slope_k).astype(bf16)
            bs_ref[keys, :] += dk_ref[:, WIDE:]
            slope_q = silu_parts(hid_ref[1, keys, lanes])[1]
            gh_ref[1, keys, lanes] = (dq_ref[j].T * DH ** (-0.5) * slope_q).astype(bf16)
            if p == PAIRS - 1:
                outputs(j)
                if per_group == 1:
                    send_group(j)
                pl.when(j == 0)(functools.partial(chips_b, PAIRS - 2))
                pl.when(j == 1)(functools.partial(planes_b, PAIRS - 3))
                pl.when(j == 2)(spread_a)
            return carry

        lax.fori_loop(0, NT, keys_step, 0)
        weights_grad(p)
        if p == 0:
            chips_a()
        elif p < PAIRS - 1:
            chips_b(p - 1)
            if p == 1:
                planes_a()
            else:
                planes_b(p - 2)

    if per_group > 1:
        for g in range(z.groups):
            send_group(g)
    hot = jnp.where(
        lax.broadcasted_iota(jnp.int32, (NB, LEN), 0) == bucket_ref[...], 1.0, 0.0
    )
    bias_grad = lax.dot_general(hot, bs_ref[...], NN, precision=highest, preferred_element_type=f32)
    for i in range(D // LANES):
        lanes = slice(i * LANES, (i + 1) * LANES)
        pack_ref[i : i + 1] = stat_ref[0:1, lanes]
        pack_ref[4 + i : 5 + i] = stat_in_ref[1:2, lanes]
        pack_ref[8 + i : 9 + i] = stat_in_ref[2:3, lanes]
    pack_ref[12:14] = stat_in_ref[3:5, :LANES]
    pack_ref[14:16] = jnp.zeros((2, LANES), f32)
    pack_ref[16:24] = bias_grad.T[0:8, :]
    packs_ref[me] = pack_ref[...]

    def pack_all(i, carry):
        pack_copy(me, me, lax.rem(me + i, n_every)).start()
        return carry

    lax.fori_loop(1, n_every, pack_all, 0)

    tg_ref[...] = jnp.zeros_like(tg_ref)
    wide = min(TB, slots)
    ask_at = lax.broadcasted_iota(jnp.int32, (z.rows_dev, wide), 0).astype(f32)

    def collect(g):
        def wait(i, carry):
            at = lax.rem(me + i, n_every)
            row_copy(g, at, at, at).wait_recv()
            return carry

        lax.fori_loop(1, n_every, wait, 0)
        for b in range(slots // wide):
            asked = asked_ref[g][:, b * wide : (b + 1) * wide]
            hot = jnp.where(ask_at == asked, 1.0, 0.0).astype(bf16)
            rows = got_ref[g, b * (wide // CH) : (b + 1) * (wide // CH)].reshape(wide, D)
            tg_ref[...] += mm(hot, rows)

    neg_rows = n_model * z.rn
    row_at = lax.broadcasted_iota(jnp.int32, (z.rows_dev, neg_rows), 0).astype(f32)
    base = (me * z.rows_dev).astype(f32)

    def negatives(at):
        hot = jnp.where(row_at == ids_ref[at] - base, 1.0, 0.0).astype(bf16)
        tg_ref[...] += mm(hot, ng_ref[at].reshape(neg_rows, D))

    planes_b(PAIRS - 2)
    swap_a()
    chips_b(PAIRS - 1)
    collect(0)
    for i in range(half):
        negatives(side * half + i)
    planes_b(PAIRS - 1)
    for g in range(1, max(1, z.groups - 1)):
        collect(g)
    total = zs_ref[k]
    for i in range(1, n_model):
        at = lax.rem(k + i, n_model)
        zw_copy(at, k).wait_recv()
        total = total + zr_ref[at]
    wg_ref[here] = total
    for i in range(1, half):
        gw_copy(i, here, lax.rem(chip + i, half)).start()
    hw_copy(here).start()
    for i in range(half):
        hn_copy((1 - side) * half + i).wait_recv()
        negatives((1 - side) * half + i)
    if z.groups > 1:
        collect(z.groups - 1)

    table_grad = tg_ref[...]
    slice_grad = wg_ref[here]
    squares = row_sum(table_grad * table_grad) + row_sum(slice_grad * slice_grad)
    sq_ref[...] = sum(squares[:, i * LANES : (i + 1) * LANES] for i in range(D // LANES))
    squares_ref[me] = sq_ref[...]

    def share(i, carry):
        to = lax.rem(me + i, n_every)
        sq_copy(me, me, to).start()
        return carry

    lax.fori_loop(1, n_every, share, 0)
    for i in range(1, half):
        at = side * half + lax.rem(chip + i, half)
        gw_copy(i, at, chip).wait_recv()
        hw_copy(at).start()
    for i in range(half):
        hw_copy((1 - side) * half + i).wait_recv()
        hw_copy(side * half + i).wait_send()
        hn_copy(side * half + i).wait_send()
    for i in range(1, half):
        to = lax.rem(chip + i, half)
        ca_copy(i, chip, to).wait_send()
        for p in range(PAIRS):
            cb_copy(p, i, chip, to).wait_send()
        gn_copy(i, here, to).wait_send()
        gw_copy(i, here, to).wait_send()
    for i in range(1, n_model):
        to = lax.rem(k + i, n_model)
        zn_copy(i, k, to).wait_send()
        zw_copy(k, to).wait_send()
    pa_copy.wait_send()
    for p in range(PAIRS):
        pb_copy(p).wait_send()

    def finish(i, carry):
        at = lax.rem(me + i, n_every)
        for g in range(z.groups):
            row_copy(g, at, at, at).wait_send()
        pack_copy(at, at, at).wait_send()
        pack_copy(at, at, at).wait_recv()
        sq_copy(at, at, at).wait_send()
        sq_copy(at, at, at).wait_recv()
        return carry

    lax.fori_loop(1, n_every, finish, 0)


def rear(
    z, scalars, x, n1, q, k, v, do, ghu, gres, w, bias, bucket, gains, slot, stat, ga, asked, ids
):
    sds = jax.ShapeDtypeStruct
    dma = pltpu.SemaphoreType.DMA
    vm = pltpu.VMEM
    every, model, half, data = (z.n_every,), (z.n_model,), (z.half,), (z.n_data,)
    groups_every = (z.groups, z.n_every)
    pairs, pairs_half = (PAIRS,), (PAIRS, z.half)
    rows_b = z.npp * z.r1
    return pl.pallas_call(
        functools.partial(rear_kernel, z),
        out_shape=(
            sds((z.rows_dev, D), f32),
            sds((z.n_data, z.rw, D), f32),
            sds((z.n_every, 24, LANES), f32),
            sds((z.n_every, 1, LANES), f32),
        ),
        in_specs=[pl.BlockSpec(memory_space=pltpu.SMEM)] + [VM] * 17,
        out_specs=(VM,) * 4,
        scratch_shapes=[
            vm((3, LEN, D), bf16),
            vm((3, LEN, D), f32),
            vm((LEN, 8), f32),
            vm((NT, WIDE, TB), f32),
            vm((TB, WIDE + LANES), f32),
            vm((TB, WIDE), f32),
            vm((LEN, LANES), f32),
            vm((4, D, D), bf16),
            vm((8, D), f32),
            vm((24, LANES), f32),
            vm((z.groups, z.n_every, CH, D), bf16),
            vm((2, PAIRS, z.half, rows_b, D), f32),
            vm((z.groups, z.n_every, CH, D), bf16),
            vm((z.half, z.ra, D), f32),
            vm((PAIRS, z.half, rows_b, D), f32),
            vm((z.half, z.ra, D), bf16),
            vm((PAIRS, z.half, rows_b, D), bf16),
            vm((z.half, z.ra, D), bf16),
            vm((PAIRS, z.half, rows_b, D), bf16),
            vm((z.n_model, z.rw, D), f32),
            vm((z.n_model, z.rw, D), f32),
            vm((z.n_data, z.n_model, z.rn, D), bf16),
            vm((1, LANES), f32),
            dma(groups_every), dma(groups_every), dma(every), dma(every),
            dma, dma, dma(pairs), dma(pairs), dma(half), dma(half), dma(pairs_half), dma(pairs_half),
            dma(model), dma(model), dma(model), dma(model), dma(half), dma(data), dma(half), dma(data),
            dma(data), dma(data), dma(data), dma(data), dma(every), dma(every),
        ],
        compiler_params=pltpu.CompilerParams(
            collective_id=1, has_side_effects=True, vmem_limit_bytes=LIMIT
        ),
        cost_estimate=pl.CostEstimate(
            flops=60_000_000_000, bytes_accessed=30_000_000, transcendentals=6_000_000
        ),
        name="rear",
    )(scalars, x, n1, q, k, v, do, ghu, gres, w, bias, bucket, gains, slot, stat, ga, asked, ids)


def adam_step(weight, grad, first, second, rate, decay):
    first_new = beta_one * first + (1.0 - beta_one) * grad
    second_new = beta_two * second + (1.0 - beta_two) * grad * grad
    fix_one = 1.0 - beta_one**STEP
    fix_two = 1.0 - beta_two**STEP
    move = first_new / fix_one / (jnp.sqrt(second_new / fix_two) + adam_floor) + decay * weight
    return (weight - rate * move, first_new, second_new)


def settle_kernel(
    z, squares_ref, packs_ref, wg_ref, tg_ref, t_ref, tm_ref, tv_ref, a_ref, am_ref, av_ref,
    b_ref, bm_ref, bv_ref, c_ref, cm_ref, cv_ref, e_ref, em_ref, ev_ref,
    t_out, tm_out, tv_out, tl_out, a_out, am_out, av_out, al_out, b_out, bm_out, bv_out, bl_out,
    c_out, cm_out, cv_out, e_out, em_out, ev_out, flat_out, factor_ref,
):
    def update(grad, refs, outs, rate, decay):
        new, first, second = adam_step(refs[0][...], grad, refs[1][...], refs[2][...], rate, decay)
        outs[0][...] = new
        outs[1][...] = first
        outs[2][...] = second
        if len(outs) > 3:
            outs[3][...] = new.astype(bf16)

    @pl.when(pl.program_id(0) == 0)
    def _():
        packs = jnp.sum(packs_ref[...], axis=0)
        gain_grad = jnp.concatenate(
            [
                jnp.concatenate([packs[4 * r + i : 4 * r + i + 1] for i in range(D // LANES)], axis=1)
                for r in range(3)
            ],
            axis=0,
        )
        bias_all = packs[16:24]
        squares = jnp.sum(squares_ref[...], axis=0) + row_sum(packs[0:12] * packs[0:12])
        squares = squares + row_sum(bias_all * bias_all)
        norm = jnp.sqrt(jnp.sum(squares, axis=1, keepdims=True))
        factor = jnp.minimum(1.0, clip_at / norm)
        factor_ref[...] = jnp.broadcast_to(factor, factor_ref.shape)
        flat_out[0:2] = packs[12:14]
        flat_out[2:3] = jnp.broadcast_to(norm, (1, LANES))
        flat_out[3:8] = jnp.zeros((5, LANES), f32)
        one = jnp.concatenate([wg_ref[z.order(d), 0 : z.r1] for d in range(z.n_data)], axis=0)
        two = jnp.concatenate(
            [wg_ref[z.order(d), z.r1 : z.r1 + z.r2] for d in range(z.n_data)], axis=0
        )
        update(one.T * factor, (a_ref, am_ref, av_ref), (a_out, am_out, av_out, al_out), 0.04, 0.1)
        update(two * factor, (b_ref, bm_ref, bv_ref), (b_out, bm_out, bv_out, bl_out), 0.04, 0.1)
        update(gain_grad * factor, (c_ref, cm_ref, cv_ref), (c_out, cm_out, cv_out), 0.5, 0.0)
        head = lax.broadcasted_iota(jnp.int32, bias_all.shape, 0)
        first_head = lax.axis_index("mp") * z.heads_dev
        mine = [
            row_sum(jnp.where(head == first_head + r, bias_all, 0.0)) for r in range(z.heads_dev)
        ]
        bias_grad = jnp.concatenate(mine, axis=0)
        update(bias_grad * factor, (e_ref, em_ref, ev_ref), (e_out, em_out, ev_out), 1.0, 0.0)

    update(
        tg_ref[...] * factor_ref[0:1, 0:1], (t_ref, tm_ref, tv_ref), (t_out, tm_out, tv_out, tl_out), 0.5, 0.1
    )


def settle(z, squares, packs, wg, tg, table, f1, f2, gains, bias):
    sds = jax.ShapeDtypeStruct
    rows = next(r for r in range(112, 0, -16) if z.rows_dev % r == 0)
    block = pl.BlockSpec((rows, D), lambda i: (i, 0))

    def like(array, dtype=f32):
        return sds(array.shape, dtype)

    return pl.pallas_call(
        functools.partial(settle_kernel, z),
        grid=(z.rows_dev // rows,),
        out_shape=(
            like(tg), like(tg), like(tg), like(tg, bf16),
            like(f1[0]), like(f1[0]), like(f1[0]), like(f1[0], bf16),
            like(f2[0]), like(f2[0]), like(f2[0]), like(f2[0], bf16),
            like(gains[0]), like(gains[0]), like(gains[0]),
            like(bias[0]), like(bias[0]), like(bias[0]), sds((8, LANES), f32),
        ),
        in_specs=[VM] * 3 + [block] * 4 + [VM] * 12,
        out_specs=(block,) * 4 + (VM,) * 15,
        scratch_shapes=[pltpu.VMEM((8, LANES), f32)],
        compiler_params=pltpu.CompilerParams(vmem_limit_bytes=LIMIT),
        cost_estimate=pl.CostEstimate(
            flops=20 * z.rows_dev * D, bytes_accessed=20_000_000, transcendentals=1_000_000
        ),
        name="settle",
    )(squares, packs, wg, tg, *table, *f1, *f2, *gains, *bias)


def pick(array, index):
    return lax.dynamic_index_in_dim(array, index, 0, keepdims=False)


def per_device(
    lengths, owners, item_rows, buckets, negatives, table, table_m, table_v, w_f1, f1_m, f1_v,
    w_f2, f2_m, f2_v, gains, gains_m, gains_v, bias, bias_m, bias_v,
):
    n_model = lax.axis_size("mp")
    n_data = lax.axis_size("dp")
    model_at = lax.axis_index("mp")
    z = Sizes(n_data, n_model, bias.shape[0], table.shape[0], negatives.shape[1])
    micro = model_at // z.copies
    heads_dev = z.heads_dev
    bucket = pick(buckets, micro)
    lead = (lax.rem(model_at, z.copies) == 0).astype(jnp.int32)
    scalars = jnp.stack([pick(lengths, micro)[0], lead])
    ids = negatives.astype(f32).reshape(MB, n_data, z.rn).transpose(1, 0, 2)
    ids_rows = ids.reshape(-1, 1, LANES)
    ids_cols = jnp.repeat(ids, z.copies, axis=1).reshape(n_data, 1, n_model * z.rn)
    bias_tile = lax.dynamic_update_slice(
        jnp.zeros((HEADS, NB), f32), bias, (model_at * heads_dev, 0)
    )

    asked, slot, w, bias_all, x, n1, q, k, v, do, ghu, gres, ga, stat_a = front(
        z, scalars, table, w_f1, w_f2, bias_tile, owners.reshape(MB, 1, LEN), item_rows, ids_rows,
        bucket, gains,
    )
    asked = asked.reshape(z.n_every, LANES)[:, : z.groups * CH].reshape(z.n_every, z.groups, CH)
    asked = asked.transpose(1, 0, 2).reshape(z.groups, 1, z.slots)
    table_grad, wg, packs, squares = rear(
        z, scalars, x, n1, q, k, v, do, ghu, gres, w, bias_all, bucket, gains, slot, stat_a,
        ga.reshape(2, z.half, z.ra, D), asked, ids_cols,
    )
    *new, flat = settle(
        z, squares, packs, wg, table_grad, (table, table_m, table_v), (w_f1, f1_m, f1_v),
        (w_f2, f2_m, f2_v), (gains, gains_m, gains_v), (bias, bias_m, bias_v),
    )
    return (flat[0, 0], flat[1, 0], flat[2, 0], *new)


def solution(mesh):
    rows, cols = P(("dp", "mp"), None), P(None, "mp")
    heads = P("mp", None)
    in_specs = (
        P(None, "dp"), P(None, "dp", None, None), P(None, "dp", None), P(None, "dp", None), P(),
        rows, rows, rows, cols, cols, cols, heads, heads, heads, P(), P(), P(), heads, heads, heads,
    )
    out_specs = (
        P(), P(), P(), rows, rows, rows, rows, cols, cols, cols, cols,
        heads, heads, heads, heads, P(), P(), P(), heads, heads, heads,
    )
    return jax.shard_map(
        per_device, mesh=mesh, in_specs=in_specs, out_specs=out_specs, check_vma=False
    )
```

time: 646 us -> 254 us (0.39)
  waiting for transfers between devices: 191 us -> 0 us
  Pallas kernels: 308 us -> 243 us
  blocking collectives: 51.9 us -> 0 us
  local copies, waits for them, and re-layouts: 31.2 us -> 6.88 us
  other arithmetic: 26.2 us -> 1.93 us
  between operations: 21.1 us -> 0.7 us
  matrix products: 14.3 us -> 0 us
    psum x2 -> x0, waiting for transfers between devices: 156 us -> none  [the longest x1 101 us: per_device(): neg_all = lax.psum(neg_term, ('dp', 'mp'))]
    pallas_call x4 -> x3, Pallas kernels: 308 us -> 243 us  [the longest x1 126 us: rear(): pl.pallas_call(functools.partial(rear_kernel, z), out_shape=(sds((z.rows_...]
    psum x1 -> x0, blocking collectives: 39.3 us -> none  [per_device(): grad_norm = jnp.sqrt(lax.psum(local, ('dp', 'mp')))]
    reduce_scatter x3 -> x0, waiting for transfers between devices: 35 us -> none  [the longest x1 35 us: per_device(): gneg_sum = lax.psum_scatter(gneg, 'dp', scatter_dimension=0, tiled=True)]
    dot_general x6 -> x0, matrix products: 14.3 us -> none  [the longest x1 5.03 us: per_device(): jnp.dot(neg_hot, table.astype(bf16), preferred_element_type=f32)]
    all_gather x1 -> x0, blocking collectives: 12.6 us -> none  [per_device(): bias_all = lax.all_gather(bias, 'mp', axis=0, tiled=True)]
    unnamed x67 -> x4, local copies, waits for them, and re-layouts: 10.7 us -> 0.01 us
    convert_element_type x7 -> x1, other arithmetic: 10.8 us -> 0.7 us  [per_device(): ids = negatives.astype(f32).reshape(MB, n_data, z.rn).transpose(1, 0, 2)]
  transfers between devices with their start and end apart: 7 -> 0, of which waited for: 3 -> 0; matrix products, arithmetic and copies ran while one was open for 5% -> 0% of each run, Pallas kernels for 42% -> 0%
where the time goes in v2:
time: 254 us; the launch traced here: 252 us
  Pallas kernels  243 us (96%)
  local copies, waits for them, and re-layouts  6.88 us (3%)
    pallas_call x1, Pallas kernels, rear(): pl.pallas_call(functools.partial(rear_kernel, z), out_shape=(sds((z.rows_...  126 us
    pallas_call x1, Pallas kernels, front(): pl.pallas_call(functools.partial(front_kernel, z), out_shape=(sds((z.n_ev...  103 us
    pallas_call x1, Pallas kernels, settle(): pl.pallas_call(functools.partial(settle_kernel, z), grid=(z.rows_dev // r...  13.1 us

profile of v2, /device:TPU:0, one launch (start us, length us, event | category | flops | bytes accessed | tf_op | source)
XLA Modules:
  0.0 252.1 jit_solution(15562521435525811531)
XLA Ops:
  0.7 0.0 copy-start
  0.7 1.2 constant_dynamic-slice_fusion
  1.9 1.2 pad_add_fusion.len_ref
  3.1 0.0 copy-done
  3.1 0.6 dynamic-slice_bitcast_fusion.bucket_ref
  3.7 0.7 constant_dynamic-update-slice_fusion.bias_ref
  4.4 0.0 copy-start.1
  4.4 0.7 convert_element_type.4
  5.1 0.1 reshape.64
  5.2 0.7 reshape_reshape_broadcast_in_dim.3.ids_ref
  5.9 0.7 reshape.65.ids_ref
  6.6 0.0 copy-done.1
  6.6 103.5 %front.1 = (f32[32,1,128]{2,1,0:T(1,128)}, f32[4,1,256]{2,1,0:T(1,128)}, bf16[8,4,80,512]{3,2,1,0:T(8,128)(2,1)}, f32[4,8,128]{2,1,0:T(8,128)}, bf16[1024,512]{1...) custom-call(s32[2]{0:T(128)} %pad_add_fusion.len_ref, ...), custom_call_target="tpu_custom_call" | custom-call | flops 60000002048 | bytes 30000000 | tf_op jit(solution)/shard_map/front/pallas_call | solution.py:597
  110.1 0.8 copy.44
  110.9 0.1 copy.45
  111.0 0.7 reshape.70.asked_ref
  111.7 126.0 %rear.1 = (f32[784,512]{1,0:T(8,128)}, f32[8,80,512]{2,1,0:T(8,128)}, f32[32,24,128]{2,1,0:T(8,128)}, f32[32,1,128]{2,1,0:T(1,128)}) custom-call(s32[2]{0:T(128)} %pad_add_fusion.len_ref, bf16[1024,512]{1,0:T(8,128)(2,1)} %get-tuple-element.58.x_ref, bf16[1024,512]{1,0:T(8,128)(2,1)} %get-tuple-element.59.n1_ref, ...), custom_call_target="tpu_custom_call" | custom-call | flops 60000002048 | bytes 30000000 | tf_op jit(solution)/shard_map/rear/pallas_call | solution.py:1049
  237.7 13.1 %settle.1 = (f32[784,512]{1,0:T(8,128)}, f32[784,512]{1,0:T(8,128)}, f32[784,512]{1,0:T(8,128)}, bf16[784,512]{1,0:T(8,128)(2,1)}, f32[512,512]{1,0:T(8,128)}, /...) custom-call(f32[32,1,128]{2,1,0:T(1,128)} %get-tuple-element.72.squa, ...), custom_call_target="tpu_custom_call" | custom-call | flops 8028160 | bytes 20000000 | tf_op jit(solution)/shard_map/settle/pallas_call | solution.py:1168
  250.8 1.3 fusion
  (2 shorter events, 0.0 us)
Async XLA Ops:
  0.7 2.5 copy-start
  4.4 2.2 copy-start.1

commit v3 on v2

--- a/solution.py
+++ b/solution.py
@@ -21,7 +21,7 @@
 WIDE = 2 * DH
 CH = 16
 LANES = 128
-ASK = 4
+SPAN = 2
 
 epsilon = 1e-06
 clip_at = 1.0
@@ -33,7 +33,7 @@
 bf16 = jnp.bfloat16
 MESH = pl.DeviceIdType.MESH
 VM = pl.BlockSpec(memory_space=pltpu.VMEM)
-LIMIT = 60 * 1024 * 1024
+LIMIT = 61 * 1024 * 1024
 
 NN = (((1,), (0,)), ((), ()))
 NT_ = (((1,), (1,)), ((), ()))
@@ -125,10 +125,10 @@
                 w2_ref[at : at + z.r2, :] = w_ref[z.order(d), k, z.r1 : z.r1 + z.r2, :]
 
 
-def key_bias(bias_ref, bucket_ref, length):
+def key_bias(bias_ref, bucket, length):
     table = jnp.sum(bias_ref[...], axis=0)
     hot = jnp.where(
-        lax.broadcasted_iota(jnp.int32, (NB, LEN), 0) == bucket_ref[...], 1.0, 0.0
+        lax.broadcasted_iota(jnp.int32, (NB, LEN), 0) == bucket, 1.0, 0.0
     )
     rows = lax.dot_general(table, hot, NN, precision=highest, preferred_element_type=f32)
     inside = lax.broadcasted_iota(jnp.int32, (8, LEN), 1) < length
@@ -222,7 +222,11 @@
     w_ref[here, k, z.r1 :, :] = mm(
         jnp.where(take, 1.0, 0.0).astype(bf16), f2_ref[...].astype(bf16)
     ).astype(bf16)
-    bias_all_ref[k] = bias_ref[...]
+    head = lax.broadcasted_iota(jnp.int32, (HEADS, NB), 0)
+    bias_tile = jnp.zeros((HEADS, NB), f32)
+    for r in range(z.heads_dev):
+        bias_tile += jnp.where(head == k * z.heads_dev + r, bias_ref[r : r + 1, :], 0.0)
+    bias_all_ref[k] = bias_tile
 
     def wz_copy(i, at, to):
         return remote(
@@ -230,7 +234,9 @@
         )
 
     def bz_copy(i, at, to):
-        return remote(bias_ref, bias_all_ref.at[at], bz_send.at[i], bz_recv.at[at], (d, to))
+        return remote(
+            bias_all_ref.at[k], bias_all_ref.at[at], bz_send.at[i], bz_recv.at[at], (d, to)
+        )
 
     for i in range(1, n_model):
         to = lax.rem(k + i, n_model)
@@ -351,15 +357,15 @@
     for g in range(2, z.groups):
         serve(g)
 
-    length = len_ref[0]
-    lead = len_ref[1]
+    length = len_ref[micro, 0]
+    lead = (lax.rem(k, z.copies) == 0).astype(jnp.int32)
     gain_in = gains_ref[0:1, :]
     gain_attn = gains_ref[1:2, :]
     gain_out = gains_ref[2:3, :]
     for i in range(1, n_model):
         at = lax.rem(k + i, n_model)
         bz_copy(i, at, k).wait_recv()
-    kb = key_bias(bias_all_ref, bucket_ref, length)
+    kb = key_bias(bias_all_ref, bucket_ref[micro], length)
     for j in range(NT):
         kb_ref[j] = kb[:, j * TB : (j + 1) * TB]
     xf_ref[LEN:, :] = jnp.zeros((8, D), f32)
@@ -450,23 +456,25 @@
         place = lax.broadcasted_iota(jnp.int32, (TB, 1), 0) + i * TB
         inv = 1.0 / (place.astype(f32) + 1.0)
         inv2 = jnp.concatenate([inv, inv], axis=0)
-        for p in range(PAIRS):
-            q2 = halves(q_ref[p, rows, :])
-
-            def part(j, total, masked, p=p, q2=q2):
-                keys = pl.ds(pl.multiple_of(j * TB, TB), TB)
-                kb = kb_ref[j]
-                kb = jnp.where(first_half, kb[2 * p : 2 * p + 1, :], kb[2 * p + 1 : 2 * p + 2, :])
-                h = mm(q2, k_ref[p, keys, :], NT_) + kb
+        o_ref[:, rows, :] = jnp.zeros((PAIRS, TB, WIDE), f32)
+
+        def part(j, masked):
+            keys = pl.ds(pl.multiple_of(j * TB, TB), TB)
+            kb = kb_ref[j]
+            for p in range(PAIRS):
+                kb2 = jnp.where(first_half, kb[2 * p : 2 * p + 1, :], kb[2 * p + 1 : 2 * p + 2, :])
+                h = mm(halves(q_ref[p, rows, :]), k_ref[p, keys, :], NT_) + kb2
                 w = (h + h * jnp.tanh(h)) * inv2
                 if masked:
                     w = jnp.where(causal, w, 0.0)
-                return total + mm(beside(w.astype(bf16)), halves(v_ref[p, keys, :]))
-
-            total = lax.fori_loop(
-                0, i, functools.partial(part, masked=False), jnp.zeros((TB, WIDE), f32)
-            )
-            o_ref[p, rows, :] = part(i, total, True)
+                o_ref[p, rows, :] += mm(beside(w.astype(bf16)), halves(v_ref[p, keys, :]))
+
+        def before(j, carry):
+            part(j, False)
+            return carry
+
+        lax.fori_loop(0, i, before, 0)
+        part(i, True)
 
     def lose(i):
         rows = pl.ds(pl.multiple_of(i * TB, TB), TB)
@@ -537,7 +545,6 @@
             release(g)
 
     def after_two():
-        neg_two()
         neg_three()
         neg_four()
         lax.fori_loop(0, NT - 2, last, 0)
@@ -545,6 +552,7 @@
     def step(i, carry):
         if per_group == 1:
             pl.when(i > 0)(lambda: arrive(i))
+        pl.when(i == NT - 2)(neg_two)
         inputs(i)
         attend(i)
         pl.when(i == 1)(after_one)
@@ -647,11 +655,11 @@
     z, len_ref, x_ref, n1_ref, q_ref, k_ref, v_ref, do_ref, ghu_ref, gres_ref, w_ref, bias_ref, bucket_ref,
     gains_ref, slot_ref, stat_in_ref, ga_ref, asked_ref, ids_ref,
     tg_ref, wg_ref, packs_ref, squares_ref,
-    gh_ref, hid_ref, kb_ref, dq_ref, dk_ref, dv_ref, bs_ref, w1_ref, stat_ref, pack_ref, out_ref, gb_ref,
+    gh_ref, hid_ref, kb_ref, dq_ref, dk_ref, dv_ref, kt_ref, bs_ref, w1_ref, stat_ref, pack_ref, out_ref, gb_ref,
     got_ref, pa_ref, pb_ref, sa_ref, sb_ref, ca_ref, cb_ref, zs_ref, zr_ref, ng_ref, sq_ref,
     row_send, row_recv, pack_send, pack_recv,
     pa_send, pa_recv, pb_send, pb_recv, ca_send, ca_recv, cb_send, cb_recv,
-    zw_send, zw_recv, zn_send, zn_recv, gw_send, gw_recv, gn_send, gn_recv,
+    zw_send, zw_recv, zf_send, zf_recv, zn_send, zn_recv, gw_send, gw_recv, gn_send, gn_recv,
     hw_send, hw_recv, hn_send, hn_recv, sq_send, sq_recv,
 ):
     n_every, n_model, half = z.n_every, z.n_model, z.half
@@ -663,6 +671,7 @@
     chip = d // 2
     here = side * half + chip
     other = d + 1 - 2 * side
+    micro = k // z.copies
     barrier = pltpu.get_barrier_semaphore()
 
     def signal(i, carry):
@@ -704,7 +713,16 @@
         )
 
     def zw_copy(at, to):
-        return remote(zs_ref.at[to], zr_ref.at[at], zw_send.at[to], zw_recv.at[at], (d, to))
+        part = pl.ds(0, z.r1)
+        return remote(
+            zs_ref.at[to, part], zr_ref.at[at, part], zw_send.at[to], zw_recv.at[at], (d, to)
+        )
+
+    def zf_copy(at, to):
+        part = pl.ds(z.r1, z.r2p)
+        return remote(
+            zs_ref.at[to, part], zr_ref.at[at, part], zf_send.at[to], zf_recv.at[at], (d, to)
+        )
 
     def gw_copy(i, at, to):
         return remote(
@@ -748,7 +766,9 @@
         ng_ref[here, k] = total[n_model * z.r2p :].astype(bf16)
         zs_ref[:, z.r1 :, :] = total[: n_model * z.r2p].reshape(n_model, z.r2p, D)
         for i in range(1, n_model):
-            zn_copy(i, k, lax.rem(k + i, n_model)).start()
+            to = lax.rem(k + i, n_model)
+            zn_copy(i, k, to).start()
+            zf_copy(k, to).start()
 
     def planes_b(p):
         total = sb_ref[p, chip].astype(f32)
@@ -776,7 +796,7 @@
 
     gain_in = gains_ref[0:1, :]
     place_weights(z, w_ref, w1_ref, None)
-    kb_ref[...] = key_bias(bias_ref, bucket_ref, len_ref[0]).T
+    kb_ref[...] = key_bias(bias_ref, bucket_ref[micro], len_ref[micro, 0]).T
 
     def inputs(i, carry):
         rows = pl.ds(pl.multiple_of(i * TB, TB), TB)
@@ -838,89 +858,117 @@
                         ]
         pb_copy(p).start()
 
+    early = range(PAIRS - SPAN)
+    late = range(PAIRS - SPAN, PAIRS)
+
+    def first_hook():
+        for p in early:
+            chips_b(p)
+
+    def second_hook():
+        swap_a()
+        for p in early:
+            planes_b(p)
+
+    def late_weights():
+        for p in late:
+            weights_grad(p)
+
     pl.semaphore_wait(barrier, n_every - 1)
     pa_copy.start()
 
-    for p in range(PAIRS):
-        lanes = slice(p * WIDE, (p + 1) * WIDE)
-        dq_ref[...] = jnp.zeros_like(dq_ref)
+    def keys_of(p, j):
+        keys = pl.ds(pl.multiple_of(j * TB, TB), TB)
+        at = p % SPAN
+        kt = k_ref[p, keys, :].astype(f32).T
+        low = lax.broadcasted_iota(jnp.int32, kt.shape, 0) < DH
+        kt_ref[at] = jnp.concatenate(
+            [jnp.where(low, kt, 0.0), jnp.where(low, 0.0, kt)], axis=1
+        ).astype(bf16)
+        dk_ref[at] = jnp.zeros((TB, WIDE + LANES), f32)
+        dv_ref[at] = jnp.zeros((TB, WIDE), f32)
+
+    def part(p, i, j, masked):
+        keys = pl.ds(pl.multiple_of(j * TB, TB), TB)
+        rows = pl.ds(pl.multiple_of(i * TB, TB), TB)
+        at = p % SPAN
+        q = q_ref[p, rows, :]
+        do = do_ref[p, rows, :]
+        kb = jnp.concatenate(
+            [kb_ref[keys, 2 * p : 2 * p + 1], kb_ref[keys, 2 * p + 1 : 2 * p + 2]], axis=0
+        )
         mark = jnp.where(
             ones_lane == jnp.where(ones_half, 2 * p + 1, 2 * p), 1.0, 0.0
         ).astype(bf16)
-
-        def keys_step(j, carry, p=p, lanes=lanes, mark=mark):
-            keys = pl.ds(pl.multiple_of(j * TB, TB), TB)
-            k2 = halves(k_ref[p, keys, :])
-            v2 = halves(v_ref[p, keys, :])
-            kt = k_ref[p, keys, :].astype(f32).T
-            low = lax.broadcasted_iota(jnp.int32, kt.shape, 0) < DH
-            kt2 = jnp.concatenate(
-                [jnp.where(low, kt, 0.0), jnp.where(low, 0.0, kt)], axis=1
-            ).astype(bf16)
-            kb = jnp.concatenate(
-                [kb_ref[keys, 2 * p : 2 * p + 1], kb_ref[keys, 2 * p + 1 : 2 * p + 2]], axis=0
-            )
-            dk_ref[...] = jnp.zeros_like(dk_ref)
-            dv_ref[...] = jnp.zeros_like(dv_ref)
-
-            def part(i, masked):
-                rows = pl.ds(pl.multiple_of(i * TB, TB), TB)
-                q = q_ref[p, rows, :]
-                do = do_ref[p, rows, :]
-                place = lax.broadcasted_iota(jnp.int32, (1, TB), 1) + i * TB
-                inv = 1.0 / (place.astype(f32) + 1.0)
-                h = mm(k2, q, NT_) + kb
-                t = jnp.tanh(h)
-                m = h * t
-                w = (h + m) * inv
-                ds = mm(v2, do, NT_) * ((1.0 + t) * (0.5 * inv)) * (1.0 + h - m)
-                if masked:
-                    w = jnp.where(causal, w, 0.0)
-                    ds = jnp.where(causal, ds, 0.0)
-                ds = ds.astype(bf16)
-                dv_ref[...] += mm(beside(w.astype(bf16)), halves(do))
-                dk_ref[...] += mm(beside(ds), jnp.concatenate([halves(q), mark], axis=1))
-                dq_ref[i] += mm(kt2, ds)
-
-            part(j, True)
+        place = lax.broadcasted_iota(jnp.int32, (1, TB), 1) + i * TB
+        inv = 1.0 / (place.astype(f32) + 1.0)
+        h = mm(halves(k_ref[p, keys, :]), q, NT_) + kb
+        t = jnp.tanh(h)
+        m = h * t
+        w = (h + m) * inv
+        ds = mm(halves(v_ref[p, keys, :]), do, NT_) * ((1.0 + t) * (0.5 * inv)) * (1.0 + h - m)
+        if masked:
+            w = jnp.where(causal, w, 0.0)
+            ds = jnp.where(causal, ds, 0.0)
+        ds = ds.astype(bf16)
+        dv_ref[at] += mm(beside(w.astype(bf16)), halves(do))
+        dk_ref[at] += mm(beside(ds), jnp.concatenate([halves(q), mark], axis=1))
+        dq_ref[at, i] += mm(kt_ref[at], ds)
+
+    def keys_end(p, j):
+        keys = pl.ds(pl.multiple_of(j * TB, TB), TB)
+        lanes = slice(p * WIDE, (p + 1) * WIDE)
+        at = p % SPAN
+        slope_v = silu_parts(hid_ref[0, keys, lanes])[1]
+        slope_k = silu_parts(hid_ref[2, keys, lanes])[1]
+        slope_q = silu_parts(hid_ref[1, keys, lanes])[1]
+        gh_ref[0, keys, lanes] = (dv_ref[at] * slope_v).astype(bf16)
+        gh_ref[2, keys, lanes] = (dk_ref[at, :, :WIDE] * 2.0 * slope_k).astype(bf16)
+        gh_ref[1, keys, lanes] = (dq_ref[at, j].T * DH ** (-0.5) * slope_q).astype(bf16)
+        bs_ref[keys, :] += dk_ref[at, :, WIDE:]
+
+    for phase in range(PAIRS // SPAN):
+        pairs = range(phase * SPAN, (phase + 1) * SPAN)
+        final = phase == PAIRS // SPAN - 1
+        dq_ref[...] = jnp.zeros_like(dq_ref)
+
+        def keys_step(j, carry, pairs=pairs, final=final, phase=phase):
+            for p in pairs:
+                keys_of(p, j)
+            for p in pairs:
+                part(p, j, j, True)
 
             def later(i, inner):
-                part(i, False)
+                for p in pairs:
+                    part(p, i, j, False)
                 return inner
 
             lax.fori_loop(j + 1, NT, later, 0)
-            slope_v = silu_parts(hid_ref[0, keys, lanes])[1]
-            slope_k = silu_parts(hid_ref[2, keys, lanes])[1]
-            gh_ref[0, keys, lanes] = (dv_ref[...] * slope_v).astype(bf16)
-            gh_ref[2, keys, lanes] = (dk_ref[:, :WIDE] * 2.0 * slope_k).astype(bf16)
-            bs_ref[keys, :] += dk_ref[:, WIDE:]
-            slope_q = silu_parts(hid_ref[1, keys, lanes])[1]
-            gh_ref[1, keys, lanes] = (dq_ref[j].T * DH ** (-0.5) * slope_q).astype(bf16)
-            if p == PAIRS - 1:
+            for p in pairs:
+                keys_end(p, j)
+            if phase == 0:
+                pl.when(j == 0)(chips_a)
+                pl.when(j == 1)(planes_a)
+                pl.when(j == 2)(spread_a)
+            if final:
+                pl.when(j == NT - 1)(late_weights)
                 outputs(j)
                 if per_group == 1:
                     send_group(j)
-                pl.when(j == 0)(functools.partial(chips_b, PAIRS - 2))
-                pl.when(j == 1)(functools.partial(planes_b, PAIRS - 3))
-                pl.when(j == 2)(spread_a)
+                pl.when(j == 0)(first_hook)
+                pl.when(j == 2)(second_hook)
             return carry
 
         lax.fori_loop(0, NT, keys_step, 0)
-        weights_grad(p)
-        if p == 0:
-            chips_a()
-        elif p < PAIRS - 1:
-            chips_b(p - 1)
-            if p == 1:
-                planes_a()
-            else:
-                planes_b(p - 2)
+        if not final:
+            for p in pairs:
+                weights_grad(p)
 
     if per_group > 1:
         for g in range(z.groups):
             send_group(g)
     hot = jnp.where(
-        lax.broadcasted_iota(jnp.int32, (NB, LEN), 0) == bucket_ref[...], 1.0, 0.0
+        lax.broadcasted_iota(jnp.int32, (NB, LEN), 0) == bucket_ref[micro], 1.0, 0.0
     )
     bias_grad = lax.dot_general(hot, bs_ref[...], NN, precision=highest, preferred_element_type=f32)
     for i in range(D // LANES):
@@ -964,27 +1012,28 @@
         hot = jnp.where(row_at == ids_ref[at] - base, 1.0, 0.0).astype(bf16)
         tg_ref[...] += mm(hot, ng_ref[at].reshape(neg_rows, D))
 
-    planes_b(PAIRS - 2)
-    swap_a()
-    chips_b(PAIRS - 1)
+    for p in late:
+        chips_b(p)
     collect(0)
     for i in range(half):
         negatives(side * half + i)
-    planes_b(PAIRS - 1)
+    for i in range(half):
+        hn_copy((1 - side) * half + i).wait_recv()
+        negatives((1 - side) * half + i)
+    for p in late:
+        planes_b(p)
     for g in range(1, max(1, z.groups - 1)):
         collect(g)
     total = zs_ref[k]
     for i in range(1, n_model):
         at = lax.rem(k + i, n_model)
         zw_copy(at, k).wait_recv()
+        zf_copy(at, k).wait_recv()
         total = total + zr_ref[at]
     wg_ref[here] = total
     for i in range(1, half):
         gw_copy(i, here, lax.rem(chip + i, half)).start()
     hw_copy(here).start()
-    for i in range(half):
-        hn_copy((1 - side) * half + i).wait_recv()
-        negatives((1 - side) * half + i)
     if z.groups > 1:
         collect(z.groups - 1)
 
@@ -1019,6 +1068,7 @@
         to = lax.rem(k + i, n_model)
         zn_copy(i, k, to).wait_send()
         zw_copy(k, to).wait_send()
+        zf_copy(k, to).wait_send()
     pa_copy.wait_send()
     for p in range(PAIRS):
         pb_copy(p).wait_send()
@@ -1060,9 +1110,10 @@
             vm((3, LEN, D), bf16),
             vm((3, LEN, D), f32),
             vm((LEN, 8), f32),
-            vm((NT, WIDE, TB), f32),
-            vm((TB, WIDE + LANES), f32),
-            vm((TB, WIDE), f32),
+            vm((SPAN, NT, WIDE, TB), f32),
+            vm((SPAN, TB, WIDE + LANES), f32),
+            vm((SPAN, TB, WIDE), f32),
+            vm((SPAN, WIDE, 2 * TB), bf16),
             vm((LEN, LANES), f32),
             vm((4, D, D), bf16),
             vm((8, D), f32),
@@ -1082,7 +1133,8 @@
             vm((1, LANES), f32),
             dma(groups_every), dma(groups_every), dma(every), dma(every),
             dma, dma, dma(pairs), dma(pairs), dma(half), dma(half), dma(pairs_half), dma(pairs_half),
-            dma(model), dma(model), dma(model), dma(model), dma(half), dma(data), dma(half), dma(data),
+            dma(model), dma(model), dma(model), dma(model), dma(model), dma(model),
+            dma(half), dma(data), dma(half), dma(data),
             dma(data), dma(data), dma(data), dma(data), dma(every), dma(every),
         ],
         compiler_params=pltpu.CompilerParams(
@@ -1108,7 +1160,7 @@
     z, squares_ref, packs_ref, wg_ref, tg_ref, t_ref, tm_ref, tv_ref, a_ref, am_ref, av_ref,
     b_ref, bm_ref, bv_ref, c_ref, cm_ref, cv_ref, e_ref, em_ref, ev_ref,
     t_out, tm_out, tv_out, tl_out, a_out, am_out, av_out, al_out, b_out, bm_out, bv_out, bl_out,
-    c_out, cm_out, cv_out, e_out, em_out, ev_out, flat_out, factor_ref,
+    c_out, cm_out, cv_out, e_out, em_out, ev_out, flat_out, factor_ref, one_ref,
 ):
     def update(grad, refs, outs, rate, decay):
         new, first, second = adam_step(refs[0][...], grad, refs[1][...], refs[2][...], rate, decay)
@@ -1141,7 +1193,7 @@
         two = jnp.concatenate(
             [wg_ref[z.order(d), z.r1 : z.r1 + z.r2] for d in range(z.n_data)], axis=0
         )
-        update(one.T * factor, (a_ref, am_ref, av_ref), (a_out, am_out, av_out, al_out), 0.04, 0.1)
+        one_ref[...] = one.T * factor
         update(two * factor, (b_ref, bm_ref, bv_ref), (b_out, bm_out, bv_out, bl_out), 0.04, 0.1)
         update(gain_grad * factor, (c_ref, cm_ref, cv_ref), (c_out, cm_out, cv_out), 0.5, 0.0)
         head = lax.broadcasted_iota(jnp.int32, bias_all.shape, 0)
@@ -1152,6 +1204,9 @@
         bias_grad = jnp.concatenate(mine, axis=0)
         update(bias_grad * factor, (e_ref, em_ref, ev_ref), (e_out, em_out, ev_out), 1.0, 0.0)
 
+    size = a_ref.shape[0]
+    rows = pl.ds(pl.multiple_of(pl.program_id(0) * size, size), size)
+    update(one_ref[rows, :], (a_ref, am_ref, av_ref), (a_out, am_out, av_out, al_out), 0.04, 0.1)
     update(
         tg_ref[...] * factor_ref[0:1, 0:1], (t_ref, tm_ref, tv_ref), (t_out, tm_out, tv_out, tl_out), 0.5, 0.1
     )
@@ -1160,14 +1215,17 @@
 def settle(z, squares, packs, wg, tg, table, f1, f2, gains, bias):
     sds = jax.ShapeDtypeStruct
     rows = next(r for r in range(112, 0, -16) if z.rows_dev % r == 0)
-    block = pl.BlockSpec((rows, D), lambda i: (i, 0))
+    blocks = z.rows_dev // rows
+    steps = next(n for n in range(blocks, 512) if D % n == 0 and D // n % 16 == 0)
+    block = pl.BlockSpec((rows, D), lambda i: (jnp.minimum(i, blocks - 1), 0))
+    part = pl.BlockSpec((D // steps, 4 * z.fw), lambda i: (i, 0))
 
     def like(array, dtype=f32):
         return sds(array.shape, dtype)
 
     return pl.pallas_call(
         functools.partial(settle_kernel, z),
-        grid=(z.rows_dev // rows,),
+        grid=(steps,),
         out_shape=(
             like(tg), like(tg), like(tg), like(tg, bf16),
             like(f1[0]), like(f1[0]), like(f1[0]), like(f1[0], bf16),
@@ -1175,9 +1233,9 @@
             like(gains[0]), like(gains[0]), like(gains[0]),
             like(bias[0]), like(bias[0]), like(bias[0]), sds((8, LANES), f32),
         ),
-        in_specs=[VM] * 3 + [block] * 4 + [VM] * 12,
-        out_specs=(block,) * 4 + (VM,) * 15,
-        scratch_shapes=[pltpu.VMEM((8, LANES), f32)],
+        in_specs=[VM] * 3 + [block] * 4 + [part] * 3 + [VM] * 9,
+        out_specs=(block,) * 4 + (part,) * 4 + (VM,) * 11,
+        scratch_shapes=[pltpu.VMEM((8, LANES), f32), pltpu.VMEM((D, 4 * z.fw), f32)],
         compiler_params=pltpu.CompilerParams(vmem_limit_bytes=LIMIT),
         cost_estimate=pl.CostEstimate(
             flops=20 * z.rows_dev * D, bytes_accessed=20_000_000, transcendentals=1_000_000
@@ -1186,6 +1244,94 @@
     )(squares, packs, wg, tg, *table, *f1, *f2, *gains, *bias)
 
 
+def settle_kernel(
+    z, squares_ref, packs_ref, wg_ref, tg_ref, t_ref, tm_ref, tv_ref, a_ref, am_ref, av_ref,
+    b_ref, bm_ref, bv_ref, c_ref, cm_ref, cv_ref, e_ref, em_ref, ev_ref,
+    t_out, tm_out, tv_out, tl_out, a_out, am_out, av_out, al_out, b_out, bm_out, bv_out, bl_out,
+    c_out, cm_out, cv_out, e_out, em_out, ev_out, flat_out, factor_ref, one_ref,
+):
+    def update(grad, refs, outs, rate, decay):
+        new, first, second = adam_step(refs[0][...], grad, refs[1][...], refs[2][...], rate, decay)
+        outs[0][...] = new
+        outs[1][...] = first
+        outs[2][...] = second
+        if len(outs) > 3:
+            outs[3][...] = new.astype(bf16)
+
+    @pl.when(pl.program_id(0) == 0)
+    def _():
+        packs = jnp.sum(packs_ref[...], axis=0)
+        gain_grad = jnp.concatenate(
+            [
+                jnp.concatenate([packs[4 * r + i : 4 * r + i + 1] for i in range(D // LANES)], axis=1)
+                for r in range(3)
+            ],
+            axis=0,
+        )
+        bias_all = packs[16:24]
+        squares = jnp.sum(squares_ref[...], axis=0) + row_sum(packs[0:12] * packs[0:12])
+        squares = squares + row_sum(bias_all * bias_all)
+        norm = jnp.sqrt(jnp.sum(squares, axis=1, keepdims=True))
+        factor = jnp.minimum(1.0, clip_at / norm)
+        factor_ref[...] = jnp.broadcast_to(factor, factor_ref.shape)
+        flat_out[0:2] = packs[12:14]
+        flat_out[2:3] = jnp.broadcast_to(norm, (1, LANES))
+        flat_out[3:8] = jnp.zeros((5, LANES), f32)
+        one = jnp.concatenate([wg_ref[z.order(d), 0 : z.r1] for d in range(z.n_data)], axis=0)
+        two = jnp.concatenate(
+            [wg_ref[z.order(d), z.r1 : z.r1 + z.r2] for d in range(z.n_data)], axis=0
+        )
+        one_ref[...] = one.T * factor
+        update(two * factor, (b_ref, bm_ref, bv_ref), (b_out, bm_out, bv_out, bl_out), 0.04, 0.1)
+        update(gain_grad * factor, (c_ref, cm_ref, cv_ref), (c_out, cm_out, cv_out), 0.5, 0.0)
+        head = lax.broadcasted_iota(jnp.int32, bias_all.shape, 0)
+        first_head = lax.axis_index("mp") * z.heads_dev
+        mine = [
+            row_sum(jnp.where(head == first_head + r, bias_all, 0.0)) for r in range(z.heads_dev)
+        ]
+        bias_grad = jnp.concatenate(mine, axis=0)
+        update(bias_grad * factor, (e_ref, em_ref, ev_ref), (e_out, em_out, ev_out), 1.0, 0.0)
+
+    size = a_ref.shape[0]
+    rows = pl.ds(pl.multiple_of(pl.program_id(0) * size, size), size)
+    update(one_ref[rows, :], (a_ref, am_ref, av_ref), (a_out, am_out, av_out, al_out), 0.04, 0.1)
+    update(
+        tg_ref[...] * factor_ref[0:1, 0:1], (t_ref, tm_ref, tv_ref), (t_out, tm_out, tv_out, tl_out), 0.5, 0.1
+    )
+
+
+def settle(z, squares, packs, wg, tg, table, f1, f2, gains, bias):
+    sds = jax.ShapeDtypeStruct
+    rows = next(r for r in range(112, 0, -16) if z.rows_dev % r == 0)
+    blocks = z.rows_dev // rows
+    steps = next(n for n in range(blocks, 512) if D % n == 0 and D // n % 16 == 0)
+    block = pl.BlockSpec((rows, D), lambda i: (jnp.minimum(i, blocks - 1), 0))
+    part = pl.BlockSpec((D // steps, 4 * z.fw), lambda i: (i, 0))
+
+    def like(array, dtype=f32):
+        return sds(array.shape, dtype)
+
+    return pl.pallas_call(
+        functools.partial(settle_kernel, z),
+        grid=(steps,),
+        out_shape=(
+            like(tg), like(tg), like(tg), like(tg, bf16),
+            like(f1[0]), like(f1[0]), like(f1[0]), like(f1[0], bf16),
+            like(f2[0]), like(f2[0]), like(f2[0]), like(f2[0], bf16),
+            like(gains[0]), like(gains[0]), like(gains[0]),
+            like(bias[0]), like(bias[0]), like(bias[0]), sds((8, LANES), f32),
+        ),
+        in_specs=[VM] * 3 + [block] * 4 + [part] * 3 + [VM] * 9,
+        out_specs=(block,) * 4 + (part,) * 4 + (VM,) * 11,
+        scratch_shapes=[pltpu.VMEM((8, LANES), f32), pltpu.VMEM((D, 4 * z.fw), f32)],
+        compiler_params=pltpu.CompilerParams(vmem_limit_bytes=LIMIT),
+        cost_estimate=pl.CostEstimate(
+            flops=20 * z.rows_dev * D, bytes_accessed=20_000_000, transcendentals=1_000_000
+        ),
+        name="settle",
+    )(squares, packs, wg, tg, *table, *f1, *f2, *gains, *bias)
+
+
 def pick(array, index):
     return lax.dynamic_index_in_dim(array, index, 0, keepdims=False)
 
@@ -1196,28 +1342,19 @@
 ):
     n_model = lax.axis_size("mp")
     n_data = lax.axis_size("dp")
-    model_at = lax.axis_index("mp")
     z = Sizes(n_data, n_model, bias.shape[0], table.shape[0], negatives.shape[1])
-    micro = model_at // z.copies
-    heads_dev = z.heads_dev
-    bucket = pick(buckets, micro)
-    lead = (lax.rem(model_at, z.copies) == 0).astype(jnp.int32)
-    scalars = jnp.stack([pick(lengths, micro)[0], lead])
     ids = negatives.astype(f32).reshape(MB, n_data, z.rn).transpose(1, 0, 2)
     ids_rows = ids.reshape(-1, 1, LANES)
     ids_cols = jnp.repeat(ids, z.copies, axis=1).reshape(n_data, 1, n_model * z.rn)
-    bias_tile = lax.dynamic_update_slice(
-        jnp.zeros((HEADS, NB), f32), bias, (model_at * heads_dev, 0)
-    )
 
     asked, slot, w, bias_all, x, n1, q, k, v, do, ghu, gres, ga, stat_a = front(
-        z, scalars, table, w_f1, w_f2, bias_tile, owners.reshape(MB, 1, LEN), item_rows, ids_rows,
-        bucket, gains,
+        z, lengths, table, w_f1, w_f2, bias, owners.reshape(MB, 1, LEN), item_rows, ids_rows,
+        buckets, gains,
     )
     asked = asked.reshape(z.n_every, LANES)[:, : z.groups * CH].reshape(z.n_every, z.groups, CH)
     asked = asked.transpose(1, 0, 2).reshape(z.groups, 1, z.slots)
     table_grad, wg, packs, squares = rear(
-        z, scalars, x, n1, q, k, v, do, ghu, gres, w, bias_all, bucket, gains, slot, stat_a,
+        z, lengths, x, n1, q, k, v, do, ghu, gres, w, bias_all, buckets, gains, slot, stat_a,
         ga.reshape(2, z.half, z.ra, D), asked, ids_cols,
     )
     *new, flat = settle(

time: 254 us -> 246 us (0.969)
  Pallas kernels: 243 us -> 237 us
    pallas_call x1, Pallas kernels: 103 us -> 99.5 us  [front(): pl.pallas_call(functools.partial(front_kernel, z), out_shape=(sds((z.n_ev...]
where the time goes in v3:
time: 246 us; the launch traced here: 244 us
  Pallas kernels  237 us (96%)
  local copies, waits for them, and re-layouts  5.66 us (2%)
    pallas_call x1, Pallas kernels, rear(): pl.pallas_call(functools.partial(rear_kernel, z), out_shape=(sds((z.rows_...  124 us
    pallas_call x1, Pallas kernels, front(): pl.pallas_call(functools.partial(front_kernel, z), out_shape=(sds((z.n_ev...  99.5 us
    pallas_call x1, Pallas kernels, settle(): pl.pallas_call(functools.partial(settle_kernel, z), grid=(steps,), out_sh...  12.9 us

profile of v3, /device:TPU:0, one launch (start us, length us, event | category | flops | bytes accessed | tf_op | source)
XLA Modules:
  0.0 243.6 jit_solution(12417871979970926520)
XLA Ops:
  0.7 1.3 copy.49.len_ref
  2.0 0.7 convert_element_type.3
  2.7 0.1 reshape.64
  2.8 0.7 reshape_reshape_broadcast_in_dim.3.ids_ref
  3.4 0.7 reshape.65.ids_ref
  4.1 99.5 %front.1 = (f32[32,1,128]{2,1,0:T(1,128)}, f32[4,1,256]{2,1,0:T(1,128)}, bf16[8,4,80,512]{3,2,1,0:T(8,128)(2,1)}, f32[4,8,128]{2,1,0:T(8,128)}, bf16[1024,512]{1...) custom-call(s32[4,1]{1,0:T(4,128)} %copy.49.len_ref, ...), custom_call_target="tpu_custom_call" | custom-call | flops 60000002048 | bytes 30000000 | tf_op jit(solution)/shard_map/front/pallas_call | solution.py:605
  103.7 0.8 copy.47
  104.5 0.1 copy.48
  104.5 0.7 reshape.70.asked_ref
  105.2 124.1 %rear.1 = (f32[784,512]{1,0:T(8,128)}, f32[8,80,512]{2,1,0:T(8,128)}, f32[32,24,128]{2,1,0:T(8,128)}, f32[32,1,128]{2,1,0:T(1,128)}) custom-call(s32[4,1]{1,0:T(4,128)} %copy.49.len_ref, bf16[1024,512]{1,0:T(8,128)(2,1)} %get-tuple-element.58.x_ref, bf16[1024,512]{1,0:T(8,128)(2,1)} %get-tuple-element.59.n1_ref, ...), custom_call_target="tpu_custom_call" | custom-call | flops 60000002048 | bytes 30000000 | tf_op jit(solution)/shard_map/rear/pallas_call | solution.py:1099
  229.3 12.9 %settle.1 = (f32[784,512]{1,0:T(8,128)}, f32[784,512]{1,0:T(8,128)}, f32[784,512]{1,0:T(8,128)}, bf16[784,512]{1,0:T(8,128)(2,1)}, f32[512,512]{1,0:T(8,128)}, /...) custom-call(f32[32,1,128]{2,1,0:T(1,128)} %get-tuple-element.72.squa, ...), custom_call_target="tpu_custom_call" | custom-call | flops 8028160 | bytes 20000000 | tf_op jit(solution)/shard_map/settle/pallas_call | solution.py:1314
  242.3 1.3 fusion
  (1 shorter events, 0.0 us)

commit v4 on v3

--- a/solution.py
+++ b/solution.py
@@ -290,7 +290,7 @@
     def release(g):
         def follow(i, carry):
             at = lax.rem(me + i, n_every)
-            row_copy(g - 1, at, at, at).wait_send()
+            row_copy(g - 2, at, at, at).wait_send()
             row_copy(g, me, me, at).start()
             return carry
 
@@ -350,6 +350,7 @@
     lax.fori_loop(0, per_side // TB, functools.partial(negatives, first=side), 0)
     if z.groups > 1:
         serve(1)
+        send_group(1)
     n1_copy.wait_recv()
     acc_ref[...] = t2_ref[side] + n1_ref[...]
     for i in range(1, half):
@@ -373,14 +374,10 @@
     stat_ref[...] = jnp.zeros_like(stat_ref)
     gw2_ref[...] = jnp.zeros_like(gw2_ref)
     gneg_ref[...] = jnp.zeros_like(gneg_ref)
-    if z.groups > 1:
-        release(1)
     for i in range(1, half):
         from_chip = lax.rem(chip + i, half)
         wc_copy(i, side * half + from_chip, chip).wait_recv()
         wp_copy(side * half + from_chip).start()
-    for g in range(2, min(3, z.groups)):
-        release(g)
     for i in range(half):
         wp_copy((1 - side) * half + i).wait_recv()
     place_weights(z, w_ref, w1_ref, w2_ref)
@@ -501,8 +498,9 @@
         total = pos_exp + jnp.sum(neg_exp, -1, keepdims=True)
         live = jnp.where(place + 1 < length, 1.0, 0.0) * lead.astype(f32)
         per = (top + jnp.log(total) - pos) * live
-        gneg = (neg_exp / total * live).astype(bf16)
-        gpos = (pos_exp / total - 1.0) * live
+        share = 1.0 / total
+        gneg = (neg_exp * (share * live)).astype(bf16)
+        gpos = (pos_exp * share - 1.0) * live
         gz = mm(gneg, neg_ref[...].reshape(half * 2 * z.rn, D)) * scale + gpos * target * scale
         gneg_ref[...] += mm(gneg, out, TN) * scale
         target_grad = gpos * zf * scale
@@ -555,6 +553,8 @@
         pl.when(i == NT - 2)(neg_two)
         inputs(i)
         attend(i)
+        if z.groups > 2:
+            pl.when(i == 0)(lambda: release(2))
         pl.when(i == 1)(after_one)
         pl.when(i == NT - 2)(after_two)
         return carry
@@ -588,7 +588,8 @@
     def finish(i, carry):
         at = lax.rem(me + i, n_every)
         ask_copy(at, at, at).wait_send()
-        row_copy(z.groups - 1, at, at, at).wait_send()
+        for g in range(max(0, z.groups - 2), z.groups):
+            row_copy(g, at, at, at).wait_send()
         return carry
 
     lax.fori_loop(1, n_every, finish, 0)
@@ -864,9 +865,9 @@
     def first_hook():
         for p in early:
             chips_b(p)
+        spread_a()
 
     def second_hook():
-        swap_a()
         for p in early:
             planes_b(p)
 
@@ -948,15 +949,15 @@
                 keys_end(p, j)
             if phase == 0:
                 pl.when(j == 0)(chips_a)
-                pl.when(j == 1)(planes_a)
-                pl.when(j == 2)(spread_a)
+                pl.when(j == 2)(planes_a)
             if final:
                 pl.when(j == NT - 1)(late_weights)
+                pl.when(j == 0)(first_hook)
                 outputs(j)
                 if per_group == 1:
                     send_group(j)
-                pl.when(j == 0)(first_hook)
-                pl.when(j == 2)(second_hook)
+                pl.when(j == 1)(second_hook)
+                pl.when(j == 2)(swap_a)
             return carry
 
         lax.fori_loop(0, NT, keys_step, 0)
@@ -1015,13 +1016,13 @@
     for p in late:
         chips_b(p)
     collect(0)
+    for p in late:
+        planes_b(p)
     for i in range(half):
         negatives(side * half + i)
     for i in range(half):
         hn_copy((1 - side) * half + i).wait_recv()
         negatives((1 - side) * half + i)
-    for p in late:
-        planes_b(p)
     for g in range(1, max(1, z.groups - 1)):
         collect(g)
     total = zs_ref[k]
@@ -1150,9 +1151,9 @@
 def adam_step(weight, grad, first, second, rate, decay):
     first_new = beta_one * first + (1.0 - beta_one) * grad
     second_new = beta_two * second + (1.0 - beta_two) * grad * grad
-    fix_one = 1.0 - beta_one**STEP
-    fix_two = 1.0 - beta_two**STEP
-    move = first_new / fix_one / (jnp.sqrt(second_new / fix_two) + adam_floor) + decay * weight
+    fix_one = 1.0 / (1.0 - beta_one**STEP)
+    fix_two = 1.0 / (1.0 - beta_two**STEP)
+    move = first_new * fix_one / (jnp.sqrt(second_new * fix_two) + adam_floor) + decay * weight
     return (weight - rate * move, first_new, second_new)
 
 

time: 246 us -> 235 us (0.955)
  Pallas kernels: 237 us -> 225 us
    pallas_call x1, Pallas kernels: 124 us -> 117 us  [rear(): pl.pallas_call(functools.partial(rear_kernel, z), out_shape=(sds((z.rows_...]
    pallas_call x1, Pallas kernels: 99.5 us -> 95.9 us  [front(): pl.pallas_call(functools.partial(front_kernel, z), out_shape=(sds((z.n_ev...]
where the time goes in v4:
time: 235 us; the launch traced here: 232 us
  Pallas kernels  225 us (96%)
  local copies, waits for them, and re-layouts  5.66 us (2%)
    pallas_call x1, Pallas kernels, rear(): pl.pallas_call(functools.partial(rear_kernel, z), out_shape=(sds((z.rows_...  117 us
    pallas_call x1, Pallas kernels, front(): pl.pallas_call(functools.partial(front_kernel, z), out_shape=(sds((z.n_ev...  95.9 us
    pallas_call x1, Pallas kernels, settle(): pl.pallas_call(functools.partial(settle_kernel, z), grid=(steps,), out_sh...  12.9 us

profile of v4, /device:TPU:0, one launch (start us, length us, event | category | flops | bytes accessed | tf_op | source)
XLA Modules:
  0.0 232.5 jit_solution(8008950918338535263)
XLA Ops:
  0.7 1.3 copy.49.len_ref
  2.0 0.7 convert_element_type.3
  2.7 0.1 reshape.64
  2.8 0.7 reshape_reshape_broadcast_in_dim.3.ids_ref
  3.4 0.7 reshape.65.ids_ref
  4.1 95.9 %front.1 = (f32[32,1,128]{2,1,0:T(1,128)}, f32[4,1,256]{2,1,0:T(1,128)}, bf16[8,4,80,512]{3,2,1,0:T(8,128)(2,1)}, f32[4,8,128]{2,1,0:T(8,128)}, bf16[1024,512]{1...) custom-call(s32[4,1]{1,0:T(4,128)} %copy.49.len_ref, ...), custom_call_target="tpu_custom_call" | custom-call | flops 60000002048 | bytes 30000000 | tf_op jit(solution)/shard_map/front/pallas_call | solution.py:606
  100.0 0.8 copy.47
  100.8 0.1 copy.48
  100.9 0.7 reshape.70.asked_ref
  101.6 116.6 %rear.1 = (f32[784,512]{1,0:T(8,128)}, f32[8,80,512]{2,1,0:T(8,128)}, f32[32,24,128]{2,1,0:T(8,128)}, f32[32,1,128]{2,1,0:T(1,128)}) custom-call(s32[4,1]{1,0:T(4,128)} %copy.49.len_ref, bf16[1024,512]{1,0:T(8,128)(2,1)} %get-tuple-element.58.x_ref, bf16[1024,512]{1,0:T(8,128)(2,1)} %get-tuple-element.59.n1_ref, ...), custom_call_target="tpu_custom_call" | custom-call | flops 60000002048 | bytes 30000000 | tf_op jit(solution)/shard_map/rear/pallas_call | solution.py:1100
  218.2 12.9 %settle.1 = (f32[784,512]{1,0:T(8,128)}, f32[784,512]{1,0:T(8,128)}, f32[784,512]{1,0:T(8,128)}, bf16[784,512]{1,0:T(8,128)(2,1)}, f32[512,512]{1,0:T(8,128)}, /...) custom-call(f32[32,1,128]{2,1,0:T(1,128)} %get-tuple-element.72.squa, ...), custom_call_target="tpu_custom_call" | custom-call | flops 8028160 | bytes 20000000 | tf_op jit(solution)/shard_map/settle/pallas_call | solution.py:1315
  231.2 1.3 fusion
  (1 shorter events, 0.0 us)

commit v5 on v4

--- a/solution.py
+++ b/solution.py
@@ -137,9 +137,9 @@
 
 def front_kernel(
     z, len_ref, table_ref, f1_ref, f2_ref, bias_ref, owner_ref, local_ref, ids_ref, bucket_ref, gains_ref,
-    asked_ref, slot_ref, w_ref, bias_all_ref,
+    wanted_ref, slot_ref, w_ref, bias_all_ref,
     x_ref, n1o_ref, q_ref, k_ref, v_ref, do_ref, ghu_ref, gres_ref, ga_ref, stat_ref,
-    low_ref, req_ref, send_ref, got_ref, t2_ref, n1_ref, n2_ref, n3_ref, acc_ref, plane_ref, neg_ref,
+    low_ref, req_ref, asked_ref, send_ref, got_ref, t2_ref, n1_ref, n2_ref, n3_ref, acc_ref, plane_ref, neg_ref,
     xf_ref, hu_ref, o_ref, carry_ref, kb_ref, w1_ref, w2_ref, gw2_ref, gneg_ref,
     ask_send, ask_recv, row_send, row_recv,
     wz_send, wz_recv, wc_send, wc_recv, wp_send, wp_recv, bz_send, bz_recv,
@@ -268,6 +268,8 @@
     turn = lax.broadcasted_iota(jnp.int32, (per * CH, n_every), 0) // CH
     asker = lax.broadcasted_iota(jnp.int32, (per * CH, n_every), 1)
     lane = lax.broadcasted_iota(jnp.int32, (per * CH, z.rows_dev), 1).astype(f32)
+    turn_row = lax.broadcasted_iota(jnp.int32, (n_every, per * CH), 1) // CH
+    asker_row = lax.broadcasted_iota(jnp.int32, (n_every, per * CH), 0)
 
     def serve(g):
         lanes = slice(g * CH, (g + 1) * CH)
@@ -275,6 +277,9 @@
             at = mm(spread, asked_high[:, lanes], NT_) * 32.0 + mm(spread, asked_low[:, lanes], NT_)
             at = jnp.where(asker == turn + b * per, at, 0.0)
             column = jnp.sum(at, axis=1, keepdims=True) - 1.0
+            row = mm(asked_high[:, lanes], spread, NT_) * 32.0 + mm(asked_low[:, lanes], spread, NT_)
+            row = row_sum(jnp.where(asker_row == turn_row + b * per, row, 0.0)) - 1.0
+            wanted_ref[g, :, b * per * CH : (b + 1) * per * CH] = row
             hot = jnp.where(lane == column, 1.0, 0.0).astype(bf16)
             found = mm(hot, low_ref[...]).astype(bf16)
             send_ref[g, b * per : (b + 1) * per] = found.reshape(per, CH, D)
@@ -606,7 +611,7 @@
     return pl.pallas_call(
         functools.partial(front_kernel, z),
         out_shape=(
-            sds((z.n_every, 1, LANES), f32),
+            sds((z.groups, 1, z.slots), f32),
             sds((NT, 1, TB), f32),
             sds((z.n_data, z.n_model, z.rw, D), bf16),
             sds((z.n_model, 8, LANES), f32),
@@ -619,6 +624,7 @@
         out_specs=(VM,) * 14,
         scratch_shapes=[
             vm(table.shape, bf16),
+            vm((z.n_every, 1, LANES), f32),
             vm((z.n_every, 1, LANES), f32),
             vm((z.groups, z.n_every, CH, D), bf16),
             vm((z.groups, z.n_every, CH, D), bf16),
@@ -1161,7 +1167,7 @@
     z, squares_ref, packs_ref, wg_ref, tg_ref, t_ref, tm_ref, tv_ref, a_ref, am_ref, av_ref,
     b_ref, bm_ref, bv_ref, c_ref, cm_ref, cv_ref, e_ref, em_ref, ev_ref,
     t_out, tm_out, tv_out, tl_out, a_out, am_out, av_out, al_out, b_out, bm_out, bv_out, bl_out,
-    c_out, cm_out, cv_out, e_out, em_out, ev_out, flat_out, factor_ref, one_ref,
+    c_out, cm_out, cv_out, e_out, em_out, ev_out, loss_out, count_out, norm_out, factor_ref, one_ref,
 ):
     def update(grad, refs, outs, rate, decay):
         new, first, second = adam_step(refs[0][...], grad, refs[1][...], refs[2][...], rate, decay)
@@ -1187,9 +1193,9 @@
         norm = jnp.sqrt(jnp.sum(squares, axis=1, keepdims=True))
         factor = jnp.minimum(1.0, clip_at / norm)
         factor_ref[...] = jnp.broadcast_to(factor, factor_ref.shape)
-        flat_out[0:2] = packs[12:14]
-        flat_out[2:3] = jnp.broadcast_to(norm, (1, LANES))
-        flat_out[3:8] = jnp.zeros((5, LANES), f32)
+        loss_out[...] = packs[12:13, 0:1]
+        count_out[...] = packs[13:14, 0:1]
+        norm_out[...] = norm
         one = jnp.concatenate([wg_ref[z.order(d), 0 : z.r1] for d in range(z.n_data)], axis=0)
         two = jnp.concatenate(
             [wg_ref[z.order(d), z.r1 : z.r1 + z.r2] for d in range(z.n_data)], axis=0
@@ -1232,98 +1238,11 @@
             like(f1[0]), like(f1[0]), like(f1[0]), like(f1[0], bf16),
             like(f2[0]), like(f2[0]), like(f2[0]), like(f2[0], bf16),
             like(gains[0]), like(gains[0]), like(gains[0]),
-            like(bias[0]), like(bias[0]), like(bias[0]), sds((8, LANES), f32),
+            like(bias[0]), like(bias[0]), like(bias[0]),
+            sds((1, 1), f32), sds((1, 1), f32), sds((1, 1), f32),
         ),
         in_specs=[VM] * 3 + [block] * 4 + [part] * 3 + [VM] * 9,
-        out_specs=(block,) * 4 + (part,) * 4 + (VM,) * 11,
-        scratch_shapes=[pltpu.VMEM((8, LANES), f32), pltpu.VMEM((D, 4 * z.fw), f32)],
-        compiler_params=pltpu.CompilerParams(vmem_limit_bytes=LIMIT),
-        cost_estimate=pl.CostEstimate(
-            flops=20 * z.rows_dev * D, bytes_accessed=20_000_000, transcendentals=1_000_000
-        ),
-        name="settle",
-    )(squares, packs, wg, tg, *table, *f1, *f2, *gains, *bias)
-
-
-def settle_kernel(
-    z, squares_ref, packs_ref, wg_ref, tg_ref, t_ref, tm_ref, tv_ref, a_ref, am_ref, av_ref,
-    b_ref, bm_ref, bv_ref, c_ref, cm_ref, cv_ref, e_ref, em_ref, ev_ref,
-    t_out, tm_out, tv_out, tl_out, a_out, am_out, av_out, al_out, b_out, bm_out, bv_out, bl_out,
-    c_out, cm_out, cv_out, e_out, em_out, ev_out, flat_out, factor_ref, one_ref,
-):
-    def update(grad, refs, outs, rate, decay):
-        new, first, second = adam_step(refs[0][...], grad, refs[1][...], refs[2][...], rate, decay)
-        outs[0][...] = new
-        outs[1][...] = first
-        outs[2][...] = second
-        if len(outs) > 3:
-            outs[3][...] = new.astype(bf16)
-
-    @pl.when(pl.program_id(0) == 0)
-    def _():
-        packs = jnp.sum(packs_ref[...], axis=0)
-        gain_grad = jnp.concatenate(
-            [
-                jnp.concatenate([packs[4 * r + i : 4 * r + i + 1] for i in range(D // LANES)], axis=1)
-                for r in range(3)
-            ],
-            axis=0,
-        )
-        bias_all = packs[16:24]
-        squares = jnp.sum(squares_ref[...], axis=0) + row_sum(packs[0:12] * packs[0:12])
-        squares = squares + row_sum(bias_all * bias_all)
-        norm = jnp.sqrt(jnp.sum(squares, axis=1, keepdims=True))
-        factor = jnp.minimum(1.0, clip_at / norm)
-        factor_ref[...] = jnp.broadcast_to(factor, factor_ref.shape)
-        flat_out[0:2] = packs[12:14]
-        flat_out[2:3] = jnp.broadcast_to(norm, (1, LANES))
-        flat_out[3:8] = jnp.zeros((5, LANES), f32)
-        one = jnp.concatenate([wg_ref[z.order(d), 0 : z.r1] for d in range(z.n_data)], axis=0)
-        two = jnp.concatenate(
-            [wg_ref[z.order(d), z.r1 : z.r1 + z.r2] for d in range(z.n_data)], axis=0
-        )
-        one_ref[...] = one.T * factor
-        update(two * factor, (b_ref, bm_ref, bv_ref), (b_out, bm_out, bv_out, bl_out), 0.04, 0.1)
-        update(gain_grad * factor, (c_ref, cm_ref, cv_ref), (c_out, cm_out, cv_out), 0.5, 0.0)
-        head = lax.broadcasted_iota(jnp.int32, bias_all.shape, 0)
-        first_head = lax.axis_index("mp") * z.heads_dev
-        mine = [
-            row_sum(jnp.where(head == first_head + r, bias_all, 0.0)) for r in range(z.heads_dev)
-        ]
-        bias_grad = jnp.concatenate(mine, axis=0)
-        update(bias_grad * factor, (e_ref, em_ref, ev_ref), (e_out, em_out, ev_out), 1.0, 0.0)
-
-    size = a_ref.shape[0]
-    rows = pl.ds(pl.multiple_of(pl.program_id(0) * size, size), size)
-    update(one_ref[rows, :], (a_ref, am_ref, av_ref), (a_out, am_out, av_out, al_out), 0.04, 0.1)
-    update(
-        tg_ref[...] * factor_ref[0:1, 0:1], (t_ref, tm_ref, tv_ref), (t_out, tm_out, tv_out, tl_out), 0.5, 0.1
-    )
-
-
-def settle(z, squares, packs, wg, tg, table, f1, f2, gains, bias):
-    sds = jax.ShapeDtypeStruct
-    rows = next(r for r in range(112, 0, -16) if z.rows_dev % r == 0)
-    blocks = z.rows_dev // rows
-    steps = next(n for n in range(blocks, 512) if D % n == 0 and D // n % 16 == 0)
-    block = pl.BlockSpec((rows, D), lambda i: (jnp.minimum(i, blocks - 1), 0))
-    part = pl.BlockSpec((D // steps, 4 * z.fw), lambda i: (i, 0))
-
-    def like(array, dtype=f32):
-        return sds(array.shape, dtype)
-
-    return pl.pallas_call(
-        functools.partial(settle_kernel, z),
-        grid=(steps,),
-        out_shape=(
-            like(tg), like(tg), like(tg), like(tg, bf16),
-            like(f1[0]), like(f1[0]), like(f1[0]), like(f1[0], bf16),
-            like(f2[0]), like(f2[0]), like(f2[0]), like(f2[0], bf16),
-            like(gains[0]), like(gains[0]), like(gains[0]),
-            like(bias[0]), like(bias[0]), like(bias[0]), sds((8, LANES), f32),
-        ),
-        in_specs=[VM] * 3 + [block] * 4 + [part] * 3 + [VM] * 9,
-        out_specs=(block,) * 4 + (part,) * 4 + (VM,) * 11,
+        out_specs=(block,) * 4 + (part,) * 4 + (VM,) * 13,
         scratch_shapes=[pltpu.VMEM((8, LANES), f32), pltpu.VMEM((D, 4 * z.fw), f32)],
         compiler_params=pltpu.CompilerParams(vmem_limit_bytes=LIMIT),
         cost_estimate=pl.CostEstimate(
@@ -1352,17 +1271,15 @@
         z, lengths, table, w_f1, w_f2, bias, owners.reshape(MB, 1, LEN), item_rows, ids_rows,
         buckets, gains,
     )
-    asked = asked.reshape(z.n_every, LANES)[:, : z.groups * CH].reshape(z.n_every, z.groups, CH)
-    asked = asked.transpose(1, 0, 2).reshape(z.groups, 1, z.slots)
     table_grad, wg, packs, squares = rear(
         z, lengths, x, n1, q, k, v, do, ghu, gres, w, bias_all, buckets, gains, slot, stat_a,
         ga.reshape(2, z.half, z.ra, D), asked, ids_cols,
     )
-    *new, flat = settle(
+    *new, loss_sum, loss_count, grad_norm = settle(
         z, squares, packs, wg, table_grad, (table, table_m, table_v), (w_f1, f1_m, f1_v),
         (w_f2, f2_m, f2_v), (gains, gains_m, gains_v), (bias, bias_m, bias_v),
     )
-    return (flat[0, 0], flat[1, 0], flat[2, 0], *new)
+    return (loss_sum.reshape(()), loss_count.reshape(()), grad_norm.reshape(()), *new)
 
 
 def solution(mesh):

time: 235 us -> 232 us (0.987)
  local copies, waits for them, and re-layouts: 5.66 us -> 2.77 us
where the time goes in v5:
time: 232 us; the launch traced here: 230 us
  Pallas kernels  226 us (97%)
  local copies, waits for them, and re-layouts  2.77 us (1%)
    pallas_call x1, Pallas kernels, rear(): pl.pallas_call(functools.partial(rear_kernel, z), out_shape=(sds((z.rows_...  117 us
    pallas_call x1, Pallas kernels, front(): pl.pallas_call(functools.partial(front_kernel, z), out_shape=(sds((z.grou...  95.7 us
    pallas_call x1, Pallas kernels, settle(): pl.pallas_call(functools.partial(settle_kernel, z), grid=(steps,), out_sh...  13 us

profile of v5, /device:TPU:0, one launch (start us, length us, event | category | flops | bytes accessed | tf_op | source)
XLA Modules:
  0.0 229.8 jit_solution(10838076122473126134)
XLA Ops:
  0.7 1.3 copy.43.len_ref
  2.0 0.7 convert_element_type.3
  2.7 0.1 reshape.64
  2.8 0.7 reshape_reshape_broadcast_in_dim.3.ids_ref
  3.4 0.7 reshape.65.ids_ref
  4.1 95.7 %front.1 = (f32[4,1,512]{2,1,0:T(1,128)}, f32[4,1,256]{2,1,0:T(1,128)}, bf16[8,4,80,512]{3,2,1,0:T(8,128)(2,1)}, f32[4,8,128]{2,1,0:T(8,128)}, bf16[1024,512]{1,...) custom-call(s32[4,1]{1,0:T(4,128)} %copy.43.len_ref, ...), custom_call_target="tpu_custom_call" | custom-call | flops 60000002048 | bytes 30000000 | tf_op jit(solution)/shard_map/front/pallas_call | solution.py:611
  99.9 116.8 %rear.1 = (f32[784,512]{1,0:T(8,128)}, f32[8,80,512]{2,1,0:T(8,128)}, f32[32,24,128]{2,1,0:T(8,128)}, f32[32,1,128]{2,1,0:T(1,128)}) custom-call(s32[4,1]{1,0:T(4,128)} %copy.43.len_ref, bf16[1024,512]{1,0:T(8,128)(2,1)} %get-tuple-element.60.x_ref, bf16[1024,512]{1,0:T(8,128)(2,1)} %get-tuple-element.61.n1_ref, ...), custom_call_target="tpu_custom_call" | custom-call | flops 60000002048 | bytes 30000000 | tf_op jit(solution)/shard_map/rear/pallas_call | solution.py:1106
  216.7 13.0 %settle.1 = (f32[784,512]{1,0:T(8,128)}, f32[784,512]{1,0:T(8,128)}, f32[784,512]{1,0:T(8,128)}, bf16[784,512]{1,0:T(8,128)(2,1)}, f32[512,512]{1,0:T(8,128)}, /...) custom-call(f32[32,1,128]{2,1,0:T(1,128)} %get-tuple-element.74.squa, ...), custom_call_target="tpu_custom_call" | custom-call | flops 8028160 | bytes 20000000 | tf_op jit(solution)/shard_map/settle/pallas_call | solution.py:1233
  (1 shorter events, 0.0 us)
